TPU v7x, 128 devices: a whole 4x4x4 slice. The times are simulated.
128 devices in a mesh: ctx: 8 (over y_lo, x), tp: 16 (over z, y_hi, core).
Axes of the slice: x: 4, y: 4 (y_hi: 2, y_lo: 2; y = y_hi * 2 + y_lo), z: 4, core: 2. Of those that a mesh axis runs over, the one named last changes fastest.
Arguments:
- stored_pages: bfloat16 [24, 128, 8192], P('ctx', None, 'tp'), may hold values from -6 to 6
- kv_weight: bfloat16 [8192, 2048], P(None, 'tp'), may hold values from -0.0625 to 0.0625
- page_table: int32 [8, 8], replicated, may hold values from 0 to 23, as said below
- page_counts: int32 [8, 8], replicated, may hold values from 0 to 1, as said below
- queries: bfloat16 [2048, 8192], P('ctx', 'tp'), may hold values from -16 to 16
- turn_kv: bfloat16 [2048, 2048], P('ctx', 'tp'), may hold values from -6 to 6
- turn_pos: int32 [2048], replicated, may hold values from 3072 to 6143, as said below
Outputs:
- attended: bfloat16 [2048, 8192], P('ctx', 'tp')
- restored_cache: bfloat16 [8192, 2048], P('ctx', 'tp')
Inputs may be any that keep to these rules, and one draw needn't show every extreme that they name: page_table[d, h] is a page of holder h (h * 3 to h * 3 + 2); where page_counts[d, h] is 0 it is h * 3. Every stored page is taken by exactly one context shard. `page_counts`: each holder hands out all its 3 pages, at most one to each context shard; one context shard takes a page from every holder. `turn_pos`: strictly increasing in steps of 1 or 2; turn_pos[0] = 3072 and the last entry is 6143.
All inputs are finite; a program needn't handle non-finite values.
Results may differ from a plain program's by a relative error of at most 0.03.
Values may be sent and summed in bfloat16 or wider, within the bound.
No kernel may reach another device: no remote copies, remote signals or barrier semaphores. Data moves between devices by JAX's collectives and lax.ppermute only.
A program may use at most 192 MiB of HBM per device.

v0:
```python
import math

import jax
import jax.numpy as jnp
from jax import lax
from jax.sharding import PartitionSpec as P

HEAD_DIM = 128


huge_value = 1e30
far_position = 1 << 30


def swapped(value, axis, stride):
    return lax.ppermute(value, axis, [(i, i ^ 1 << stride) for i in range(lax.axis_size(axis))])


def passed_along(value, axis, by):
    peers = lax.axis_size(axis)
    return lax.ppermute(value, axis, [(i, (i + by) % peers) for i in range(peers)])


def inverse_freq(head_width):
    half_width = head_width // 2
    exponent = jnp.arange(half_width, dtype=jnp.float32) * 2.0 / head_width
    base_freq = jnp.exp(-exponent * math.log(500000.0))
    wavelength = 2.0 * math.pi / base_freq
    smooth = (8192.0 / wavelength - 1.0) / 3.0
    blended = (1.0 - smooth) * base_freq / 8.0 + smooth * base_freq
    return jnp.where(
        wavelength < 2048.0, base_freq, jnp.where(wavelength > 8192.0, base_freq / 8.0, blended)
    )


def rotate(values, positions):
    head_width = values.shape[-1]
    half_width = head_width // 2
    angle = positions.astype(jnp.float32)[:, None] * inverse_freq(head_width)[None, :]
    angle = angle.reshape((angle.shape[0],) + (1,) * (values.ndim - 2) + (half_width,))
    cosine = jnp.cos(angle)
    sine = jnp.sin(angle)
    first_half = values[..., :half_width]
    second_half = values[..., half_width:]
    return jnp.concatenate(
        [first_half * cosine - second_half * sine, second_half * cosine + first_half * sine],
        axis=-1,
    )


def rope_blocks(values, positions, first_block):
    row_count = values.shape[0]
    block_count = values.shape[1] // HEAD_DIM
    shaped = values.reshape(row_count, block_count, HEAD_DIM)
    is_key = (first_block + jnp.arange(block_count)) % 2 == 0
    turned = jnp.where(is_key[None, :, None], rotate(shaped, positions), shaped)
    return turned.reshape(row_count, block_count * HEAD_DIM)


def attend(softmax_state, query_flat, query_pos, key_block, value_block, key_pos):
    running_max, denominator, numerator = softmax_state
    scale = 1.0 / math.sqrt(HEAD_DIM)
    scores = (
        lax.dot_general(
            query_flat, key_block, (((1,), (1,)), ((), ())), preferred_element_type=jnp.float32
        )
        * scale
    )
    visible = key_pos[None, :] <= query_pos[:, None]
    new_max = jnp.maximum(running_max, jnp.max(jnp.where(visible, scores, -huge_value), axis=1))
    decay = jnp.exp(running_max - new_max)
    weights = jnp.where(visible, jnp.exp(scores - new_max[:, None]), 0.0)
    denominator = denominator * decay + jnp.sum(weights, axis=1)
    numerator = numerator * decay[:, None] + jnp.dot(
        weights.astype(jnp.bfloat16), value_block, preferred_element_type=jnp.float32
    )
    return (new_max, denominator, numerator)


def local(stored_pages, kv_weight, page_table, page_counts, queries, turn_kv, turn_pos):
    ctx_count = lax.axis_size("ctx")
    ctx_index = lax.axis_index("ctx")
    tp_index = lax.axis_index("tp")
    held_pages, page_rows, local_width = stored_pages.shape
    columns = kv_weight.shape[1]
    blocks_dev = columns // HEAD_DIM
    first_block = tp_index * blocks_dev
    tok_new = queries.shape[0]
    heads_dev = queries.shape[1] // HEAD_DIM
    given_pages = lax.dynamic_index_in_dim(page_table, ctx_index, 1, keepdims=False)
    given_live = lax.dynamic_index_in_dim(page_counts, ctx_index, 1, keepdims=False) > 0
    local_pick = given_pages - ctx_index * held_pages
    outgoing = jnp.where(
        given_live[:, None, None],
        jnp.take(stored_pages, local_pick, axis=0),
        jnp.zeros((), jnp.bfloat16),
    )
    arrived = lax.all_to_all(outgoing, "ctx", split_axis=0, concat_axis=0, tiled=True)
    arrived_flat = arrived.reshape(ctx_count * page_rows, local_width)
    projected = jnp.dot(
        lax.all_gather(arrived_flat, "tp", axis=1, tiled=True),
        kv_weight,
        preferred_element_type=jnp.float32,
    )
    slot_pages = lax.dynamic_index_in_dim(page_table, ctx_index, 0, keepdims=False)
    slot_pos = (
        slot_pages[:, None] * page_rows + jnp.arange(page_rows, dtype=jnp.int32)[None, :]
    ).reshape(-1)
    own_cache = rope_blocks(projected, slot_pos, first_block).astype(jnp.bfloat16)
    local_pos = lax.dynamic_slice_in_dim(turn_pos, ctx_index * tok_new, tok_new)
    own_turn = rope_blocks(turn_kv.astype(jnp.float32), local_pos, first_block).astype(jnp.bfloat16)
    other_cache, other_turn = swapped((own_cache, own_turn), "tp", 0)
    is_even = tp_index % 2 == 0
    key_cache = jnp.where(is_even, own_cache, other_cache)
    value_cache = jnp.where(is_even, other_cache, own_cache)
    key_turn = jnp.where(is_even, own_turn, other_turn)
    value_turn = jnp.where(is_even, other_turn, own_turn)
    key_block = jnp.concatenate([key_cache, key_turn], axis=0)
    value_block = jnp.concatenate([value_cache, value_turn], axis=0)
    rotated = rotate(
        queries.astype(jnp.float32).reshape(tok_new, heads_dev, HEAD_DIM), local_pos
    ).astype(jnp.bfloat16)
    query_heads = jnp.transpose(rotated, (1, 0, 2))

    def key_positions(source):
        live_pages = lax.dynamic_index_in_dim(page_counts, source, 0, keepdims=False) > 0
        cache_pos = jnp.where(jnp.repeat(live_pages, page_rows), -1, far_position).astype(jnp.int32)
        source_turn = lax.dynamic_slice_in_dim(turn_pos, source * tok_new, tok_new)
        return jnp.concatenate([cache_pos, source_turn])

    query_flat = query_heads.reshape(heads_dev * tok_new, HEAD_DIM)
    query_pos = jnp.tile(local_pos, heads_dev)
    row_total = heads_dev * tok_new
    start_state = (
        jnp.full((row_total,), -huge_value, jnp.float32),
        jnp.zeros((row_total,), jnp.float32),
        jnp.zeros((row_total, HEAD_DIM), jnp.float32),
    )

    def cycle_step(turn_index, carried):
        softmax_state, keys_now, values_now = carried
        source = (ctx_index - turn_index) % ctx_count
        softmax_state = attend(
            softmax_state, query_flat, query_pos, keys_now, values_now, key_positions(source)
        )
        keys_now, values_now = passed_along((keys_now, values_now), "ctx", 1)
        return (softmax_state, keys_now, values_now)

    softmax_state, keys_last, values_last = lax.fori_loop(
        0, ctx_count - 1, cycle_step, (start_state, key_block, value_block)
    )
    last_source = (ctx_index + 1) % ctx_count
    final_max, final_total, final_values = attend(
        softmax_state, query_flat, query_pos, keys_last, values_last, key_positions(last_source)
    )
    result = (final_values / final_total[:, None]).reshape(heads_dev, tok_new, HEAD_DIM)
    attended = (
        jnp.transpose(result, (1, 0, 2)).reshape(tok_new, heads_dev * HEAD_DIM).astype(jnp.bfloat16)
    )
    return (attended, own_cache)


def solution(mesh):
    placed = (P("ctx", None, "tp"), P(None, "tp"), P(), P(), P("ctx", "tp"), P("ctx", "tp"), P())
    return jax.shard_map(
        local,
        mesh=mesh,
        in_specs=placed,
        out_specs=(P("ctx", "tp"), P("ctx", "tp")),
        check_vma=False,
    )
```

profile of v0, /device:TPU:1, one launch (start us, length us, event | category | flops | bytes accessed | tf_op | source)
XLA Modules:
  0.0 293.1 jit_solution(3023230092277732770)
XLA Ops:
  7.3 1.0 fusion.47
  8.3 0.9 and_reduce_fusion
  9.2 0.9 fusion.46
  10.0 1.6 gather_fusion
  11.8 20.6 %all_to_all.5 = bf16[8,128,512]{2,1,0:T(8,128)(2,1)} all-to-all(bf16[8,128,512]{2,1,0:T(8,128)(2,1)S(1)} %select_select_fusion), channel_id=1, replica_groups=mesh['ctx'=8,'tp'=16] {'ctx'}, dimensions={0} | all-to-all | bytes 2097152 | tf_op jit(solution)/shard_map/all_to_all | solution.py:98
  32.6 0.8 fusion.53
  33.8 1.9 collective-permute-start.3
  35.9 0.7 fusion.49
  38.4 0.9 pad_maximum_fusion.2
  39.4 114.2 %all-gather.2.cloned.1.call-done = bf16[1024,8192]{1,0:T(8,128)(2,1)} async-done(((bf16[1024,512]{1,0:T(8,128)(2,1)}), bf16[1024,8192]{1,0:T(8,128)(2,1)}) %all-gather.2.cloned.1.call-update) | async-done | bytes 16777232 | tf_op jit(solution)/shard_map/all_gather | solution.py:101
  153.6 11.4 %fusion.55 = f32[1024,128]{0,1:T(8,128)S(1)} fusion(bf16[1024,8192]{1,0:T(8,128)(2,1)} %all-gather.2.cloned.1.call-done, bf16[8192,128]{1,0:T(8,128)(2,1)S(1)} %copy-done), kind=kOutput, calls=%fused_computation.92 | convolution fusion | flops 2147483648 | bytes 19398656 | tf_op jit(solution)/shard_map/dot_general | solution.py:100
  165.0 1.2 fusion.34
  166.8 0.8 copy.15
  168.6 111.0 %while.24 = (s32[]{:T(128)}, f32[1024]{0:T(1024)S(1)}, f32[1024]{0:T(1024)S(1)}, f32[1024,128]{1,0:T(8,128)}, bf16[1280,128]{1,0:T(8,128)(2,1)S(1)}, /*index=5*/...) while((s32[]{:T(128)}, f32[1024]{0:T(1024)S(1)}, ...), condition=%wide.region_3.4_spmd.clone, body=%wide.region_0.0_spmd.clone.sunk | while | flops 689838336 | bytes 42721860 | solution.py:149
  168.7 1.3 collective-permute-start
  169.9 1.3 collective-permute-start.1
  172.0 0.8 dynamic_slice.72
  172.7 2.1 fusion.78
  174.8 2.3 copy-done.1
  177.1 1.8 fusion.79
  178.9 4.5 %fusion.81 = f32[1024,128]{1,0:T(8,128)} fusion(bf16[1280,128]{1,0:T(8,128)(2,1)S(1)} %copy.40, f32[1024,1280]{1,0:T(8,128)} %copy-done.1, f32[1024]{0:T(1024)S(1)} %select_maximum_fusion.2, s32[1280]{0:T(1024)S(1)} %pad_add_fusion.3, s32[1024]{0:T(1024)S(1)} %bitcast.68, f32[1024,128]{1,0:T(8,128)} %get-tuple-element.472, ...), kind=kOutput, calls=%fused_computation.8.clone.1 | convolution fusion | flops 342491136 | bytes 6636545 | tf_op jit(solution)/shard_map/while/body/eval_jaxpr/dot_general | solution.py:74
  183.5 3.5 %collective-permute-done.1 = bf16[1280,128]{1,0:T(8,128)(2,1)S(1)} collective-permute-done((bf16[1280,128]{1,0:T(8,128)(2,1)S(1)}, bf16[1280,128]{1,0:T(8,128)(2,1)S(1)}, u32[]{:S(2)}, u32[]{:S(2)}) %collective-permute-start.1) | collective-permute-done | bytes 327712 | tf_op jit(solution)/shard_map/while/body/eval_jaxpr/ppermute | solution.py:21
  188.1 0.8 dynamic_slice.72
  188.9 2.1 fusion.78
  191.0 2.3 copy-done.1
  193.3 1.8 fusion.79
  195.1 4.7 %fusion.81 = f32[1024,128]{1,0:T(8,128)} fusion(bf16[1280,128]{1,0:T(8,128)(2,1)S(1)} %copy.40, f32[1024,1280]{1,0:T(8,128)} %copy-done.1, f32[1024]{0:T(1024)S(1)} %select_maximum_fusion.2, s32[1280]{0:T(1024)S(1)} %pad_add_fusion.3, s32[1024]{0:T(1024)S(1)} %bitcast.68, f32[1024,128]{1,0:T(8,128)} %get-tuple-element.472, ...), kind=kOutput, calls=%fused_computation.8.clone.1 | convolution fusion | flops 342491136 | bytes 6636545 | tf_op jit(solution)/shard_map/while/body/eval_jaxpr/dot_general | solution.py:74
  199.8 4.5 %collective-permute-done.1 = bf16[1280,128]{1,0:T(8,128)(2,1)S(1)} collective-permute-done((bf16[1280,128]{1,0:T(8,128)(2,1)S(1)}, bf16[1280,128]{1,0:T(8,128)(2,1)S(1)}, u32[]{:S(2)}, u32[]{:S(2)}) %collective-permute-start.1) | collective-permute-done | bytes 327712 | tf_op jit(solution)/shard_map/while/body/eval_jaxpr/ppermute | solution.py:21
  204.5 0.7 fusion.77
  205.3 0.8 dynamic_slice.72
  206.1 2.1 fusion.78
  208.2 2.3 copy-done.1
  210.4 1.8 fusion.79
  212.3 4.7 %fusion.81 = f32[1024,128]{1,0:T(8,128)} fusion(bf16[1280,128]{1,0:T(8,128)(2,1)S(1)} %copy.40, f32[1024,1280]{1,0:T(8,128)} %copy-done.1, f32[1024]{0:T(1024)S(1)} %select_maximum_fusion.2, s32[1280]{0:T(1024)S(1)} %pad_add_fusion.3, s32[1024]{0:T(1024)S(1)} %bitcast.68, f32[1024,128]{1,0:T(8,128)} %get-tuple-element.472, ...), kind=kOutput, calls=%fused_computation.8.clone.1 | convolution fusion | flops 342491136 | bytes 6636545 | tf_op jit(solution)/shard_map/while/body/eval_jaxpr/dot_general | solution.py:74
  216.9 3.8 %collective-permute-done.1 = bf16[1280,128]{1,0:T(8,128)(2,1)S(1)} collective-permute-done((bf16[1280,128]{1,0:T(8,128)(2,1)S(1)}, bf16[1280,128]{1,0:T(8,128)(2,1)S(1)}, u32[]{:S(2)}, u32[]{:S(2)}) %collective-permute-start.1) | collective-permute-done | bytes 327712 | tf_op jit(solution)/shard_map/while/body/eval_jaxpr/ppermute | solution.py:21
  221.0 0.7 fusion.77
  221.8 0.8 dynamic_slice.72
  222.5 2.1 fusion.78
  224.6 2.3 copy-done.1
  226.9 1.8 fusion.79
  228.7 4.7 %fusion.81 = f32[1024,128]{1,0:T(8,128)} fusion(bf16[1280,128]{1,0:T(8,128)(2,1)S(1)} %copy.40, f32[1024,1280]{1,0:T(8,128)} %copy-done.1, f32[1024]{0:T(1024)S(1)} %select_maximum_fusion.2, s32[1280]{0:T(1024)S(1)} %pad_add_fusion.3, s32[1024]{0:T(1024)S(1)} %bitcast.68, f32[1024,128]{1,0:T(8,128)} %get-tuple-element.472, ...), kind=kOutput, calls=%fused_computation.8.clone.1 | convolution fusion | flops 342491136 | bytes 6636545 | tf_op jit(solution)/shard_map/while/body/eval_jaxpr/dot_general | solution.py:74
  233.4 2.9 collective-permute-done.1
  237.8 0.8 dynamic_slice.72
  238.6 2.1 fusion.78
  240.7 2.3 copy-done.1
  243.0 1.8 fusion.79
  244.8 4.7 %fusion.81 = f32[1024,128]{1,0:T(8,128)} fusion(bf16[1280,128]{1,0:T(8,128)(2,1)S(1)} %copy.40, f32[1024,1280]{1,0:T(8,128)} %copy-done.1, f32[1024]{0:T(1024)S(1)} %select_maximum_fusion.2, s32[1280]{0:T(1024)S(1)} %pad_add_fusion.3, s32[1024]{0:T(1024)S(1)} %bitcast.68, f32[1024,128]{1,0:T(8,128)} %get-tuple-element.472, ...), kind=kOutput, calls=%fused_computation.8.clone.1 | convolution fusion | flops 342491136 | bytes 6636545 | tf_op jit(solution)/shard_map/while/body/eval_jaxpr/dot_general | solution.py:74
  249.4 1.4 collective-permute-done.1
  251.0 1.6 collective-permute-start.1
  253.4 0.8 dynamic_slice.72
  254.1 2.1 fusion.78
  256.2 2.3 copy-done.1
  258.5 1.8 fusion.79
  260.3 4.7 %fusion.81 = f32[1024,128]{1,0:T(8,128)} fusion(bf16[1280,128]{1,0:T(8,128)(2,1)S(1)} %copy.40, f32[1024,1280]{1,0:T(8,128)} %copy-done.1, f32[1024]{0:T(1024)S(1)} %select_maximum_fusion.2, s32[1280]{0:T(1024)S(1)} %pad_add_fusion.3, s32[1024]{0:T(1024)S(1)} %bitcast.68, f32[1024,128]{1,0:T(8,128)} %get-tuple-element.472, ...), kind=kOutput, calls=%fused_computation.8.clone.1 | convolution fusion | flops 342491136 | bytes 6636545 | tf_op jit(solution)/shard_map/while/body/eval_jaxpr/dot_general | solution.py:74
  265.1 2.0 collective-permute-start.1
  268.0 0.8 dynamic_slice.72
  268.7 2.1 fusion.78
  270.8 2.3 copy-done.1
  273.1 1.8 fusion.79
  274.9 4.7 %fusion.81 = f32[1024,128]{1,0:T(8,128)} fusion(bf16[1280,128]{1,0:T(8,128)(2,1)S(1)} %copy.40, f32[1024,1280]{1,0:T(8,128)} %copy-done.1, f32[1024]{0:T(1024)S(1)} %select_maximum_fusion.2, s32[1280]{0:T(1024)S(1)} %pad_add_fusion.3, s32[1024]{0:T(1024)S(1)} %bitcast.68, f32[1024,128]{1,0:T(8,128)} %get-tuple-element.472, ...), kind=kOutput, calls=%fused_computation.8.clone.1 | convolution fusion | flops 342491136 | bytes 6636545 | tf_op jit(solution)/shard_map/while/body/eval_jaxpr/dot_general | solution.py:74
  279.6 2.1 fusion.14
  281.7 1.8 fusion.15
  283.6 1.9 fusion.25
  285.5 0.7 copy.26
  (135 shorter events, 10.5 us)
Async XLA Ops:
  7.2 146.4 %copy-start = (bf16[8192,128]{1,0:T(8,128)(2,1)S(1)}, bf16[8192,128]{1,0:T(8,128)(2,1)}, u32[]{:S(2)}) copy-start(bf16[8192,128]{1,0:T(8,128)(2,1)} %param.10) | copy-start | bytes 6291460
  7.2 25.3 %copy-start.3 = (bf16[256,128]{1,0:T(8,128)(2,1)S(1)}, bf16[256,128]{1,0:T(8,128)(2,1)}, u32[]{:S(2)}) copy-start(bf16[256,128]{1,0:T(8,128)(2,1)} %param.14) | copy-start | bytes 196612
  7.2 28.6 %copy-start.2 = (bf16[256,512]{1,0:T(8,128)(2,1)S(1)}, bf16[256,512]{1,0:T(8,128)(2,1)}, u32[]{:S(2)}) copy-start(bf16[256,512]{1,0:T(8,128)(2,1)} %param.13) | copy-start | bytes 786436
  7.2 146.4 %all-gather.2.cloned.1.call-start = ((), (), s32[]{:S(2)}) async-start(), calls=%async_computation.1 | async-start | bytes 17825792 | tf_op jit(solution)/shard_map/all_gather | solution.py:101
  33.8 133.0 %collective-permute-start.3 = (bf16[256,128]{0,1:T(8,128)(2,1)S(1)}, bf16[256,128]{0,1:T(8,128)(2,1)S(1)}, u32[]{:S(2)}, u32[]{:S(2)}) collective-permute-start(bf16[256,128]{0,1:T(8,128)(2,1)S(1)} %fusion.37), channel_id=1, source_target_pairs={{0,1},{1,0},{2,3},{3,2},{4,5},{5,4},{6,7},{7,6},{8,9},{9,8},{10,11... | collective-permute-start | bytes 196616 | tf_op jit(solution)/shard_map/ppermute | solution.py:16
  166.3 1.8 collective-permute-start.2
  168.7 14.8 %collective-permute-start = (bf16[1280,128]{1,0:T(8,128)(2,1)S(1)}, bf16[1280,128]{1,0:T(8,128)(2,1)S(1)}, u32[]{:S(2)}, u32[]{:S(2)}) collective-permute-start(bf16[1280,128]{1,0:T(8,128)(2,1)S(1)} %copy.39), channel_id=1, source_target_pairs={{0,16},{16,32},{32,48},{48,64},{64,80},{80,96},{96,112},{112,0},{1... | collective-permute-start | bytes 983048 | tf_op jit(solution)/shard_map/while/body/eval_jaxpr/ppermute | solution.py:21
  169.9 17.0 %collective-permute-start.1 = (bf16[1280,128]{1,0:T(8,128)(2,1)S(1)}, bf16[1280,128]{1,0:T(8,128)(2,1)S(1)}, u32[]{:S(2)}, u32[]{:S(2)}) collective-permute-start(bf16[1280,128]{1,0:T(8,128)(2,1)S(1)} %copy.40), channel_id=1, source_target_pairs={{0,16},{16,32},{32,48},{48,64},{64,80},{80,96},{96,112},{112,0},{1... | collective-permute-start | bytes 983048 | tf_op jit(solution)/shard_map/while/body/eval_jaxpr/ppermute | solution.py:21
  174.8 2.3 copy-start.1
  186.9 12.8 %collective-permute-start = (bf16[1280,128]{1,0:T(8,128)(2,1)S(1)}, bf16[1280,128]{1,0:T(8,128)(2,1)S(1)}, u32[]{:S(2)}, u32[]{:S(2)}) collective-permute-start(bf16[1280,128]{1,0:T(8,128)(2,1)S(1)} %copy.39), channel_id=1, source_target_pairs={{0,16},{16,32},{32,48},{48,64},{64,80},{80,96},{96,112},{112,0},{1... | collective-permute-start | bytes 983048 | tf_op jit(solution)/shard_map/while/body/eval_jaxpr/ppermute | solution.py:21
  187.1 17.2 %collective-permute-start.1 = (bf16[1280,128]{1,0:T(8,128)(2,1)S(1)}, bf16[1280,128]{1,0:T(8,128)(2,1)S(1)}, u32[]{:S(2)}, u32[]{:S(2)}) collective-permute-start(bf16[1280,128]{1,0:T(8,128)(2,1)S(1)} %copy.40), channel_id=1, source_target_pairs={{0,16},{16,32},{32,48},{48,64},{64,80},{80,96},{96,112},{112,0},{1... | collective-permute-start | bytes 983048 | tf_op jit(solution)/shard_map/while/body/eval_jaxpr/ppermute | solution.py:21
  191.0 2.3 copy-start.1
  204.3 12.6 %collective-permute-start = (bf16[1280,128]{1,0:T(8,128)(2,1)S(1)}, bf16[1280,128]{1,0:T(8,128)(2,1)S(1)}, u32[]{:S(2)}, u32[]{:S(2)}) collective-permute-start(bf16[1280,128]{1,0:T(8,128)(2,1)S(1)} %copy.39), channel_id=1, source_target_pairs={{0,16},{16,32},{32,48},{48,64},{64,80},{80,96},{96,112},{112,0},{1... | collective-permute-start | bytes 983048 | tf_op jit(solution)/shard_map/while/body/eval_jaxpr/ppermute | solution.py:21
  204.4 16.3 %collective-permute-start.1 = (bf16[1280,128]{1,0:T(8,128)(2,1)S(1)}, bf16[1280,128]{1,0:T(8,128)(2,1)S(1)}, u32[]{:S(2)}, u32[]{:S(2)}) collective-permute-start(bf16[1280,128]{1,0:T(8,128)(2,1)S(1)} %copy.40), channel_id=1, source_target_pairs={{0,16},{16,32},{32,48},{48,64},{64,80},{80,96},{96,112},{112,0},{1... | collective-permute-start | bytes 983048 | tf_op jit(solution)/shard_map/while/body/eval_jaxpr/ppermute | solution.py:21
  208.1 2.3 copy-start.1
  220.8 12.6 %collective-permute-start = (bf16[1280,128]{1,0:T(8,128)(2,1)S(1)}, bf16[1280,128]{1,0:T(8,128)(2,1)S(1)}, u32[]{:S(2)}, u32[]{:S(2)}) collective-permute-start(bf16[1280,128]{1,0:T(8,128)(2,1)S(1)} %copy.39), channel_id=1, source_target_pairs={{0,16},{16,32},{32,48},{48,64},{64,80},{80,96},{96,112},{112,0},{1... | collective-permute-start | bytes 983048 | tf_op jit(solution)/shard_map/while/body/eval_jaxpr/ppermute | solution.py:21
  220.9 15.4 %collective-permute-start.1 = (bf16[1280,128]{1,0:T(8,128)(2,1)S(1)}, bf16[1280,128]{1,0:T(8,128)(2,1)S(1)}, u32[]{:S(2)}, u32[]{:S(2)}) collective-permute-start(bf16[1280,128]{1,0:T(8,128)(2,1)S(1)} %copy.40), channel_id=1, source_target_pairs={{0,16},{16,32},{32,48},{48,64},{64,80},{80,96},{96,112},{112,0},{1... | collective-permute-start | bytes 983048 | tf_op jit(solution)/shard_map/while/body/eval_jaxpr/ppermute | solution.py:21
  224.6 2.3 copy-start.1
  236.3 13.2 %collective-permute-start = (bf16[1280,128]{1,0:T(8,128)(2,1)S(1)}, bf16[1280,128]{1,0:T(8,128)(2,1)S(1)}, u32[]{:S(2)}, u32[]{:S(2)}) collective-permute-start(bf16[1280,128]{1,0:T(8,128)(2,1)S(1)} %copy.39), channel_id=1, source_target_pairs={{0,16},{16,32},{32,48},{48,64},{64,80},{80,96},{96,112},{112,0},{1... | collective-permute-start | bytes 983048 | tf_op jit(solution)/shard_map/while/body/eval_jaxpr/ppermute | solution.py:21
  236.4 14.5 %collective-permute-start.1 = (bf16[1280,128]{1,0:T(8,128)(2,1)S(1)}, bf16[1280,128]{1,0:T(8,128)(2,1)S(1)}, u32[]{:S(2)}, u32[]{:S(2)}) collective-permute-start(bf16[1280,128]{1,0:T(8,128)(2,1)S(1)} %copy.40), channel_id=1, source_target_pairs={{0,16},{16,32},{32,48},{48,64},{64,80},{80,96},{96,112},{112,0},{1... | collective-permute-start | bytes 983048 | tf_op jit(solution)/shard_map/while/body/eval_jaxpr/ppermute | solution.py:21
  240.7 2.3 copy-start.1
  250.9 14.1 %collective-permute-start = (bf16[1280,128]{1,0:T(8,128)(2,1)S(1)}, bf16[1280,128]{1,0:T(8,128)(2,1)S(1)}, u32[]{:S(2)}, u32[]{:S(2)}) collective-permute-start(bf16[1280,128]{1,0:T(8,128)(2,1)S(1)} %copy.39), channel_id=1, source_target_pairs={{0,16},{16,32},{32,48},{48,64},{64,80},{80,96},{96,112},{112,0},{1... | collective-permute-start | bytes 983048 | tf_op jit(solution)/shard_map/while/body/eval_jaxpr/ppermute | solution.py:21
  251.0 14.0 %collective-permute-start.1 = (bf16[1280,128]{1,0:T(8,128)(2,1)S(1)}, bf16[1280,128]{1,0:T(8,128)(2,1)S(1)}, u32[]{:S(2)}, u32[]{:S(2)}) collective-permute-start(bf16[1280,128]{1,0:T(8,128)(2,1)S(1)} %copy.40), channel_id=1, source_target_pairs={{0,16},{16,32},{32,48},{48,64},{64,80},{80,96},{96,112},{112,0},{1... | collective-permute-start | bytes 983048 | tf_op jit(solution)/shard_map/while/body/eval_jaxpr/ppermute | solution.py:21
  256.2 2.3 copy-start.1
  265.0 14.6 %collective-permute-start = (bf16[1280,128]{1,0:T(8,128)(2,1)S(1)}, bf16[1280,128]{1,0:T(8,128)(2,1)S(1)}, u32[]{:S(2)}, u32[]{:S(2)}) collective-permute-start(bf16[1280,128]{1,0:T(8,128)(2,1)S(1)} %copy.39), channel_id=1, source_target_pairs={{0,16},{16,32},{32,48},{48,64},{64,80},{80,96},{96,112},{112,0},{1... | collective-permute-start | bytes 983048 | tf_op jit(solution)/shard_map/while/body/eval_jaxpr/ppermute | solution.py:21
  265.1 14.4 %collective-permute-start.1 = (bf16[1280,128]{1,0:T(8,128)(2,1)S(1)}, bf16[1280,128]{1,0:T(8,128)(2,1)S(1)}, u32[]{:S(2)}, u32[]{:S(2)}) collective-permute-start(bf16[1280,128]{1,0:T(8,128)(2,1)S(1)} %copy.40), channel_id=1, source_target_pairs={{0,16},{16,32},{32,48},{48,64},{64,80},{80,96},{96,112},{112,0},{1... | collective-permute-start | bytes 983048 | tf_op jit(solution)/shard_map/while/body/eval_jaxpr/ppermute | solution.py:21
  270.8 2.3 copy-start.1
  279.6 4.0 %copy-start.4 = (f32[1024,128]{1,0:T(8,128)S(1)}, f32[1024,128]{1,0:T(8,128)}, u32[]{:S(2)}) copy-start(f32[1024,128]{1,0:T(8,128)} %get-tuple-element.271) | copy-start | bytes 1572868
Sparse Core Ops, SparseCore 0:
  32.6 120.9 all-gather.1
where the time goes:
time: 299 us; the launch traced here: 293 us
  waiting for transfers between devices  131 us (44%)
  matrix products  62.4 us (21%)
  other arithmetic  27.9 us (9%)
  local copies, waits for them, and re-layouts  26.5 us (9%)
  blocking collectives  20.6 us (7%)
  between operations  14.3 us (5%)
  starting transfers between devices  10.2 us (3%)
    all_gather x1, waiting for transfers between devices, local(): lax.all_gather(arrived_flat, 'tp', axis=1, tiled=True)  114 us
    dot_general x8, matrix products, attend(): jnp.dot(weights.astype(jnp.bfloat16), value_block, preferred_element_type...  34.4 us
    all_to_all x1, blocking collectives, local(): lax.all_to_all(outgoing, 'ctx', split_axis=0, concat_axis=0, tiled=True)  20.6 us
    dot_general x8, matrix products, attend(): lax.dot_general(query_flat, key_block, (((1,), (1,)), ((), ())), preferre...  16.6 us
    while x49, local copies, waits for them, and re-layouts  16.3 us
    ppermute x14, waiting for transfers between devices, passed_along(): lax.ppermute(value, axis, [(i, (i + by) % peers) for i in range(peers)])  16.1 us
    reduce_sum x8, other arithmetic, attend(): denominator = denominator * decay + jnp.sum(weights, axis=1)  14.3 us
    dot_general x1, matrix products, local(): jnp.dot(lax.all_gather(arrived_flat, 'tp', axis=1, tiled=True), kv_weight...  11.4 us
  transfers between devices with their start and end apart: 17, of which 7 were waited for; matrix products, arithmetic and copies ran while one was open for 30% of the time, Pallas kernels for 0%

commit v1 on v0

v1 whole, which is shorter than its diff:
```python
import functools
import math

import jax
import jax.numpy as jnp
from jax import lax
from jax.experimental import pallas as pl
from jax.experimental.pallas import tpu as pltpu
from jax.sharding import PartitionSpec as P

HEAD_DIM = 128
PAGE = 128
SOURCES = 8
huge_value = 1e30
SCORE_SCALE = math.log2(math.e) / math.sqrt(HEAD_DIM)
VMEM_BYTES = 32 * 1024 * 1024


def swapped(value, bits):
    return lax.ppermute(value, "tp", [(i, i ^ bits) for i in range(lax.axis_size("tp"))])


def inverse_freq(head_width):
    half_width = head_width // 2
    exponent = jnp.arange(half_width, dtype=jnp.float32) * 2.0 / head_width
    base_freq = jnp.exp(-exponent * math.log(500000.0))
    wavelength = 2.0 * math.pi / base_freq
    smooth = (8192.0 / wavelength - 1.0) / 3.0
    blended = (1.0 - smooth) * base_freq / 8.0 + smooth * base_freq
    return jnp.where(
        wavelength < 2048.0, base_freq, jnp.where(wavelength > 8192.0, base_freq / 8.0, blended)
    )


def rope_tables(positions):
    angle = positions.astype(jnp.float32)[:, None] * inverse_freq(HEAD_DIM)[None, :]
    cosine = jnp.cos(angle)
    sine = jnp.sin(angle)
    return (
        jnp.concatenate([cosine, cosine], axis=1),
        jnp.concatenate([-sine, sine], axis=1),
    )


def turned(value, cosine, sine):
    return value * cosine + pltpu.roll(value, HEAD_DIM // 2, 1) * sine


def any_spec():
    return pl.BlockSpec(memory_space=pl.ANY)


def vmem_spec():
    return pl.BlockSpec(memory_space=pltpu.VMEM)


def smem_spec():
    return pl.BlockSpec(memory_space=pltpu.SMEM)


def prepare_kernel(queries, turn_kv, cosine, sine, query_out, turn_out):
    is_key = lax.axis_index("tp") % 2 == 0
    c = cosine[...]
    s = sine[...]
    for head in range(query_out.shape[0]):
        block = queries[:, head * HEAD_DIM : (head + 1) * HEAD_DIM].astype(jnp.float32)
        query_out[head] = turned(block, c, s).astype(jnp.bfloat16)
    block = turn_kv[...].astype(jnp.float32)
    block = turned(block, jnp.where(is_key, c, 1.0), jnp.where(is_key, s, 0.0)).astype(jnp.bfloat16)
    for peer in range(SOURCES):
        turn_out[peer] = block


def project_kernel(x0, x1, x2, x3, weight, w1, w2, w3, own_out, out1, out2, out3, x_buf, w_buf, sems):
    tp = lax.axis_index("tp")
    core = tp % 2
    pair = tp // 8
    spot = (tp // 2) % 4
    depth = x_buf.shape[2]
    copies = []
    for r, x in enumerate((x0, x1, x2, x3)):
        at = spot ^ r
        row = ((pair * 4 + at) * 2 + core) * depth
        group = [pltpu.make_async_copy(x, x_buf.at[r], sems.at[r, 0])]
        group.append(
            pltpu.make_async_copy(
                weight.at[pl.ds(pl.multiple_of(row, depth), depth)],
                w_buf.at[r, :, pl.ds(0, HEAD_DIM)],
                sems.at[r, 1],
            )
        )
        for b, w in enumerate((w1, w2, w3)):
            group.append(
                pltpu.make_async_copy(
                    w.at[at], w_buf.at[r, :, pl.ds((b + 1) * HEAD_DIM, HEAD_DIM)], sems.at[r, b + 2]
                )
            )
        for copy in group:
            copy.start()
        copies.append(group)
    total = None
    for r in range(4):
        for copy in copies[r]:
            copy.wait()
        part = jnp.dot(x_buf[r], w_buf[r], preferred_element_type=jnp.float32)
        total = part if total is None else total + part
    own_out[...] = total[:, :HEAD_DIM]
    for b, out in enumerate((out1, out2, out3)):
        out[...] = total[:, (b + 1) * HEAD_DIM : (b + 2) * HEAD_DIM].astype(jnp.bfloat16)


def finish_kernel(own, p1, p2, p3, cosine, sine, out):
    is_key = lax.axis_index("tp") % 2 == 0
    value = own[...] + p1[...].astype(jnp.float32)
    value = value + (p2[...].astype(jnp.float32) + p3[...].astype(jnp.float32))
    c = jnp.where(is_key, cosine[...], 1.0)
    s = jnp.where(is_key, sine[...], 0.0)
    block = turned(value, c, s).astype(jnp.bfloat16)
    for peer in range(SOURCES):
        out[peer] = block


def scores_of(query, keys):
    return lax.dot_general(
        query, keys, (((1,), (1,)), ((), ())), preferred_element_type=jnp.float32
    )


def softmax_step(state, scores, values):
    top, total, acc = state
    new_top = jnp.maximum(top, jnp.max(scores, axis=1, keepdims=True))
    decay = jnp.exp2((top - new_top) * SCORE_SCALE)
    weights = jnp.exp2((scores - new_top) * SCORE_SCALE)
    total = total * decay + jnp.sum(weights, axis=1, keepdims=True)
    acc = acc * decay + jnp.dot(
        weights.astype(jnp.bfloat16), values, preferred_element_type=jnp.float32
    )
    return new_top, total, acc


def load_pair(own, other, key_buf, value_buf, sems, act):
    core = lax.axis_index("tp") % 2

    @pl.when(core == 0)
    def _():
        act(pltpu.make_async_copy(own, key_buf, sems.at[0]))
        act(pltpu.make_async_copy(other, value_buf, sems.at[1]))

    @pl.when(core == 1)
    def _():
        act(pltpu.make_async_copy(other, key_buf, sems.at[0]))
        act(pltpu.make_async_copy(own, value_buf, sems.at[1]))


def turn_kernel(queries, own, other, top_out, total_out, acc_out, key_buf, value_buf, sems):
    ctx = lax.axis_index("ctx")
    heads, rows, _ = queries.shape
    load_pair(own, other, key_buf, value_buf, sems, lambda copy: copy.start())
    load_pair(own, other, key_buf, value_buf, sems, lambda copy: copy.wait())
    shape = (rows, rows)
    seen = lax.broadcasted_iota(jnp.int32, shape, 1) <= lax.broadcasted_iota(jnp.int32, shape, 0)

    def keep(head, state):
        top, total, acc = state
        top_out[head] = jnp.broadcast_to(top, (rows, HEAD_DIM))
        total_out[head] = jnp.broadcast_to(total, (rows, HEAD_DIM))
        acc_out[head] = acc

    for head in range(heads):
        scores = jnp.where(seen, scores_of(queries[head], key_buf[ctx]), -huge_value)
        top = jnp.max(scores, axis=1, keepdims=True)
        weights = jnp.exp2((scores - top) * SCORE_SCALE)
        total = jnp.sum(weights, axis=1, keepdims=True)
        acc = jnp.dot(
            weights.astype(jnp.bfloat16), value_buf[ctx], preferred_element_type=jnp.float32
        )
        keep(head, (top, total, acc))

    def source_step(source, carried):
        for head in range(heads):
            state = (top_out[head][:, :1], total_out[head][:, :1], acc_out[head])
            scores = scores_of(queries[head], key_buf[source])
            keep(head, softmax_step(state, scores, value_buf[source]))
        return carried

    lax.fori_loop(0, ctx, source_step, 0)


def page_kernel(
    page_table, page_counts, queries, own, other, top_in, total_in, acc_in,
    out, cache_out, key_buf, value_buf, zero_buf, sems, cache_sems,
):
    ctx = lax.axis_index("ctx")
    core = lax.axis_index("tp") % 2
    heads, rows, _ = queries.shape
    chunk = 1024
    zero_buf[...] = jnp.zeros_like(zero_buf)
    load_pair(own, other, key_buf, value_buf, sems, lambda copy: copy.start())
    load_pair(own, other, key_buf, value_buf, sems, lambda copy: copy.wait())

    def cache_copy(slot, source):
        return pltpu.make_async_copy(
            source, cache_out.at[pl.ds(slot * PAGE, PAGE)], cache_sems.at[slot]
        )

    for slot in range(SOURCES):
        live = page_counts[ctx, slot] > 0
        start = pl.multiple_of(page_table[ctx, slot] * PAGE, PAGE)

        @pl.when(jnp.logical_and(live, core == 0))
        def _():
            cache_copy(slot, key_buf.at[pl.ds(start, PAGE)]).start()

        @pl.when(jnp.logical_and(live, core == 1))
        def _():
            cache_copy(slot, value_buf.at[pl.ds(start, PAGE)]).start()

        @pl.when(jnp.logical_not(live))
        def _():
            cache_copy(slot, zero_buf).start()

    for head in range(heads):
        state = (top_in[head][:, :1], total_in[head][:, :1], acc_in[head])
        for at in range(0, key_buf.shape[0], chunk):
            scores = scores_of(queries[head], key_buf[at : at + chunk])
            state = softmax_step(state, scores, value_buf[at : at + chunk])
        out[:, head * HEAD_DIM : (head + 1) * HEAD_DIM] = (state[2] / state[1]).astype(jnp.bfloat16)
    for slot in range(SOURCES):
        cache_copy(slot, zero_buf).wait()


def local(stored_pages, kv_weight, page_table, page_counts, queries, turn_kv, turn_pos):
    ctx_index = lax.axis_index("ctx")
    tp_index = lax.axis_index("tp")
    core = tp_index % 2
    pair = tp_index // 8
    held, page_rows, width = stored_pages.shape
    rows = held * page_rows
    tok_new = queries.shape[0]
    heads_dev = queries.shape[1] // HEAD_DIM
    bf16 = jnp.bfloat16
    f32 = jnp.float32
    params = pltpu.CompilerParams(vmem_limit_bytes=VMEM_BYTES)

    own_x = stored_pages.reshape(rows, width)
    by_group = kv_weight.reshape(2, 4, 2, width, HEAD_DIM)

    def weight_rows(which_pair, which_core):
        picked = lax.dynamic_slice(
            by_group, (which_pair, 0, which_core, 0, 0), (1, 4, 1, width, HEAD_DIM)
        )
        return picked.reshape(4, width, HEAD_DIM)

    w2 = swapped(weight_rows(1 - pair, core), 12)
    w3 = swapped(weight_rows(1 - pair, 1 - core), 13)
    x1 = swapped(own_x, 2)
    x2 = swapped(own_x, 4)
    x3 = swapped(own_x, 6)
    w1 = swapped(weight_rows(pair, 1 - core), 1)

    local_pos = lax.dynamic_slice_in_dim(turn_pos, ctx_index * tok_new, tok_new)
    page_pos = ctx_index * rows + jnp.arange(rows, dtype=jnp.int32)
    cosine, sine = rope_tables(jnp.concatenate([local_pos, page_pos]))

    query_heads, turn_block = pl.pallas_call(
        prepare_kernel,
        out_shape=(
            jax.ShapeDtypeStruct((heads_dev, tok_new, HEAD_DIM), bf16),
            jax.ShapeDtypeStruct((SOURCES, tok_new, HEAD_DIM), bf16),
        ),
        in_specs=[vmem_spec()] * 4,
        out_specs=(vmem_spec(), vmem_spec()),
        compiler_params=params,
        name="prepare",
    )(queries, turn_kv, cosine[:tok_new], sine[:tok_new])
    own_turn = lax.all_to_all(turn_block, "ctx", split_axis=0, concat_axis=0)
    other_turn = swapped(own_turn, 1)

    state_shape = jax.ShapeDtypeStruct((heads_dev, tok_new, HEAD_DIM), f32)
    state = pl.pallas_call(
        turn_kernel,
        out_shape=(state_shape,) * 3,
        in_specs=[vmem_spec(), any_spec(), any_spec()],
        out_specs=(vmem_spec(),) * 3,
        scratch_shapes=[
            pltpu.VMEM((SOURCES, tok_new, HEAD_DIM), bf16),
            pltpu.VMEM((SOURCES, tok_new, HEAD_DIM), bf16),
            pltpu.SemaphoreType.DMA((2,)),
        ],
        compiler_params=params,
        name="turn_attention",
    )(query_heads, own_turn, other_turn)

    part_shape = jax.ShapeDtypeStruct((rows, HEAD_DIM), bf16)
    own_part, part1, part2, part3 = pl.pallas_call(
        project_kernel,
        out_shape=(jax.ShapeDtypeStruct((rows, HEAD_DIM), f32),) + (part_shape,) * 3,
        in_specs=[any_spec()] * 8,
        out_specs=(vmem_spec(),) * 4,
        scratch_shapes=[
            pltpu.VMEM((4, rows, width), bf16),
            pltpu.VMEM((4, width, 4 * HEAD_DIM), bf16),
            pltpu.SemaphoreType.DMA((4, 5)),
        ],
        compiler_params=params,
        name="project",
    )(own_x, x1, x2, x3, kv_weight, w1, w2, w3)
    got1 = swapped(part1, 1)
    got2 = swapped(part2, 12)
    got3 = swapped(part3, 13)
    own_block = pl.pallas_call(
        finish_kernel,
        out_shape=jax.ShapeDtypeStruct((SOURCES, rows, HEAD_DIM), bf16),
        in_specs=[vmem_spec()] * 6,
        out_specs=vmem_spec(),
        compiler_params=params,
        name="finish",
    )(own_part, got1, got2, got3, cosine[tok_new:], sine[tok_new:])
    own_pages = lax.all_to_all(own_block, "ctx", split_axis=0, concat_axis=0)
    own_pages = own_pages.reshape(SOURCES * rows, HEAD_DIM)
    other_pages = swapped(own_pages, 1)

    attended, cache = pl.pallas_call(
        page_kernel,
        out_shape=(
            jax.ShapeDtypeStruct((tok_new, heads_dev * HEAD_DIM), bf16),
            jax.ShapeDtypeStruct((SOURCES * PAGE, HEAD_DIM), bf16),
        ),
        in_specs=[smem_spec(), smem_spec(), vmem_spec(), any_spec(), any_spec()] + [vmem_spec()] * 3,
        out_specs=(vmem_spec(), any_spec()),
        scratch_shapes=[
            pltpu.VMEM((SOURCES * rows, HEAD_DIM), bf16),
            pltpu.VMEM((SOURCES * rows, HEAD_DIM), bf16),
            pltpu.VMEM((PAGE, HEAD_DIM), bf16),
            pltpu.SemaphoreType.DMA((2,)),
            pltpu.SemaphoreType.DMA((SOURCES,)),
        ],
        compiler_params=params,
        name="page_attention",
    )(page_table, page_counts, query_heads, own_pages, other_pages, *state)
    return (attended, cache)


def solution(mesh):
    placed = (P("ctx", None, "tp"), P(None, "tp"), P(), P(), P("ctx", "tp"), P("ctx", "tp"), P())
    return jax.shard_map(
        local,
        mesh=mesh,
        in_specs=placed,
        out_specs=(P("ctx", "tp"), P("ctx", "tp")),
        check_vma=False,
    )
```

time: 299 us -> 109 us (0.36)
  the two profiles are of different devices: /device:TPU:1 before, /device:TPU:15 now
where the time goes in v1:
time: 109 us
  waiting for transfers between devices  39.4 us (36%)
  Pallas kernels  34.4 us (32%)
  starting transfers between devices  29.1 us (27%)
  local copies, waits for them, and re-layouts  3.55 us (3%)
  other arithmetic  1.56 us (1%)
    ppermute x11, waiting for transfers between devices, swapped(): lax.ppermute(value, 'tp', [(i, i ^ bits) for i in range(lax.axis_size('tp...  24.8 us
    pallas_call x1, Pallas kernels, local(): pl.pallas_call(turn_kernel, out_shape=(state_shape,) * 3, in_specs=[vmem_...  20.2 us
    ppermute x11, starting transfers between devices, swapped(): lax.ppermute(value, 'tp', [(i, i ^ bits) for i in range(lax.axis_size('tp...  17.4 us
    pallas_call x1, Pallas kernels, local(): pl.pallas_call(page_kernel, out_shape=(jax.ShapeDtypeStruct((tok_new, hea...  9.5 us
    all_to_all x1, waiting for transfers between devices, local(): own_pages = lax.all_to_all(own_block, 'ctx', split_axis=0, concat_axis=0)  8.67 us
    all_to_all x1, starting transfers between devices, local(): own_turn = lax.all_to_all(turn_block, 'ctx', split_axis=0, concat_axis=0)  6.57 us
    all_to_all x1, waiting for transfers between devices, local(): own_turn = lax.all_to_all(turn_block, 'ctx', split_axis=0, concat_axis=0)  5.85 us
    all_to_all x1, starting transfers between devices, local(): own_pages = lax.all_to_all(own_block, 'ctx', split_axis=0, concat_axis=0)  5.11 us
  transfers between devices with their start and end apart: 13, of which 8 were waited for; matrix products, arithmetic and copies ran while one was open for 5% of the time, Pallas kernels for 19%

profile of v1, /device:TPU:15, one launch (start us, length us, event | category | flops | bytes accessed | tf_op | source)
XLA Modules:
  0.0 108.9 jit_solution(18296804486420254085)
XLA Ops:
  0.6 0.0 copy-start.1
  0.6 2.1 %collective-permute-start = (bf16[384,512]{1,0:T(8,128)(2,1)}, bf16[384,512]{1,0:T(8,128)(2,1)}, u32[]{:S(2)}, u32[]{:S(2)}) collective-permute-start(bf16[384,512]{1,0:T(8,128)(2,1)} %bitcast.18), channel_id=1, source_target_pairs={{0,2},{1,3},{2,0},{3,1},{4,6},{5,7},{6,4},{7,5},{8,10},{9,11},{10,... | collective-permute-start | bytes 1179656 | tf_op jit(solution)/shard_map/ppermute | solution.py:20
  2.7 1.6 %collective-permute-start.1 = (bf16[384,512]{1,0:T(8,128)(2,1)}, bf16[384,512]{1,0:T(8,128)(2,1)}, u32[]{:S(2)}, u32[]{:S(2)}) collective-permute-start(bf16[384,512]{1,0:T(8,128)(2,1)} %bitcast.19), channel_id=1, source_target_pairs={{0,4},{1,5},{2,6},{3,7},{4,0},{5,1},{6,2},{7,3},{8,12},{9,13},{10,... | collective-permute-start | bytes 1179656 | tf_op jit(solution)/shard_map/ppermute | solution.py:20
  4.4 0.0 copy-start
  4.4 2.7 %dynamic-slice_bitcast_fusion = (bf16[4,512,128]{2,1,0:T(8,128)(2,1)}, bf16[4,512,128]{2,1,0:T(8,128)(2,1)}, bf16[4,512,128]{2,1,0:T(8,128)(2,1)}) fusion(bf16[2,4,2,512,128]{4,3,2,1,0:T(8,128)(2,1)} %bitcast.15, s32[]{:T(128)S(6)} %select_n.50, s32[]{:T(128)S(6)} %select_n.49, s32[]{:T(128)S(6)} %select_n.51, s32[]{:T(128)S(6)} %select_n.47), kind=kLoop, calls=%fused_computation | loop fusion | bytes 3145744 | tf_op jit(solution)/shard_map/reshape | solution.py:252
  7.1 1.2 %collective-permute-start.3 = (bf16[4,512,128]{2,1,0:T(8,128)(2,1)}, bf16[4,512,128]{2,1,0:T(8,128)(2,1)S(1)}, u32[]{:S(2)}, u32[]{:S(2)}) collective-permute-start(bf16[4,512,128]{2,1,0:T(8,128)(2,1)} %get-tuple-element.22), channel_id=1, source_target_pairs={{0,1},{1,0},{2,3},{3,2},{4,5},{5,4},{6,7},{7,6},{8,9},{9,8},{10,11... | collective-permute-start | bytes 1572872 | tf_op jit(solution)/shard_map/ppermute | solution.py:20
  8.3 2.2 %collective-permute-start.4 = (bf16[4,512,128]{2,1,0:T(8,128)(2,1)}, bf16[4,512,128]{2,1,0:T(8,128)(2,1)S(1)}, u32[]{:S(2)}, u32[]{:S(2)}) collective-permute-start(bf16[4,512,128]{2,1,0:T(8,128)(2,1)} %get-tuple-element.21), channel_id=1, source_target_pairs={{0,12},{1,13},{2,14},{3,15},{4,8},{5,9},{6,10},{7,11},{8,4},{9,5},... | collective-permute-start | bytes 1572872 | tf_op jit(solution)/shard_map/ppermute | solution.py:20
  10.6 0.6 collective-permute-start.5
  11.2 1.3 %collective-permute-done.x1 = bf16[384,512]{1,0:T(8,128)(2,1)} collective-permute-done((bf16[384,512]{1,0:T(8,128)(2,1)}, bf16[384,512]{1,0:T(8,128)(2,1)}, u32[]{:S(2)}, u32[]{:S(2)}) %collective-permute-start) | collective-permute-done | bytes 393248 | tf_op jit(solution)/shard_map/ppermute | solution.py:20
  12.5 0.0 copy-done.1
  12.5 3.4 %collective-permute-start.2 = (bf16[384,512]{1,0:T(8,128)(2,1)S(1)}, bf16[384,512]{1,0:T(8,128)(2,1)}, u32[]{:S(2)}, u32[]{:S(2)}) collective-permute-start(bf16[384,512]{1,0:T(8,128)(2,1)S(1)} %bitcast.20), channel_id=1, source_target_pairs={{0,6},{1,7},{2,4},{3,5},{4,2},{5,3},{6,0},{7,1},{8,14},{9,15},{10,... | collective-permute-start | bytes 1179656 | tf_op jit(solution)/shard_map/ppermute | solution.py:20
  15.9 0.8 dynamic_slice.12
  16.7 1.2 %fusion = (f32[640,64]{1,0:T(8,128)S(1)}, f32[640,64]{1,0:T(8,128)S(1)}, f32[640,64]{1,0:T(8,128)S(1)}) fusion(f32[64]{0:T(128)S(1)} %compare_select_fusion.1, f32[640]{0:T(1024)S(1)} %add_convert_fusion), kind=kLoop, calls=%fused_computation.9 | loop fusion | flops 81920 | bytes 494336 | tf_op jit(solution)/shard_map/neg | solution.py:41
  17.9 0.0 copy-start.6
  17.9 0.0 copy-start.8
  17.9 0.0 copy-start.10
  17.9 0.0 collective-permute-done.1.x2
  18.0 6.1 %collective-permute-done.2.x3 = bf16[384,512]{1,0:T(8,128)(2,1)} collective-permute-done((bf16[384,512]{1,0:T(8,128)(2,1)S(1)}, bf16[384,512]{1,0:T(8,128)(2,1)}, u32[]{:S(2)}, u32[]{:S(2)}) %collective-permute-start.2) | collective-permute-done | bytes 393248 | tf_op jit(solution)/shard_map/ppermute | solution.py:20
  24.1 0.0 collective-permute-done.3.w1
  24.1 0.0 collective-permute-done.4.w2
  24.1 10.7 %collective-permute-done.5.w3 = bf16[4,512,128]{2,1,0:T(8,128)(2,1)} collective-permute-done((bf16[4,512,128]{2,1,0:T(8,128)(2,1)}, bf16[4,512,128]{2,1,0:T(8,128)(2,1)}, u32[]{:S(2)}, u32[]{:S(2)}) %collective-permute-start.5) | collective-permute-done | bytes 524320 | tf_op jit(solution)/shard_map/ppermute | solution.py:20
  34.8 0.0 copy-done
  34.8 2.6 %project.1 = (f32[384,128]{1,0:T(8,128)S(1)}, bf16[384,128]{1,0:T(8,128)(2,1)S(1)}, bf16[384,128]{1,0:T(8,128)(2,1)S(1)}, bf16[384,128]{1,0:T(8,128)(2,1)S(1)}) custom-call(bf16[384,512]{1,0:T(8,128)(2,1)S(1)} %bitcast.21, bf16[384,512]{1,0:T(8,128)(2,1)} %collective-permute-done.x1, bf16[384,512]{1,0:T(8,128)(2,1)} %collective-permute-done.1.x2, ...), custom_call_target="tpu_custom_call" | custom-call | tf_op jit(solution)/shard_map/project/pallas_call | solution.py:295
  37.4 0.4 collective-permute-start.6
  37.8 2.2 %collective-permute-start.7 = (bf16[384,128]{1,0:T(8,128)(2,1)S(1)}, bf16[384,128]{1,0:T(8,128)(2,1)S(1)}, u32[]{:S(2)}, u32[]{:S(2)}) collective-permute-start(bf16[384,128]{1,0:T(8,128)(2,1)S(1)} %get-tuple-element.14), channel_id=1, source_target_pairs={{0,12},{1,13},{2,14},{3,15},{4,8},{5,9},{6,10},{7,11},{8,4},{9,5},... | collective-permute-start | bytes 294920 | tf_op jit(solution)/shard_map/ppermute | solution.py:20
  40.0 0.8 collective-permute-start.8
  40.8 0.0 copy-done.6
  40.8 0.0 copy-done.8
  40.8 0.0 copy-done.10
  40.8 0.2 pad_maximum_fusion
  41.0 0.0 copy-start.7
  41.0 0.0 copy-start.9
  41.0 0.0 copy-start.11
  41.0 0.0 collective-permute-done.6.p1
  41.0 2.1 %collective-permute-done.7.p2 = bf16[384,128]{1,0:T(8,128)(2,1)S(1)} collective-permute-done((bf16[384,128]{1,0:T(8,128)(2,1)S(1)}, bf16[384,128]{1,0:T(8,128)(2,1)S(1)}, u32[]{:S(2)}, u32[]{:S(2)}) %collective-permute-start.7) | collective-permute-done | bytes 98336 | tf_op jit(solution)/shard_map/ppermute | solution.py:20
  43.2 3.0 %collective-permute-done.8.p3 = bf16[384,128]{1,0:T(8,128)(2,1)S(1)} collective-permute-done((bf16[384,128]{1,0:T(8,128)(2,1)S(1)}, bf16[384,128]{1,0:T(8,128)(2,1)S(1)}, u32[]{:S(2)}, u32[]{:S(2)}) %collective-permute-start.8) | collective-permute-done | bytes 98336 | tf_op jit(solution)/shard_map/ppermute | solution.py:20
  46.2 0.0 copy-start.2
  46.2 0.0 copy-start.3
  46.2 1.0 finish.1
  47.2 5.1 %all-to-all-start = ((bf16[8,384,128]{2,1,0:T(8,128)(2,1)}), bf16[8,384,128]{2,1,0:T(8,128)(2,1)S(1)}, u32[]{:S(2)}, u32[]{:S(2)}) async-start(bf16[8,384,128]{2,1,0:T(8,128)(2,1)} %finish.1), calls=%async_computation | async-start | bytes 1572864 | tf_op jit(solution)/shard_map/all_to_all | solution.py:319
  52.4 0.0 copy-done.7
  52.4 0.0 copy-done.9
  52.4 0.0 copy-done.11
  52.4 0.0 copy-start.4
  52.4 0.0 copy-start.5
  52.4 0.1 pad_maximum_fusion.2
  52.5 0.0 copy-done.2
  52.6 0.0 copy-done.3
  52.6 1.0 prepare.1
  53.6 8.7 %all-to-all-done = bf16[8,384,128]{2,1,0:T(8,128)(2,1)S(1)} async-done(((bf16[8,384,128]{2,1,0:T(8,128)(2,1)}), bf16[8,384,128]{2,1,0:T(8,128)(2,1)S(1)}, u32[]{:S(2)}, u32[]{:S(2)}) %all-to-all-start) | async-done | bytes 786464 | tf_op jit(solution)/shard_map/all_to_all | solution.py:319
  62.3 6.6 %all-to-all-start.1 = ((bf16[8,256,128]{2,1,0:T(8,128)(2,1)}), bf16[8,256,128]{2,1,0:T(8,128)(2,1)S(1)}, u32[]{:S(2)}, u32[]{:S(2)}) async-start(bf16[8,256,128]{2,1,0:T(8,128)(2,1)} %get-tuple-element.16), calls=%async_computation.1 | async-start | bytes 1048576 | tf_op jit(solution)/shard_map/all_to_all | solution.py:276
  68.8 1.1 collective-permute-start.9
  69.9 5.8 %all-to-all-done.1.own = bf16[8,256,128]{2,1,0:T(8,128)(2,1)S(1)} async-done(((bf16[8,256,128]{2,1,0:T(8,128)(2,1)}), bf16[8,256,128]{2,1,0:T(8,128)(2,1)S(1)}, u32[]{:S(2)}, u32[]{:S(2)}) %all-to-all-start.1) | async-done | bytes 524320 | tf_op jit(solution)/shard_map/all_to_all | solution.py:276
  75.8 1.7 %collective-permute-start.10 = (bf16[8,256,128]{2,1,0:T(8,128)(2,1)S(1)}, bf16[8,256,128]{2,1,0:T(8,128)(2,1)S(1)}, u32[]{:S(2)}, u32[]{:S(2)}) collective-permute-start(bf16[8,256,128]{2,1,0:T(8,128)(2,1)S(1)} %all-to-all-done.1.own), channel_id=1, source_target_pairs={{0,1},{1,0},{2,3},{3,2},{4,5},{5,4},{6,7},{7,6},{8,9},{9,8},{10,11... | collective-permute-start | bytes 1572872 | tf_op jit(solution)/shard_map/ppermute | solution.py:20
  77.5 1.5 %collective-permute-done.10.other = bf16[8,256,128]{2,1,0:T(8,128)(2,1)S(1)} collective-permute-done((bf16[8,256,128]{2,1,0:T(8,128)(2,1)S(1)}, bf16[8,256,128]{2,1,0:T(8,128)(2,1)S(1)}, u32[]{:S(2)}, u32[]{:S(2)}) %collective-permute-start.10) | collective-permute-done | bytes 524320 | tf_op jit(solution)/shard_map/ppermute | solution.py:20
  79.0 20.2 %turn_attention.1 = (f32[4,256,128]{2,1,0:T(8,128)S(1)}, f32[4,256,128]{2,1,0:T(8,128)S(1)}, f32[4,256,128]{2,1,0:T(8,128)S(1)}) custom-call(bf16[4,256,128]{2,1,0:T(8,128)(2,1)S(1)} %get-tuple-element.11.queries, bf16[8,256,128]{2,1,0:T(8,128)(2,1)S(1)} %all-to-all-done.1.own, bf16[8,256,128]{2,1,0:T(8,128)(2,1)S(1)} %collective-permute-done.10.other), custom_call_target="tpu_custom_call" | custom-call | tf_op jit(solution)/shard_map/turn_attention/pallas_call | solution.py:280
  99.2 0.0 collective-permute-done.9.other
  99.2 0.0 copy-done.4
  99.2 0.0 copy-done.5
  99.2 9.5 %page_attention.1 = (bf16[256,512]{1,0:T(8,128)(2,1)}, bf16[1024,128]{1,0:T(8,128)(2,1)}) custom-call(s32[8,8]{1,0:T(8,128)S(1)} %copy-done.4, s32[8,8]{1,0:T(8,128)S(1)} %copy-done.5, bf16[4,256,128]{2,1,0:T(8,128)(2,1)S(1)} %get-tuple-element.11.queries, bf16[3072,128]{1,0:T(8,128)(2,1)S(1)} %bitcast.17, ...), custom_call_target="tpu_custom_call" | custom-call | tf_op jit(solution)/shard_map/page_attention/pallas_call | solution.py:323
  (3 shorter events, 0.0 us)
Async XLA Ops:
  0.6 11.9 %copy-start.1 = (bf16[3,128,512]{2,1,0:T(8,128)(2,1)S(1)}, bf16[3,128,512]{2,1,0:T(8,128)(2,1)}, u32[]{:S(2)}) copy-start(bf16[3,128,512]{2,1,0:T(8,128)(2,1)} %param.7) | copy-start | bytes 1179652
  0.6 11.9 %collective-permute-start = (bf16[384,512]{1,0:T(8,128)(2,1)}, bf16[384,512]{1,0:T(8,128)(2,1)}, u32[]{:S(2)}, u32[]{:S(2)}) collective-permute-start(bf16[384,512]{1,0:T(8,128)(2,1)} %bitcast.18), channel_id=1, source_target_pairs={{0,2},{1,3},{2,0},{3,1},{4,6},{5,7},{6,4},{7,5},{8,10},{9,11},{10,... | collective-permute-start | bytes 1179656 | tf_op jit(solution)/shard_map/ppermute | solution.py:20
  2.7 15.2 %collective-permute-start.1 = (bf16[384,512]{1,0:T(8,128)(2,1)}, bf16[384,512]{1,0:T(8,128)(2,1)}, u32[]{:S(2)}, u32[]{:S(2)}) collective-permute-start(bf16[384,512]{1,0:T(8,128)(2,1)} %bitcast.19), channel_id=1, source_target_pairs={{0,4},{1,5},{2,6},{3,7},{4,0},{5,1},{6,2},{7,3},{8,12},{9,13},{10,... | collective-permute-start | bytes 1179656 | tf_op jit(solution)/shard_map/ppermute | solution.py:20
  4.4 30.4 %copy-start = (bf16[8192,128]{1,0:T(8,128)(2,1)S(1)}, bf16[8192,128]{1,0:T(8,128)(2,1)}, u32[]{:S(2)}) copy-start(bf16[8192,128]{1,0:T(8,128)(2,1)} %weight.1) | copy-start | bytes 6291460
  7.1 17.0 %collective-permute-start.3 = (bf16[4,512,128]{2,1,0:T(8,128)(2,1)}, bf16[4,512,128]{2,1,0:T(8,128)(2,1)S(1)}, u32[]{:S(2)}, u32[]{:S(2)}) collective-permute-start(bf16[4,512,128]{2,1,0:T(8,128)(2,1)} %get-tuple-element.22), channel_id=1, source_target_pairs={{0,1},{1,0},{2,3},{3,2},{4,5},{5,4},{6,7},{7,6},{8,9},{9,8},{10,11... | collective-permute-start | bytes 1572872 | tf_op jit(solution)/shard_map/ppermute | solution.py:20
  8.3 15.8 %collective-permute-start.4 = (bf16[4,512,128]{2,1,0:T(8,128)(2,1)}, bf16[4,512,128]{2,1,0:T(8,128)(2,1)S(1)}, u32[]{:S(2)}, u32[]{:S(2)}) collective-permute-start(bf16[4,512,128]{2,1,0:T(8,128)(2,1)} %get-tuple-element.21), channel_id=1, source_target_pairs={{0,12},{1,13},{2,14},{3,15},{4,8},{5,9},{6,10},{7,11},{8,4},{9,5},... | collective-permute-start | bytes 1572872 | tf_op jit(solution)/shard_map/ppermute | solution.py:20
  10.6 24.2 %collective-permute-start.5 = (bf16[4,512,128]{2,1,0:T(8,128)(2,1)}, bf16[4,512,128]{2,1,0:T(8,128)(2,1)}, u32[]{:S(2)}, u32[]{:S(2)}) collective-permute-start(bf16[4,512,128]{2,1,0:T(8,128)(2,1)} %get-tuple-element.20), channel_id=1, source_target_pairs={{0,13},{1,12},{2,15},{3,14},{4,9},{5,8},{6,11},{7,10},{8,5},{9,4},... | collective-permute-start | bytes 1572872 | tf_op jit(solution)/shard_map/ppermute | solution.py:20
  12.5 11.6 %collective-permute-start.2 = (bf16[384,512]{1,0:T(8,128)(2,1)S(1)}, bf16[384,512]{1,0:T(8,128)(2,1)}, u32[]{:S(2)}, u32[]{:S(2)}) collective-permute-start(bf16[384,512]{1,0:T(8,128)(2,1)S(1)} %bitcast.20), channel_id=1, source_target_pairs={{0,6},{1,7},{2,4},{3,5},{4,2},{5,3},{6,0},{7,1},{8,14},{9,15},{10,... | collective-permute-start | bytes 1179656 | tf_op jit(solution)/shard_map/ppermute | solution.py:20
  17.9 22.9 %copy-start.6 = (f32[640,64]{1,0:T(8,128)}, f32[640,64]{1,0:T(8,128)S(1)}, u32[]{:S(2)}) copy-start(f32[640,64]{1,0:T(8,128)S(1)} %get-tuple-element.23) | copy-start | bytes 491524
  17.9 22.9 %copy-start.8 = (f32[640,64]{1,0:T(8,128)}, f32[640,64]{1,0:T(8,128)S(1)}, u32[]{:S(2)}) copy-start(f32[640,64]{1,0:T(8,128)S(1)} %get-tuple-element.24) | copy-start | bytes 491524
  17.9 22.9 %copy-start.10 = (f32[640,64]{1,0:T(8,128)}, f32[640,64]{1,0:T(8,128)S(1)}, u32[]{:S(2)}) copy-start(f32[640,64]{1,0:T(8,128)S(1)} %get-tuple-element.25) | copy-start | bytes 491524
  37.4 3.6 %collective-permute-start.6 = (bf16[384,128]{1,0:T(8,128)(2,1)S(1)}, bf16[384,128]{1,0:T(8,128)(2,1)S(1)}, u32[]{:S(2)}, u32[]{:S(2)}) collective-permute-start(bf16[384,128]{1,0:T(8,128)(2,1)S(1)} %get-tuple-element.13), channel_id=1, source_target_pairs={{0,1},{1,0},{2,3},{3,2},{4,5},{5,4},{6,7},{7,6},{8,9},{9,8},{10,11... | collective-permute-start | bytes 294920 | tf_op jit(solution)/shard_map/ppermute | solution.py:20
  37.8 5.4 %collective-permute-start.7 = (bf16[384,128]{1,0:T(8,128)(2,1)S(1)}, bf16[384,128]{1,0:T(8,128)(2,1)S(1)}, u32[]{:S(2)}, u32[]{:S(2)}) collective-permute-start(bf16[384,128]{1,0:T(8,128)(2,1)S(1)} %get-tuple-element.14), channel_id=1, source_target_pairs={{0,12},{1,13},{2,14},{3,15},{4,8},{5,9},{6,10},{7,11},{8,4},{9,5},... | collective-permute-start | bytes 294920 | tf_op jit(solution)/shard_map/ppermute | solution.py:20
  40.0 6.2 %collective-permute-start.8 = (bf16[384,128]{1,0:T(8,128)(2,1)S(1)}, bf16[384,128]{1,0:T(8,128)(2,1)S(1)}, u32[]{:S(2)}, u32[]{:S(2)}) collective-permute-start(bf16[384,128]{1,0:T(8,128)(2,1)S(1)} %get-tuple-element.15), channel_id=1, source_target_pairs={{0,13},{1,12},{2,15},{3,14},{4,9},{5,8},{6,11},{7,10},{8,5},{9,4},... | collective-permute-start | bytes 294920 | tf_op jit(solution)/shard_map/ppermute | solution.py:20
  41.0 11.4 %copy-start.7 = (f32[640,64]{1,0:T(8,128)S(1)}, f32[640,64]{1,0:T(8,128)}, u32[]{:S(2)}) copy-start(f32[640,64]{1,0:T(8,128)} %copy-done.6) | copy-start | bytes 491524
  41.0 11.4 %copy-start.9 = (f32[640,64]{1,0:T(8,128)S(1)}, f32[640,64]{1,0:T(8,128)}, u32[]{:S(2)}) copy-start(f32[640,64]{1,0:T(8,128)} %copy-done.8) | copy-start | bytes 491524
  41.0 11.4 %copy-start.11 = (f32[640,64]{1,0:T(8,128)S(1)}, f32[640,64]{1,0:T(8,128)}, u32[]{:S(2)}) copy-start(f32[640,64]{1,0:T(8,128)} %copy-done.10) | copy-start | bytes 491524
  46.2 6.3 %copy-start.2 = (bf16[256,512]{1,0:T(8,128)(2,1)S(1)}, bf16[256,512]{1,0:T(8,128)(2,1)}, u32[]{:S(2)}) copy-start(bf16[256,512]{1,0:T(8,128)(2,1)} %queries.1) | copy-start | bytes 786436
  46.2 6.3 %copy-start.3 = (bf16[256,128]{1,0:T(8,128)(2,1)S(1)}, bf16[256,128]{1,0:T(8,128)(2,1)}, u32[]{:S(2)}) copy-start(bf16[256,128]{1,0:T(8,128)(2,1)} %turn_kv.1) | copy-start | bytes 196612
  47.2 15.0 %all-to-all-start = ((bf16[8,384,128]{2,1,0:T(8,128)(2,1)}), bf16[8,384,128]{2,1,0:T(8,128)(2,1)S(1)}, u32[]{:S(2)}, u32[]{:S(2)}) async-start(bf16[8,384,128]{2,1,0:T(8,128)(2,1)} %finish.1), calls=%async_computation | async-start | bytes 1572864 | tf_op jit(solution)/shard_map/all_to_all | solution.py:319
  52.4 46.8 %copy-start.4 = (s32[8,8]{1,0:T(8,128)S(1)}, s32[8,8]{1,0:T(8,128)}, u32[]{:S(2)}) copy-start(s32[8,8]{1,0:T(8,128)} %page_table.1) | copy-start | bytes 772
  52.4 46.8 %copy-start.5 = (s32[8,8]{1,0:T(8,128)S(1)}, s32[8,8]{1,0:T(8,128)}, u32[]{:S(2)}) copy-start(s32[8,8]{1,0:T(8,128)} %page_counts.1) | copy-start | bytes 772
  62.3 13.5 %all-to-all-start.1 = ((bf16[8,256,128]{2,1,0:T(8,128)(2,1)}), bf16[8,256,128]{2,1,0:T(8,128)(2,1)S(1)}, u32[]{:S(2)}, u32[]{:S(2)}) async-start(bf16[8,256,128]{2,1,0:T(8,128)(2,1)} %get-tuple-element.16), calls=%async_computation.1 | async-start | bytes 1048576 | tf_op jit(solution)/shard_map/all_to_all | solution.py:276
  68.8 30.3 %collective-permute-start.9 = (bf16[3072,128]{1,0:T(8,128)(2,1)S(1)}, bf16[3072,128]{1,0:T(8,128)(2,1)S(1)}, u32[]{:S(2)}, u32[]{:S(2)}) collective-permute-start(bf16[3072,128]{1,0:T(8,128)(2,1)S(1)} %bitcast.16), channel_id=1, source_target_pairs={{0,1},{1,0},{2,3},{3,2},{4,5},{5,4},{6,7},{7,6},{8,9},{9,8},{10,11... | collective-permute-start | bytes 2359304 | tf_op jit(solution)/shard_map/ppermute | solution.py:20
  75.8 3.2 %collective-permute-start.10 = (bf16[8,256,128]{2,1,0:T(8,128)(2,1)S(1)}, bf16[8,256,128]{2,1,0:T(8,128)(2,1)S(1)}, u32[]{:S(2)}, u32[]{:S(2)}) collective-permute-start(bf16[8,256,128]{2,1,0:T(8,128)(2,1)S(1)} %all-to-all-done.1.own), channel_id=1, source_target_pairs={{0,1},{1,0},{2,3},{3,2},{4,5},{5,4},{6,7},{7,6},{8,9},{9,8},{10,11... | collective-permute-start | bytes 1572872 | tf_op jit(solution)/shard_map/ppermute | solution.py:20

commit v2 on v1

--- a/solution.py
+++ b/solution.py
@@ -18,6 +18,12 @@
 
 def swapped(value, bits):
     return lax.ppermute(value, "tp", [(i, i ^ bits) for i in range(lax.axis_size("tp"))])
+
+
+def across(value, bits):
+    peers = lax.axis_size("ctx") * lax.axis_size("tp")
+    flip = 4 * lax.axis_size("tp") + 2 + bits
+    return lax.ppermute(value, ("ctx", "tp"), [(i, i ^ flip) for i in range(peers)])
 
 
 def inverse_freq(head_width):
@@ -73,14 +79,13 @@
 
 def project_kernel(x0, x1, x2, x3, weight, w1, w2, w3, own_out, out1, out2, out3, x_buf, w_buf, sems):
     tp = lax.axis_index("tp")
-    core = tp % 2
-    pair = tp // 8
-    spot = (tp // 2) % 4
+    low = tp % 4
+    spot = tp // 4
     depth = x_buf.shape[2]
     copies = []
     for r, x in enumerate((x0, x1, x2, x3)):
         at = spot ^ r
-        row = ((pair * 4 + at) * 2 + core) * depth
+        row = (at * 4 + low) * depth
         group = [pltpu.make_async_copy(x, x_buf.at[r], sems.at[r, 0])]
         group.append(
             pltpu.make_async_copy(
@@ -157,30 +162,27 @@
     heads, rows, _ = queries.shape
     load_pair(own, other, key_buf, value_buf, sems, lambda copy: copy.start())
     load_pair(own, other, key_buf, value_buf, sems, lambda copy: copy.wait())
-    shape = (rows, rows)
-    seen = lax.broadcasted_iota(jnp.int32, shape, 1) <= lax.broadcasted_iota(jnp.int32, shape, 0)
-
-    def keep(head, state):
+    stacked = queries[...].reshape(heads * rows, HEAD_DIM)
+    shape = (heads * rows, rows)
+    token = lax.broadcasted_iota(jnp.int32, shape, 0) % rows
+    seen = lax.broadcasted_iota(jnp.int32, shape, 1) <= token
+
+    def keep(state):
         top, total, acc = state
-        top_out[head] = jnp.broadcast_to(top, (rows, HEAD_DIM))
-        total_out[head] = jnp.broadcast_to(total, (rows, HEAD_DIM))
-        acc_out[head] = acc
-
-    for head in range(heads):
-        scores = jnp.where(seen, scores_of(queries[head], key_buf[ctx]), -huge_value)
-        top = jnp.max(scores, axis=1, keepdims=True)
-        weights = jnp.exp2((scores - top) * SCORE_SCALE)
-        total = jnp.sum(weights, axis=1, keepdims=True)
-        acc = jnp.dot(
-            weights.astype(jnp.bfloat16), value_buf[ctx], preferred_element_type=jnp.float32
-        )
-        keep(head, (top, total, acc))
+        top_out[...] = jnp.broadcast_to(top, top_out.shape)
+        total_out[...] = jnp.broadcast_to(total, total_out.shape)
+        acc_out[...] = acc
+
+    scores = jnp.where(seen, scores_of(stacked, key_buf[ctx]), -huge_value)
+    top = jnp.max(scores, axis=1, keepdims=True)
+    weights = jnp.exp2((scores - top) * SCORE_SCALE)
+    total = jnp.sum(weights, axis=1, keepdims=True)
+    acc = jnp.dot(weights.astype(jnp.bfloat16), value_buf[ctx], preferred_element_type=jnp.float32)
+    keep((top, total, acc))
 
     def source_step(source, carried):
-        for head in range(heads):
-            state = (top_out[head][:, :1], total_out[head][:, :1], acc_out[head])
-            scores = scores_of(queries[head], key_buf[source])
-            keep(head, softmax_step(state, scores, value_buf[source]))
+        state = (top_out[:, :1], total_out[:, :1], acc_out[...])
+        keep(softmax_step(state, scores_of(stacked, key_buf[source]), value_buf[source]))
         return carried
 
     lax.fori_loop(0, ctx, source_step, 0)
@@ -193,7 +195,7 @@
     ctx = lax.axis_index("ctx")
     core = lax.axis_index("tp") % 2
     heads, rows, _ = queries.shape
-    chunk = 1024
+    chunk = 512
     zero_buf[...] = jnp.zeros_like(zero_buf)
     load_pair(own, other, key_buf, value_buf, sems, lambda copy: copy.start())
     load_pair(own, other, key_buf, value_buf, sems, lambda copy: copy.wait())
@@ -219,12 +221,14 @@
         def _():
             cache_copy(slot, zero_buf).start()
 
+    stacked = queries[...].reshape(heads * rows, HEAD_DIM)
+    state = (top_in[:, :1], total_in[:, :1], acc_in[...])
+    for at in range(0, key_buf.shape[0], chunk):
+        scores = scores_of(stacked, key_buf[at : at + chunk])
+        state = softmax_step(state, scores, value_buf[at : at + chunk])
+    result = (state[2] / state[1]).astype(jnp.bfloat16)
     for head in range(heads):
-        state = (top_in[head][:, :1], total_in[head][:, :1], acc_in[head])
-        for at in range(0, key_buf.shape[0], chunk):
-            scores = scores_of(queries[head], key_buf[at : at + chunk])
-            state = softmax_step(state, scores, value_buf[at : at + chunk])
-        out[:, head * HEAD_DIM : (head + 1) * HEAD_DIM] = (state[2] / state[1]).astype(jnp.bfloat16)
+        out[:, head * HEAD_DIM : (head + 1) * HEAD_DIM] = result[head * rows : (head + 1) * rows]
     for slot in range(SOURCES):
         cache_copy(slot, zero_buf).wait()
 
@@ -232,8 +236,6 @@
 def local(stored_pages, kv_weight, page_table, page_counts, queries, turn_kv, turn_pos):
     ctx_index = lax.axis_index("ctx")
     tp_index = lax.axis_index("tp")
-    core = tp_index % 2
-    pair = tp_index // 8
     held, page_rows, width = stored_pages.shape
     rows = held * page_rows
     tok_new = queries.shape[0]
@@ -243,20 +245,18 @@
     params = pltpu.CompilerParams(vmem_limit_bytes=VMEM_BYTES)
 
     own_x = stored_pages.reshape(rows, width)
-    by_group = kv_weight.reshape(2, 4, 2, width, HEAD_DIM)
-
-    def weight_rows(which_pair, which_core):
-        picked = lax.dynamic_slice(
-            by_group, (which_pair, 0, which_core, 0, 0), (1, 4, 1, width, HEAD_DIM)
-        )
+    by_group = kv_weight.reshape(4, 4, width, HEAD_DIM)
+
+    def weight_rows(bits):
+        picked = lax.dynamic_slice_in_dim(by_group, (tp_index % 4) ^ bits, 1, axis=1)
         return picked.reshape(4, width, HEAD_DIM)
 
-    w2 = swapped(weight_rows(1 - pair, core), 12)
-    w3 = swapped(weight_rows(1 - pair, 1 - core), 13)
-    x1 = swapped(own_x, 2)
-    x2 = swapped(own_x, 4)
-    x3 = swapped(own_x, 6)
-    w1 = swapped(weight_rows(pair, 1 - core), 1)
+    w2 = across(weight_rows(2), 0)
+    w3 = across(weight_rows(3), 1)
+    x1 = swapped(own_x, 4)
+    x2 = swapped(own_x, 8)
+    x3 = swapped(own_x, 12)
+    w1 = swapped(weight_rows(1), 1)
 
     local_pos = lax.dynamic_slice_in_dim(turn_pos, ctx_index * tok_new, tok_new)
     page_pos = ctx_index * rows + jnp.arange(rows, dtype=jnp.int32)
@@ -275,8 +275,9 @@
     )(queries, turn_kv, cosine[:tok_new], sine[:tok_new])
     own_turn = lax.all_to_all(turn_block, "ctx", split_axis=0, concat_axis=0)
     other_turn = swapped(own_turn, 1)
-
-    state_shape = jax.ShapeDtypeStruct((heads_dev, tok_new, HEAD_DIM), f32)
+    own_turn, other_turn, own_x = lax.optimization_barrier((own_turn, other_turn, own_x))
+
+    state_shape = jax.ShapeDtypeStruct((heads_dev * tok_new, HEAD_DIM), f32)
     state = pl.pallas_call(
         turn_kernel,
         out_shape=(state_shape,) * 3,
@@ -306,8 +307,8 @@
         name="project",
     )(own_x, x1, x2, x3, kv_weight, w1, w2, w3)
     got1 = swapped(part1, 1)
-    got2 = swapped(part2, 12)
-    got3 = swapped(part3, 13)
+    got2 = swapped(part2, 2)
+    got3 = swapped(part3, 3)
     own_block = pl.pallas_call(
         finish_kernel,
         out_shape=jax.ShapeDtypeStruct((SOURCES, rows, HEAD_DIM), bf16),

time: 109 us -> 116 us (1.064)
  blocking collectives: 0 us -> 27.4 us
  starting transfers between devices: 29.1 us -> 17.2 us
  waiting for transfers between devices: 39.4 us -> 29.2 us
  Pallas kernels: 34.4 us -> 37.9 us
  local copies, waits for them, and re-layouts: 3.55 us -> 1.86 us
    all_to_all x0 -> x2, blocking collectives: none -> 27.4 us  [the longest x1 15.7 us: local(): own_pages = lax.all_to_all(own_block, 'ctx', split_axis=0, concat_axis=0)]
    all_to_all x2 -> x0, waiting for transfers between devices: 14.5 us -> none  [the longest x1 8.67 us: local(): own_pages = lax.all_to_all(own_block, 'ctx', split_axis=0, concat_axis=0)]
    all_to_all x2 -> x0, starting transfers between devices: 11.7 us -> none  [the longest x1 6.57 us: local(): own_turn = lax.all_to_all(turn_block, 'ctx', split_axis=0, concat_axis=0)]
    pallas_call x1, Pallas kernels: 9.5 us -> 14.4 us  [local(): pl.pallas_call(page_kernel, out_shape=(jax.ShapeDtypeStruct((tok_new, hea...]
    ppermute x11 -> x9, waiting for transfers between devices: 24.8 us -> 29.2 us  [swapped(): lax.ppermute(value, 'tp', [(i, i ^ bits) for i in range(lax.axis_size('tp...]
    reshape x1, local copies, waits for them, and re-layouts: 2.73 us -> 0.11 us  [weight_rows(): return picked.reshape(4, width, HEAD_DIM)]
    ppermute x11 -> x9, starting transfers between devices: 17.4 us -> 15.3 us  [swapped(): lax.ppermute(value, 'tp', [(i, i ^ bits) for i in range(lax.axis_size('tp...]
    ppermute x0 -> x2, starting transfers between devices: none -> 1.92 us  [across(): lax.ppermute(value, ('ctx', 'tp'), [(i, i ^ flip) for i in range(peers)])]
  transfers between devices with their start and end apart: 13 -> 11, of which waited for: 8 -> 5; matrix products, arithmetic and copies ran while one was open for 5% -> 0% of each run, Pallas kernels for 19% -> 18%
where the time goes in v2:
time: 116 us
  Pallas kernels  37.9 us (33%)
  waiting for transfers between devices  29.2 us (25%)
  blocking collectives  27.4 us (24%)
  starting transfers between devices  17.2 us (15%)
  local copies, waits for them, and re-layouts  1.86 us (2%)
  other arithmetic  1.56 us (1%)
    ppermute x9, waiting for transfers between devices, swapped(): lax.ppermute(value, 'tp', [(i, i ^ bits) for i in range(lax.axis_size('tp...  29.2 us
    pallas_call x1, Pallas kernels, local(): pl.pallas_call(turn_kernel, out_shape=(state_shape,) * 3, in_specs=[vmem_...  20.9 us
    all_to_all x1, blocking collectives, local(): own_pages = lax.all_to_all(own_block, 'ctx', split_axis=0, concat_axis=0)  15.7 us
    ppermute x9, starting transfers between devices, swapped(): lax.ppermute(value, 'tp', [(i, i ^ bits) for i in range(lax.axis_size('tp...  15.3 us
    pallas_call x1, Pallas kernels, local(): pl.pallas_call(page_kernel, out_shape=(jax.ShapeDtypeStruct((tok_new, hea...  14.4 us
    all_to_all x1, blocking collectives, local(): own_turn = lax.all_to_all(turn_block, 'ctx', split_axis=0, concat_axis=0)  11.7 us
    pallas_call x1, Pallas kernels, local(): pl.pallas_call(project_kernel, out_shape=(jax.ShapeDtypeStruct((rows, HEA...  2.34 us
  transfers between devices with their start and end apart: 11, of which 5 were waited for; matrix products, arithmetic and copies ran while one was open for 0% of the time, Pallas kernels for 18%

profile of v2, /device:TPU:15, one launch (start us, length us, event | category | flops | bytes accessed | tf_op | source)
XLA Modules:
  0.0 116.1 jit_solution(11249042469794247442)
XLA Ops:
  0.6 0.0 copy-start.2
  0.6 0.0 copy-start.1
  0.7 0.0 copy-start
  0.7 0.9 dynamic_slice.12
  1.6 1.2 %fusion = (f32[640,64]{1,0:T(8,128)S(1)}, f32[640,64]{1,0:T(8,128)S(1)}, f32[640,64]{1,0:T(8,128)S(1)}) fusion(f32[64]{0:T(128)S(1)} %compare_select_fusion.1, f32[640]{0:T(1024)S(1)} %add_convert_fusion), kind=kLoop, calls=%fused_computation.9 | loop fusion | flops 81920 | bytes 494336 | tf_op jit(solution)/shard_map/neg | solution.py:47
  2.9 0.0 copy-start.5
  2.9 0.0 copy-start.7
  2.9 0.0 copy-start.9
  2.9 0.1 pad_maximum_fusion.2
  3.0 0.6 copy-done.5
  3.6 0.1 copy-done.7
  3.7 0.1 copy-done.9
  3.8 0.0 copy-done.2
  3.8 0.0 copy-done.1
  3.8 0.2 prepare.1
  4.1 11.7 %all_to_all.10.own = bf16[8,256,128]{2,1,0:T(8,128)(2,1)S(1)} all-to-all(bf16[8,256,128]{2,1,0:T(8,128)(2,1)S(1)} %get-tuple-element.15), channel_id=1, replica_groups=mesh['ctx'=8,'tp'=16] {'ctx'}, dimensions={0} | all-to-all | bytes 1048576 | tf_op jit(solution)/shard_map/all_to_all | solution.py:276
  15.7 1.9 %collective-permute-start = (bf16[8,256,128]{2,1,0:T(8,128)(2,1)S(1)}, bf16[8,256,128]{2,1,0:T(8,128)(2,1)S(1)}, u32[]{:S(2)}, u32[]{:S(2)}) collective-permute-start(bf16[8,256,128]{2,1,0:T(8,128)(2,1)S(1)} %all_to_all.10.own), channel_id=1, source_target_pairs={{0,1},{1,0},{2,3},{3,2},{4,5},{5,4},{6,7},{7,6},{8,9},{9,8},{10,11... | collective-permute-start | bytes 1572872 | tf_op jit(solution)/shard_map/ppermute | solution.py:20
  17.6 3.8 %collective-permute-start.3 = (bf16[384,512]{1,0:T(8,128)(2,1)}, bf16[384,512]{1,0:T(8,128)(2,1)}, u32[]{:S(2)}, u32[]{:S(2)}) collective-permute-start(bf16[384,512]{1,0:T(8,128)(2,1)} %bitcast.x0), channel_id=1, source_target_pairs={{0,12},{1,13},{2,14},{3,15},{4,8},{5,9},{6,10},{7,11},{8,4},{9,5},... | collective-permute-start | bytes 1179656 | tf_op jit(solution)/shard_map/ppermute | solution.py:20
  21.4 0.0 copy-done
  21.4 0.1 dynamic-slice_bitcast_fusion
  21.5 1.9 %collective-permute-start.6 = (bf16[4,512,128]{2,1,0:T(8,128)(2,1)S(1)}, bf16[4,512,128]{2,1,0:T(8,128)(2,1)S(1)}, u32[]{:S(2)}, u32[]{:S(2)}) collective-permute-start(bf16[4,512,128]{2,1,0:T(8,128)(2,1)S(1)} %get-tuple-element.26), channel_id=1, source_target_pairs={{0,67},{1,66},{2,65},{3,64},{4,71},{5,70},{6,69},{7,68},{8,75},{9,... | collective-permute-start | bytes 1572872 | tf_op jit(solution)/shard_map/ppermute | solution.py:26
  23.4 0.0 collective-permute-start.5
  23.4 0.0 copy-start.6
  23.4 0.0 copy-start.8
  23.4 0.0 copy-start.10
  23.4 0.5 collective-permute-start.4
  23.9 7.3 %collective-permute-done.3.x3 = bf16[384,512]{1,0:T(8,128)(2,1)} collective-permute-done((bf16[384,512]{1,0:T(8,128)(2,1)}, bf16[384,512]{1,0:T(8,128)(2,1)}, u32[]{:S(2)}, u32[]{:S(2)}) %collective-permute-start.3) | collective-permute-done | bytes 393248 | tf_op jit(solution)/shard_map/ppermute | solution.py:20
  31.2 1.1 collective-permute-start.2
  32.3 0.0 collective-permute-done.other
  32.3 1.9 %collective-permute-start.1 = (bf16[384,512]{1,0:T(8,128)(2,1)}, bf16[384,512]{1,0:T(8,128)(2,1)S(1)}, u32[]{:S(2)}, u32[]{:S(2)}) collective-permute-start(bf16[384,512]{1,0:T(8,128)(2,1)} %bitcast.x0), channel_id=1, source_target_pairs={{0,4},{1,5},{2,6},{3,7},{4,0},{5,1},{6,2},{7,3},{8,12},{9,13},{10,... | collective-permute-start | bytes 1179656 | tf_op jit(solution)/shard_map/ppermute | solution.py:20
  34.2 8.7 %collective-permute-done.2.x2 = bf16[384,512]{1,0:T(8,128)(2,1)S(1)} collective-permute-done((bf16[384,512]{1,0:T(8,128)(2,1)}, bf16[384,512]{1,0:T(8,128)(2,1)S(1)}, u32[]{:S(2)}, u32[]{:S(2)}) %collective-permute-start.2) | collective-permute-done | bytes 393248 | tf_op jit(solution)/shard_map/ppermute | solution.py:20
  43.0 8.3 %collective-permute-done.1.x1 = bf16[384,512]{1,0:T(8,128)(2,1)S(1)} collective-permute-done((bf16[384,512]{1,0:T(8,128)(2,1)}, bf16[384,512]{1,0:T(8,128)(2,1)S(1)}, u32[]{:S(2)}, u32[]{:S(2)}) %collective-permute-start.1) | collective-permute-done | bytes 393248 | tf_op jit(solution)/shard_map/ppermute | solution.py:20
  51.2 0.0 collective-permute-done.6.w3
  51.3 0.0 collective-permute-done.5.w2
  51.3 0.0 collective-permute-done.4.w1
  51.3 2.3 %project.1 = (f32[384,128]{1,0:T(8,128)S(1)}, bf16[384,128]{1,0:T(8,128)(2,1)S(1)}, bf16[384,128]{1,0:T(8,128)(2,1)S(1)}, bf16[384,128]{1,0:T(8,128)(2,1)S(1)}) custom-call(bf16[384,512]{1,0:T(8,128)(2,1)} %bitcast.x0, bf16[384,512]{1,0:T(8,128)(2,1)S(1)} %collective-permute-done.1.x1, bf16[384,512]{1,0:T(8,128)(2,1)S(1)} %collective-permute-done.2.x2, ...), custom_call_target="tpu_custom_call" | custom-call | tf_op jit(solution)/shard_map/project/pallas_call | solution.py:296
  53.6 1.8 %collective-permute-start.7 = (bf16[384,128]{1,0:T(8,128)(2,1)S(1)}, bf16[384,128]{1,0:T(8,128)(2,1)S(1)}, u32[]{:S(2)}, u32[]{:S(2)}) collective-permute-start(bf16[384,128]{1,0:T(8,128)(2,1)S(1)} %get-tuple-element.18), channel_id=1, source_target_pairs={{0,1},{1,0},{2,3},{3,2},{4,5},{5,4},{6,7},{7,6},{8,9},{9,8},{10,11... | collective-permute-start | bytes 294920 | tf_op jit(solution)/shard_map/ppermute | solution.py:20
  55.4 2.0 %collective-permute-start.8 = (bf16[384,128]{1,0:T(8,128)(2,1)S(1)}, bf16[384,128]{1,0:T(8,128)(2,1)S(1)}, u32[]{:S(2)}, u32[]{:S(2)}) collective-permute-start(bf16[384,128]{1,0:T(8,128)(2,1)S(1)} %get-tuple-element.19), channel_id=1, source_target_pairs={{0,2},{1,3},{2,0},{3,1},{4,6},{5,7},{6,4},{7,5},{8,10},{9,11},{10,... | collective-permute-start | bytes 294920 | tf_op jit(solution)/shard_map/ppermute | solution.py:20
  57.4 1.2 %collective-permute-start.9 = (bf16[384,128]{1,0:T(8,128)(2,1)S(1)}, bf16[384,128]{1,0:T(8,128)(2,1)S(1)}, u32[]{:S(2)}, u32[]{:S(2)}) collective-permute-start(bf16[384,128]{1,0:T(8,128)(2,1)S(1)} %get-tuple-element.20), channel_id=1, source_target_pairs={{0,3},{1,2},{2,1},{3,0},{4,7},{5,6},{6,5},{7,4},{8,11},{9,10},{10,... | collective-permute-start | bytes 294920 | tf_op jit(solution)/shard_map/ppermute | solution.py:20
  58.6 0.0 copy-done.6
  58.6 0.0 copy-done.8
  58.6 0.0 copy-done.10
  58.6 0.2 pad_maximum_fusion
  58.8 0.0 collective-permute-done.7.p1
  58.8 2.4 %collective-permute-done.8.p2 = bf16[384,128]{1,0:T(8,128)(2,1)S(1)} collective-permute-done((bf16[384,128]{1,0:T(8,128)(2,1)S(1)}, bf16[384,128]{1,0:T(8,128)(2,1)S(1)}, u32[]{:S(2)}, u32[]{:S(2)}) %collective-permute-start.8) | collective-permute-done | bytes 98336 | tf_op jit(solution)/shard_map/ppermute | solution.py:20
  61.2 2.4 %collective-permute-done.9.p3 = bf16[384,128]{1,0:T(8,128)(2,1)S(1)} collective-permute-done((bf16[384,128]{1,0:T(8,128)(2,1)S(1)}, bf16[384,128]{1,0:T(8,128)(2,1)S(1)}, u32[]{:S(2)}, u32[]{:S(2)}) %collective-permute-start.9) | collective-permute-done | bytes 98336 | tf_op jit(solution)/shard_map/ppermute | solution.py:20
  63.7 0.0 copy-start.3
  63.7 0.0 copy-start.4
  63.7 0.1 finish.1
  63.8 15.7 %all_to_all.11 = bf16[8,384,128]{2,1,0:T(8,128)(2,1)S(1)} all-to-all(bf16[8,384,128]{2,1,0:T(8,128)(2,1)S(1)} %finish.1), channel_id=1, replica_groups=mesh['ctx'=8,'tp'=16] {'ctx'}, dimensions={0} | all-to-all | bytes 1572864 | tf_op jit(solution)/shard_map/all_to_all | solution.py:320
  79.5 1.2 %collective-permute-start.10 = (bf16[3072,128]{1,0:T(8,128)(2,1)S(1)}, bf16[3072,128]{1,0:T(8,128)(2,1)S(1)}, u32[]{:S(2)}, u32[]{:S(2)}) collective-permute-start(bf16[3072,128]{1,0:T(8,128)(2,1)S(1)} %bitcast.16), channel_id=1, source_target_pairs={{0,1},{1,0},{2,3},{3,2},{4,5},{5,4},{6,7},{7,6},{8,9},{9,8},{10,11... | collective-permute-start | bytes 2359304 | tf_op jit(solution)/shard_map/ppermute | solution.py:20
  80.7 20.9 %turn_attention.1 = (f32[1024,128]{1,0:T(8,128)S(1)}, f32[1024,128]{1,0:T(8,128)S(1)}, f32[1024,128]{1,0:T(8,128)S(1)}) custom-call(bf16[4,256,128]{2,1,0:T(8,128)(2,1)S(1)} %get-tuple-element.14.queries, bf16[8,256,128]{2,1,0:T(8,128)(2,1)S(1)} %all_to_all.10.own, bf16[8,256,128]{2,1,0:T(8,128)(2,1)S(1)} %collective-permute-done.other), custom_call_target="tpu_custom_call" | custom-call | tf_op jit(solution)/shard_map/turn_attention/pallas_call | solution.py:281
  101.6 0.0 collective-permute-done.10.other
  101.6 0.0 copy-done.3
  101.6 0.0 copy-done.4
  101.6 14.4 %page_attention.1 = (bf16[256,512]{1,0:T(8,128)(2,1)}, bf16[1024,128]{1,0:T(8,128)(2,1)}) custom-call(s32[8,8]{1,0:T(8,128)S(1)} %copy-done.3, s32[8,8]{1,0:T(8,128)S(1)} %copy-done.4, bf16[4,256,128]{2,1,0:T(8,128)(2,1)S(1)} %get-tuple-element.14.queries, bf16[3072,128]{1,0:T(8,128)(2,1)S(1)} %bitcast.17, ...), custom_call_target="tpu_custom_call" | custom-call | tf_op jit(solution)/shard_map/page_attention/pallas_call | solution.py:324
  (3 shorter events, 0.0 us)
Async XLA Ops:
  0.6 3.2 %copy-start.2 = (bf16[256,128]{1,0:T(8,128)(2,1)S(1)}, bf16[256,128]{1,0:T(8,128)(2,1)}, u32[]{:S(2)}) copy-start(bf16[256,128]{1,0:T(8,128)(2,1)} %turn_kv.1) | copy-start | bytes 196612
  0.6 3.2 %copy-start.1 = (bf16[256,512]{1,0:T(8,128)(2,1)S(1)}, bf16[256,512]{1,0:T(8,128)(2,1)}, u32[]{:S(2)}) copy-start(bf16[256,512]{1,0:T(8,128)(2,1)} %queries.1) | copy-start | bytes 786436
  0.7 20.7 %copy-start = (bf16[8192,128]{1,0:T(8,128)(2,1)S(1)}, bf16[8192,128]{1,0:T(8,128)(2,1)}, u32[]{:S(2)}) copy-start(bf16[8192,128]{1,0:T(8,128)(2,1)} %weight.1) | copy-start | bytes 6291460
  2.9 0.8 copy-start.5
  2.9 0.9 copy-start.7
  2.9 1.0 copy-start.9
  15.7 16.5 %collective-permute-start = (bf16[8,256,128]{2,1,0:T(8,128)(2,1)S(1)}, bf16[8,256,128]{2,1,0:T(8,128)(2,1)S(1)}, u32[]{:S(2)}, u32[]{:S(2)}) collective-permute-start(bf16[8,256,128]{2,1,0:T(8,128)(2,1)S(1)} %all_to_all.10.own), channel_id=1, source_target_pairs={{0,1},{1,0},{2,3},{3,2},{4,5},{5,4},{6,7},{7,6},{8,9},{9,8},{10,11... | collective-permute-start | bytes 1572872 | tf_op jit(solution)/shard_map/ppermute | solution.py:20
  17.6 13.6 %collective-permute-start.3 = (bf16[384,512]{1,0:T(8,128)(2,1)}, bf16[384,512]{1,0:T(8,128)(2,1)}, u32[]{:S(2)}, u32[]{:S(2)}) collective-permute-start(bf16[384,512]{1,0:T(8,128)(2,1)} %bitcast.x0), channel_id=1, source_target_pairs={{0,12},{1,13},{2,14},{3,15},{4,8},{5,9},{6,10},{7,11},{8,4},{9,5},... | collective-permute-start | bytes 1179656 | tf_op jit(solution)/shard_map/ppermute | solution.py:20
  21.5 29.8 %collective-permute-start.6 = (bf16[4,512,128]{2,1,0:T(8,128)(2,1)S(1)}, bf16[4,512,128]{2,1,0:T(8,128)(2,1)S(1)}, u32[]{:S(2)}, u32[]{:S(2)}) collective-permute-start(bf16[4,512,128]{2,1,0:T(8,128)(2,1)S(1)} %get-tuple-element.26), channel_id=1, source_target_pairs={{0,67},{1,66},{2,65},{3,64},{4,71},{5,70},{6,69},{7,68},{8,75},{9,... | collective-permute-start | bytes 1572872 | tf_op jit(solution)/shard_map/ppermute | solution.py:26
  23.4 27.9 %collective-permute-start.5 = (bf16[4,512,128]{2,1,0:T(8,128)(2,1)S(1)}, bf16[4,512,128]{2,1,0:T(8,128)(2,1)S(1)}, u32[]{:S(2)}, u32[]{:S(2)}) collective-permute-start(bf16[4,512,128]{2,1,0:T(8,128)(2,1)S(1)} %get-tuple-element.27), channel_id=1, source_target_pairs={{0,66},{1,67},{2,64},{3,65},{4,70},{5,71},{6,68},{7,69},{8,74},{9,... | collective-permute-start | bytes 1572872 | tf_op jit(solution)/shard_map/ppermute | solution.py:26
  23.4 35.2 %copy-start.6 = (f32[640,64]{1,0:T(8,128)S(1)}, f32[640,64]{1,0:T(8,128)}, u32[]{:S(2)}) copy-start(f32[640,64]{1,0:T(8,128)} %copy-done.5) | copy-start | bytes 491524
  23.4 35.2 %copy-start.8 = (f32[640,64]{1,0:T(8,128)S(1)}, f32[640,64]{1,0:T(8,128)}, u32[]{:S(2)}) copy-start(f32[640,64]{1,0:T(8,128)} %copy-done.7) | copy-start | bytes 491524
  23.4 35.2 %copy-start.10 = (f32[640,64]{1,0:T(8,128)S(1)}, f32[640,64]{1,0:T(8,128)}, u32[]{:S(2)}) copy-start(f32[640,64]{1,0:T(8,128)} %copy-done.9) | copy-start | bytes 491524
  23.4 27.8 %collective-permute-start.4 = (bf16[4,512,128]{2,1,0:T(8,128)(2,1)S(1)}, bf16[4,512,128]{2,1,0:T(8,128)(2,1)S(1)}, u32[]{:S(2)}, u32[]{:S(2)}) collective-permute-start(bf16[4,512,128]{2,1,0:T(8,128)(2,1)S(1)} %get-tuple-element.28), channel_id=1, source_target_pairs={{0,1},{1,0},{2,3},{3,2},{4,5},{5,4},{6,7},{7,6},{8,9},{9,8},{10,11... | collective-permute-start | bytes 1572872 | tf_op jit(solution)/shard_map/ppermute | solution.py:20
  31.2 11.8 %collective-permute-start.2 = (bf16[384,512]{1,0:T(8,128)(2,1)}, bf16[384,512]{1,0:T(8,128)(2,1)S(1)}, u32[]{:S(2)}, u32[]{:S(2)}) collective-permute-start(bf16[384,512]{1,0:T(8,128)(2,1)} %bitcast.x0), channel_id=1, source_target_pairs={{0,8},{1,9},{2,10},{3,11},{4,12},{5,13},{6,14},{7,15},{8,0},{9,1},... | collective-permute-start | bytes 1179656 | tf_op jit(solution)/shard_map/ppermute | solution.py:20
  32.3 19.0 %collective-permute-start.1 = (bf16[384,512]{1,0:T(8,128)(2,1)}, bf16[384,512]{1,0:T(8,128)(2,1)S(1)}, u32[]{:S(2)}, u32[]{:S(2)}) collective-permute-start(bf16[384,512]{1,0:T(8,128)(2,1)} %bitcast.x0), channel_id=1, source_target_pairs={{0,4},{1,5},{2,6},{3,7},{4,0},{5,1},{6,2},{7,3},{8,12},{9,13},{10,... | collective-permute-start | bytes 1179656 | tf_op jit(solution)/shard_map/ppermute | solution.py:20
  53.6 5.2 %collective-permute-start.7 = (bf16[384,128]{1,0:T(8,128)(2,1)S(1)}, bf16[384,128]{1,0:T(8,128)(2,1)S(1)}, u32[]{:S(2)}, u32[]{:S(2)}) collective-permute-start(bf16[384,128]{1,0:T(8,128)(2,1)S(1)} %get-tuple-element.18), channel_id=1, source_target_pairs={{0,1},{1,0},{2,3},{3,2},{4,5},{5,4},{6,7},{7,6},{8,9},{9,8},{10,11... | collective-permute-start | bytes 294920 | tf_op jit(solution)/shard_map/ppermute | solution.py:20
  55.4 5.9 %collective-permute-start.8 = (bf16[384,128]{1,0:T(8,128)(2,1)S(1)}, bf16[384,128]{1,0:T(8,128)(2,1)S(1)}, u32[]{:S(2)}, u32[]{:S(2)}) collective-permute-start(bf16[384,128]{1,0:T(8,128)(2,1)S(1)} %get-tuple-element.19), channel_id=1, source_target_pairs={{0,2},{1,3},{2,0},{3,1},{4,6},{5,7},{6,4},{7,5},{8,10},{9,11},{10,... | collective-permute-start | bytes 294920 | tf_op jit(solution)/shard_map/ppermute | solution.py:20
  57.4 6.3 %collective-permute-start.9 = (bf16[384,128]{1,0:T(8,128)(2,1)S(1)}, bf16[384,128]{1,0:T(8,128)(2,1)S(1)}, u32[]{:S(2)}, u32[]{:S(2)}) collective-permute-start(bf16[384,128]{1,0:T(8,128)(2,1)S(1)} %get-tuple-element.20), channel_id=1, source_target_pairs={{0,3},{1,2},{2,1},{3,0},{4,7},{5,6},{6,5},{7,4},{8,11},{9,10},{10,... | collective-permute-start | bytes 294920 | tf_op jit(solution)/shard_map/ppermute | solution.py:20
  63.7 37.9 %copy-start.3 = (s32[8,8]{1,0:T(8,128)S(1)}, s32[8,8]{1,0:T(8,128)}, u32[]{:S(2)}) copy-start(s32[8,8]{1,0:T(8,128)} %page_table.1) | copy-start | bytes 772
  63.7 37.9 %copy-start.4 = (s32[8,8]{1,0:T(8,128)S(1)}, s32[8,8]{1,0:T(8,128)}, u32[]{:S(2)}) copy-start(s32[8,8]{1,0:T(8,128)} %page_counts.1) | copy-start | bytes 772
  79.5 22.1 %collective-permute-start.10 = (bf16[3072,128]{1,0:T(8,128)(2,1)S(1)}, bf16[3072,128]{1,0:T(8,128)(2,1)S(1)}, u32[]{:S(2)}, u32[]{:S(2)}) collective-permute-start(bf16[3072,128]{1,0:T(8,128)(2,1)S(1)} %bitcast.16), channel_id=1, source_target_pairs={{0,1},{1,0},{2,3},{3,2},{4,5},{5,4},{6,7},{7,6},{8,9},{9,8},{10,11... | collective-permute-start | bytes 2359304 | tf_op jit(solution)/shard_map/ppermute | solution.py:20

commit v3 on v2

--- a/solution.py
+++ b/solution.py
@@ -73,8 +73,7 @@
         query_out[head] = turned(block, c, s).astype(jnp.bfloat16)
     block = turn_kv[...].astype(jnp.float32)
     block = turned(block, jnp.where(is_key, c, 1.0), jnp.where(is_key, s, 0.0)).astype(jnp.bfloat16)
-    for peer in range(SOURCES):
-        turn_out[peer] = block
+    turn_out[...] = block
 
 
 def project_kernel(x0, x1, x2, x3, weight, w1, w2, w3, own_out, out1, out2, out3, x_buf, w_buf, sems):
@@ -131,12 +130,19 @@
     )
 
 
+def widened(value, width):
+    return value if width == HEAD_DIM else jnp.concatenate([value] * (width // HEAD_DIM), axis=1)
+
+
 def softmax_step(state, scores, values):
     top, total, acc = state
+    width = scores.shape[1]
     new_top = jnp.maximum(top, jnp.max(scores, axis=1, keepdims=True))
     decay = jnp.exp2((top - new_top) * SCORE_SCALE)
-    weights = jnp.exp2((scores - new_top) * SCORE_SCALE)
-    total = total * decay + jnp.sum(weights, axis=1, keepdims=True)
+    weights = jnp.exp2((scores - widened(new_top, width)) * SCORE_SCALE)
+    total = total * decay
+    for at in range(0, width, HEAD_DIM):
+        total = total + weights[:, at : at + HEAD_DIM]
     acc = acc * decay + jnp.dot(
         weights.astype(jnp.bfloat16), values, preferred_element_type=jnp.float32
     )
@@ -157,32 +163,26 @@
         act(pltpu.make_async_copy(own, value_buf, sems.at[1]))
 
 
-def turn_kernel(queries, own, other, top_out, total_out, acc_out, key_buf, value_buf, sems):
+def turn_kernel(queries, pairs, top_out, total_out, acc_out):
     ctx = lax.axis_index("ctx")
+    core = lax.axis_index("tp") % 2
     heads, rows, _ = queries.shape
-    load_pair(own, other, key_buf, value_buf, sems, lambda copy: copy.start())
-    load_pair(own, other, key_buf, value_buf, sems, lambda copy: copy.wait())
     stacked = queries[...].reshape(heads * rows, HEAD_DIM)
     shape = (heads * rows, rows)
     token = lax.broadcasted_iota(jnp.int32, shape, 0) % rows
     seen = lax.broadcasted_iota(jnp.int32, shape, 1) <= token
 
     def keep(state):
-        top, total, acc = state
-        top_out[...] = jnp.broadcast_to(top, top_out.shape)
-        total_out[...] = jnp.broadcast_to(total, total_out.shape)
-        acc_out[...] = acc
-
-    scores = jnp.where(seen, scores_of(stacked, key_buf[ctx]), -huge_value)
-    top = jnp.max(scores, axis=1, keepdims=True)
-    weights = jnp.exp2((scores - top) * SCORE_SCALE)
-    total = jnp.sum(weights, axis=1, keepdims=True)
-    acc = jnp.dot(weights.astype(jnp.bfloat16), value_buf[ctx], preferred_element_type=jnp.float32)
-    keep((top, total, acc))
+        top_out[...], total_out[...], acc_out[...] = state
+
+    none = jnp.zeros(top_out.shape, jnp.float32)
+    scores = jnp.where(seen, scores_of(stacked, pairs[ctx, core]), -huge_value)
+    keep(softmax_step((none - huge_value, none, none), scores, pairs[ctx, 1 - core]))
 
     def source_step(source, carried):
-        state = (top_out[:, :1], total_out[:, :1], acc_out[...])
-        keep(softmax_step(state, scores_of(stacked, key_buf[source]), value_buf[source]))
+        state = (top_out[...], total_out[...], acc_out[...])
+        scores = scores_of(stacked, pairs[source, core])
+        keep(softmax_step(state, scores, pairs[source, 1 - core]))
         return carried
 
     lax.fori_loop(0, ctx, source_step, 0)
@@ -222,11 +222,11 @@
             cache_copy(slot, zero_buf).start()
 
     stacked = queries[...].reshape(heads * rows, HEAD_DIM)
-    state = (top_in[:, :1], total_in[:, :1], acc_in[...])
+    state = (top_in[...], total_in[...], acc_in[...])
     for at in range(0, key_buf.shape[0], chunk):
         scores = scores_of(stacked, key_buf[at : at + chunk])
         state = softmax_step(state, scores, value_buf[at : at + chunk])
-    result = (state[2] / state[1]).astype(jnp.bfloat16)
+    result = (state[2] / jnp.sum(state[1], axis=1, keepdims=True)).astype(jnp.bfloat16)
     for head in range(heads):
         out[:, head * HEAD_DIM : (head + 1) * HEAD_DIM] = result[head * rows : (head + 1) * rows]
     for slot in range(SOURCES):
@@ -266,31 +266,15 @@
         prepare_kernel,
         out_shape=(
             jax.ShapeDtypeStruct((heads_dev, tok_new, HEAD_DIM), bf16),
-            jax.ShapeDtypeStruct((SOURCES, tok_new, HEAD_DIM), bf16),
+            jax.ShapeDtypeStruct((tok_new, HEAD_DIM), bf16),
         ),
         in_specs=[vmem_spec()] * 4,
         out_specs=(vmem_spec(), vmem_spec()),
         compiler_params=params,
         name="prepare",
     )(queries, turn_kv, cosine[:tok_new], sine[:tok_new])
-    own_turn = lax.all_to_all(turn_block, "ctx", split_axis=0, concat_axis=0)
-    other_turn = swapped(own_turn, 1)
-    own_turn, other_turn, own_x = lax.optimization_barrier((own_turn, other_turn, own_x))
-
-    state_shape = jax.ShapeDtypeStruct((heads_dev * tok_new, HEAD_DIM), f32)
-    state = pl.pallas_call(
-        turn_kernel,
-        out_shape=(state_shape,) * 3,
-        in_specs=[vmem_spec(), any_spec(), any_spec()],
-        out_specs=(vmem_spec(),) * 3,
-        scratch_shapes=[
-            pltpu.VMEM((SOURCES, tok_new, HEAD_DIM), bf16),
-            pltpu.VMEM((SOURCES, tok_new, HEAD_DIM), bf16),
-            pltpu.SemaphoreType.DMA((2,)),
-        ],
-        compiler_params=params,
-        name="turn_attention",
-    )(query_heads, own_turn, other_turn)
+    pair = jnp.stack([turn_block, swapped(turn_block, 1)])
+    turn_pairs = lax.all_gather(pair, "ctx", axis=0)
 
     part_shape = jax.ShapeDtypeStruct((rows, HEAD_DIM), bf16)
     own_part, part1, part2, part3 = pl.pallas_call(
@@ -317,7 +301,23 @@
         compiler_params=params,
         name="finish",
     )(own_part, got1, got2, got3, cosine[tok_new:], sine[tok_new:])
+    own_block, turn_pairs = lax.optimization_barrier((own_block, turn_pairs))
     own_pages = lax.all_to_all(own_block, "ctx", split_axis=0, concat_axis=0)
+    state_shape = jax.ShapeDtypeStruct((heads_dev * tok_new, HEAD_DIM), f32)
+    state = pl.pallas_call(
+        turn_kernel,
+        out_shape=(state_shape,) * 3,
+        in_specs=[vmem_spec()] * 2,
+        out_specs=(vmem_spec(),) * 3,
+        compiler_params=params,
+        cost_estimate=pl.CostEstimate(
+            flops=8 * heads_dev * tok_new * tok_new * SOURCES * HEAD_DIM,
+            bytes_accessed=6 * 1024 * 1024,
+            transcendentals=heads_dev * tok_new * tok_new * SOURCES,
+        ),
+        name="turn_attention",
+    )(query_heads, turn_pairs)
+    own_pages, state = lax.optimization_barrier((own_pages, state))
     own_pages = own_pages.reshape(SOURCES * rows, HEAD_DIM)
     other_pages = swapped(own_pages, 1)
 

time: 116 us -> 91.7 us (0.79)
  the two profiles are of different devices: /device:TPU:15 before, /device:TPU:1 now
where the time goes in v3:
time: 91.7 us; the launch traced here: 91.5 us
  waiting for transfers between devices  39.3 us (43%)
  starting transfers between devices  22.3 us (24%)
  between operations  14.2 us (15%)
  Pallas kernels  10.6 us (12%)
  local copies, waits for them, and re-layouts  2.96 us (3%)
  other arithmetic  2.23 us (2%)
    ppermute x9, waiting for transfers between devices, swapped(): lax.ppermute(value, 'tp', [(i, i ^ bits) for i in range(lax.axis_size('tp...  28.1 us
    ppermute x9, starting transfers between devices, swapped(): lax.ppermute(value, 'tp', [(i, i ^ bits) for i in range(lax.axis_size('tp...  15.2 us
    all_to_all x1, waiting for transfers between devices, local(): own_pages = lax.all_to_all(own_block, 'ctx', split_axis=0, concat_axis=0)  11.1 us
    pallas_call x1, Pallas kernels, local(): pl.pallas_call(page_kernel, out_shape=(jax.ShapeDtypeStruct((tok_new, hea...  6.24 us
    all_to_all x1, starting transfers between devices, local(): own_pages = lax.all_to_all(own_block, 'ctx', split_axis=0, concat_axis=0)  4.06 us
    ppermute x2, starting transfers between devices, across(): lax.ppermute(value, ('ctx', 'tp'), [(i, i ^ flip) for i in range(peers)])  2.93 us
    pallas_call x1, Pallas kernels, local(): pl.pallas_call(project_kernel, out_shape=(jax.ShapeDtypeStruct((rows, HEA...  2.49 us
    unnamed x22, local copies, waits for them, and re-layouts  1.93 us
  transfers between devices with their start and end apart: 13, of which 8 were waited for; matrix products, arithmetic and copies ran while one was open for 0% of the time, Pallas kernels for 5%

profile of v3, /device:TPU:1, one launch (start us, length us, event | category | flops | bytes accessed | tf_op | source)
XLA Modules:
  0.0 91.5 jit_solution(9693832183172612549)
XLA Ops:
  7.2 0.0 copy-start.2
  7.2 0.0 copy-start.3
  7.2 0.0 copy-start.1
  7.2 0.0 copy-start
  7.2 0.0 all-gather.3.cloned.1.call-start
  7.3 0.9 %dynamic_slice.12 = s32[256]{0:T(256)S(1)} dynamic-slice(s32[2048]{0:T(1024)} %param.13, s32[]{:T(128)S(6)} %select_n.38), dynamic_slice_sizes={256} | dynamic-slice | bytes 2052 | tf_op jit(solution)/shard_map/dynamic_slice | solution.py:261
  8.2 1.2 %fusion = (f32[640,64]{1,0:T(8,128)S(1)}, f32[640,64]{1,0:T(8,128)S(1)}, f32[640,64]{1,0:T(8,128)S(1)}) fusion(f32[64]{0:T(128)S(1)} %compare_select_fusion.1, f32[640]{0:T(1024)S(1)} %add_convert_fusion), kind=kLoop, calls=%fused_computation.10 | loop fusion | flops 81920 | bytes 494336 | tf_op jit(solution)/shard_map/neg | solution.py:47
  9.4 0.0 copy-start.7
  9.5 0.0 copy-start.9
  9.5 0.1 pad_maximum_fusion.2
  9.6 0.6 copy-done.7
  10.2 0.1 copy-done.9
  10.3 0.0 copy-done.2
  10.3 0.0 copy-done.3
  10.3 0.2 prepare.1
  10.5 1.5 %collective-permute-start.9 = (bf16[256,128]{1,0:T(8,128)(2,1)S(1)}, bf16[256,128]{1,0:T(8,128)(2,1)S(1)}, u32[]{:S(2)}, u32[]{:S(2)}) collective-permute-start(bf16[256,128]{1,0:T(8,128)(2,1)S(1)} %get-tuple-element.22), channel_id=1, source_target_pairs={{0,1},{1,0},{2,3},{3,2},{4,5},{5,4},{6,7},{7,6},{8,9},{9,8},{10,11... | collective-permute-start | bytes 196616 | tf_op jit(solution)/shard_map/ppermute | solution.py:20
  12.0 0.9 collective-permute-done.9
  12.9 0.7 pad_maximum_fusion.4
  13.6 0.0 all-gather.3.cloned.1.call-update
  13.6 0.0 copy-done.1
  13.6 1.8 %collective-permute-start = (bf16[384,512]{1,0:T(8,128)(2,1)S(1)}, bf16[384,512]{1,0:T(8,128)(2,1)S(1)}, u32[]{:S(2)}, u32[]{:S(2)}) collective-permute-start(bf16[384,512]{1,0:T(8,128)(2,1)S(1)} %bitcast.21), channel_id=1, source_target_pairs={{0,4},{1,5},{2,6},{3,7},{4,0},{5,1},{6,2},{7,3},{8,12},{9,13},{10,... | collective-permute-start | bytes 1179656 | tf_op jit(solution)/shard_map/ppermute | solution.py:20
  15.4 0.0 copy-done
  15.4 0.1 dynamic-slice_bitcast_fusion
  15.5 0.7 collective-permute-start.3
  16.2 2.7 %collective-permute-start.4 = (bf16[4,512,128]{2,1,0:T(8,128)(2,1)S(1)}, bf16[4,512,128]{2,1,0:T(8,128)(2,1)S(1)}, u32[]{:S(2)}, u32[]{:S(2)}) collective-permute-start(bf16[4,512,128]{2,1,0:T(8,128)(2,1)S(1)} %get-tuple-element.33), channel_id=1, source_target_pairs={{0,66},{1,67},{2,64},{3,65},{4,70},{5,71},{6,68},{7,69},{8,74},{9,... | collective-permute-start | bytes 1572872 | tf_op jit(solution)/shard_map/ppermute | solution.py:26
  19.0 0.0 copy-start.8
  19.0 0.0 copy-start.10
  19.0 0.2 collective-permute-start.5
  19.2 3.3 %collective-permute-start.1 = (bf16[384,512]{1,0:T(8,128)(2,1)S(1)}, bf16[384,512]{1,0:T(8,128)(2,1)S(1)}, u32[]{:S(2)}, u32[]{:S(2)}) collective-permute-start(bf16[384,512]{1,0:T(8,128)(2,1)S(1)} %bitcast.22), channel_id=1, source_target_pairs={{0,8},{1,9},{2,10},{3,11},{4,12},{5,13},{6,14},{7,15},{8,0},{9,1},... | collective-permute-start | bytes 1179656 | tf_op jit(solution)/shard_map/ppermute | solution.py:20
  22.5 2.1 %collective-permute-done.x1 = bf16[384,512]{1,0:T(8,128)(2,1)S(1)} collective-permute-done((bf16[384,512]{1,0:T(8,128)(2,1)S(1)}, bf16[384,512]{1,0:T(8,128)(2,1)S(1)}, u32[]{:S(2)}, u32[]{:S(2)}) %collective-permute-start) | collective-permute-done | bytes 393248 | tf_op jit(solution)/shard_map/ppermute | solution.py:20
  24.6 3.3 %collective-permute-start.2 = (bf16[384,512]{1,0:T(8,128)(2,1)S(1)}, bf16[384,512]{1,0:T(8,128)(2,1)S(1)}, u32[]{:S(2)}, u32[]{:S(2)}) collective-permute-start(bf16[384,512]{1,0:T(8,128)(2,1)S(1)} %bitcast.23), channel_id=1, source_target_pairs={{0,12},{1,13},{2,14},{3,15},{4,8},{5,9},{6,10},{7,11},{8,4},{9,5},... | collective-permute-start | bytes 1179656 | tf_op jit(solution)/shard_map/ppermute | solution.py:20
  27.9 8.2 %collective-permute-done.1.x2 = bf16[384,512]{1,0:T(8,128)(2,1)S(1)} collective-permute-done((bf16[384,512]{1,0:T(8,128)(2,1)S(1)}, bf16[384,512]{1,0:T(8,128)(2,1)S(1)}, u32[]{:S(2)}, u32[]{:S(2)}) %collective-permute-start.1) | collective-permute-done | bytes 393248 | tf_op jit(solution)/shard_map/ppermute | solution.py:20
  36.1 9.0 %collective-permute-done.2.x3 = bf16[384,512]{1,0:T(8,128)(2,1)S(1)} collective-permute-done((bf16[384,512]{1,0:T(8,128)(2,1)S(1)}, bf16[384,512]{1,0:T(8,128)(2,1)S(1)}, u32[]{:S(2)}, u32[]{:S(2)}) %collective-permute-start.2) | collective-permute-done | bytes 393248 | tf_op jit(solution)/shard_map/ppermute | solution.py:20
  45.1 0.0 collective-permute-done.3.w1
  45.1 0.0 collective-permute-done.4.w2
  45.1 0.0 collective-permute-done.5.w3
  45.1 2.5 %project.1 = (f32[384,128]{1,0:T(8,128)S(1)}, bf16[384,128]{1,0:T(8,128)(2,1)S(1)}, bf16[384,128]{1,0:T(8,128)(2,1)S(1)}, bf16[384,128]{1,0:T(8,128)(2,1)S(1)}) custom-call(bf16[384,512]{1,0:T(8,128)(2,1)S(1)} %bitcast.24, bf16[384,512]{1,0:T(8,128)(2,1)S(1)} %collective-permute-done.x1, bf16[384,512]{1,0:T(8,128)(2,1)S(1)} %collective-permute-done.1.x2, ...), custom_call_target="tpu_custom_call" | custom-call | tf_op jit(solution)/shard_map/project/pallas_call | solution.py:280
  47.6 0.6 collective-permute-start.6
  48.2 2.9 %collective-permute-start.7 = (bf16[384,128]{1,0:T(8,128)(2,1)S(1)}, bf16[384,128]{1,0:T(8,128)(2,1)S(1)}, u32[]{:S(2)}, u32[]{:S(2)}) collective-permute-start(bf16[384,128]{1,0:T(8,128)(2,1)S(1)} %get-tuple-element.20), channel_id=1, source_target_pairs={{0,2},{1,3},{2,0},{3,1},{4,6},{5,7},{6,4},{7,5},{8,10},{9,11},{10,... | collective-permute-start | bytes 294920 | tf_op jit(solution)/shard_map/ppermute | solution.py:20
  51.1 0.3 collective-permute-start.8
  51.4 0.0 copy-done.8
  51.4 0.0 copy-done.10
  51.4 0.2 pad_maximum_fusion
  51.6 0.0 collective-permute-done.6.p1
  51.6 2.8 %collective-permute-done.7.p2 = bf16[384,128]{1,0:T(8,128)(2,1)S(1)} collective-permute-done((bf16[384,128]{1,0:T(8,128)(2,1)S(1)}, bf16[384,128]{1,0:T(8,128)(2,1)S(1)}, u32[]{:S(2)}, u32[]{:S(2)}) %collective-permute-start.7) | collective-permute-done | bytes 98336 | tf_op jit(solution)/shard_map/ppermute | solution.py:20
  54.4 3.2 %collective-permute-done.8.p3 = bf16[384,128]{1,0:T(8,128)(2,1)S(1)} collective-permute-done((bf16[384,128]{1,0:T(8,128)(2,1)S(1)}, bf16[384,128]{1,0:T(8,128)(2,1)S(1)}, u32[]{:S(2)}, u32[]{:S(2)}) %collective-permute-start.8) | collective-permute-done | bytes 98336 | tf_op jit(solution)/shard_map/ppermute | solution.py:20
  57.6 1.0 %finish.1 = bf16[8,384,128]{2,1,0:T(8,128)(2,1)} custom-call(f32[384,128]{1,0:T(8,128)S(1)} %get-tuple-element.18.own, bf16[384,128]{1,0:T(8,128)(2,1)S(1)} %collective-permute-done.6.p1, bf16[384,128]{1,0:T(8,128)(2,1)S(1)} %collective-permute-done.7.p2, bf16[384,128]{1,0:T(8,128)(2,1)S(1)} %collective-permute-done.8.p3, ...), custom_call_target="tpu_custom_call" | custom-call | tf_op jit(solution)/shard_map/finish/pallas_call | solution.py:296
  58.6 0.0 all-gather.3.cloned.1.call-done
  58.6 4.1 %all-to-all-start = ((bf16[8,384,128]{2,1,0:T(8,128)(2,1)}), bf16[8,384,128]{2,1,0:T(8,128)(2,1)S(1)}, u32[]{:S(2)}, u32[]{:S(2)}) async-start(bf16[8,384,128]{2,1,0:T(8,128)(2,1)} %finish.1), calls=%async_computation | async-start | bytes 1572864 | tf_op jit(solution)/shard_map/all_to_all | solution.py:305
  62.6 0.0 copy-start.6
  62.6 1.2 %copy-done.6 = bf16[16,256,128]{2,1,0:T(8,128)(2,1)S(1)} copy-done((bf16[16,256,128]{2,1,0:T(8,128)(2,1)S(1)}, bf16[16,256,128]{2,1,0:T(8,128)(2,1)}, u32[]{:S(2)}) %copy-start.6) | copy-done | bytes 1048600
  63.9 0.0 copy-start.4
  63.9 0.0 copy-start.5
  63.9 0.7 turn_attention.1
  64.5 11.1 %all-to-all-done = bf16[8,384,128]{2,1,0:T(8,128)(2,1)S(1)} async-done(((bf16[8,384,128]{2,1,0:T(8,128)(2,1)}), bf16[8,384,128]{2,1,0:T(8,128)(2,1)S(1)}, u32[]{:S(2)}, u32[]{:S(2)}) %all-to-all-start) | async-done | bytes 786464 | tf_op jit(solution)/shard_map/all_to_all | solution.py:305
  75.7 0.8 collective-permute-start.10
  76.5 1.9 %collective-permute-done.10.other = bf16[3072,128]{1,0:T(8,128)(2,1)S(1)} collective-permute-done((bf16[3072,128]{1,0:T(8,128)(2,1)S(1)}, bf16[3072,128]{1,0:T(8,128)(2,1)S(1)}, u32[]{:S(2)}, u32[]{:S(2)}) %collective-permute-start.10) | collective-permute-done | bytes 786464 | tf_op jit(solution)/shard_map/ppermute | solution.py:20
  78.4 0.0 copy-done.4
  78.4 0.0 copy-done.5
  78.4 6.2 %page_attention.1 = (bf16[256,512]{1,0:T(8,128)(2,1)}, bf16[1024,128]{1,0:T(8,128)(2,1)}) custom-call(s32[8,8]{1,0:T(8,128)S(1)} %copy-done.4, s32[8,8]{1,0:T(8,128)S(1)} %copy-done.5, bf16[4,256,128]{2,1,0:T(8,128)(2,1)S(1)} %get-tuple-element.17.queries, bf16[3072,128]{1,0:T(8,128)(2,1)S(1)} %bitcast.20, ...), custom_call_target="tpu_custom_call" | custom-call | tf_op jit(solution)/shard_map/page_attention/pallas_call | solution.py:324
  (3 shorter events, 0.0 us)
Async XLA Ops:
  7.2 3.1 %copy-start.2 = (bf16[256,512]{1,0:T(8,128)(2,1)S(1)}, bf16[256,512]{1,0:T(8,128)(2,1)}, u32[]{:S(2)}) copy-start(bf16[256,512]{1,0:T(8,128)(2,1)} %queries.1) | copy-start | bytes 786436
  7.2 3.1 %copy-start.3 = (bf16[256,128]{1,0:T(8,128)(2,1)S(1)}, bf16[256,128]{1,0:T(8,128)(2,1)}, u32[]{:S(2)}) copy-start(bf16[256,128]{1,0:T(8,128)(2,1)} %turn_kv.1) | copy-start | bytes 196612
  7.2 6.4 %copy-start.1 = (bf16[3,128,512]{2,1,0:T(8,128)(2,1)S(1)}, bf16[3,128,512]{2,1,0:T(8,128)(2,1)}, u32[]{:S(2)}) copy-start(bf16[3,128,512]{2,1,0:T(8,128)(2,1)} %param.7) | copy-start | bytes 1179652
  7.2 8.2 %copy-start = (bf16[8192,128]{1,0:T(8,128)(2,1)S(1)}, bf16[8192,128]{1,0:T(8,128)(2,1)}, u32[]{:S(2)}) copy-start(bf16[8192,128]{1,0:T(8,128)(2,1)} %weight.1) | copy-start | bytes 6291460
  7.2 51.4 %all-gather.3.cloned.1.call-start = ((), (), s32[]{:S(2)}) async-start(), calls=%async_computation.1 | async-start | bytes 1179648 | tf_op jit(solution)/shard_map/all_gather | solution.py:277
  9.4 0.7 copy-start.7
  9.5 0.8 copy-start.9
  10.5 2.4 %collective-permute-start.9 = (bf16[256,128]{1,0:T(8,128)(2,1)S(1)}, bf16[256,128]{1,0:T(8,128)(2,1)S(1)}, u32[]{:S(2)}, u32[]{:S(2)}) collective-permute-start(bf16[256,128]{1,0:T(8,128)(2,1)S(1)} %get-tuple-element.22), channel_id=1, source_target_pairs={{0,1},{1,0},{2,3},{3,2},{4,5},{5,4},{6,7},{7,6},{8,9},{9,8},{10,11... | collective-permute-start | bytes 196616 | tf_op jit(solution)/shard_map/ppermute | solution.py:20
  13.6 11.0 %collective-permute-start = (bf16[384,512]{1,0:T(8,128)(2,1)S(1)}, bf16[384,512]{1,0:T(8,128)(2,1)S(1)}, u32[]{:S(2)}, u32[]{:S(2)}) collective-permute-start(bf16[384,512]{1,0:T(8,128)(2,1)S(1)} %bitcast.21), channel_id=1, source_target_pairs={{0,4},{1,5},{2,6},{3,7},{4,0},{5,1},{6,2},{7,3},{8,12},{9,13},{10,... | collective-permute-start | bytes 1179656 | tf_op jit(solution)/shard_map/ppermute | solution.py:20
  15.5 29.6 %collective-permute-start.3 = (bf16[4,512,128]{2,1,0:T(8,128)(2,1)S(1)}, bf16[4,512,128]{2,1,0:T(8,128)(2,1)S(1)}, u32[]{:S(2)}, u32[]{:S(2)}) collective-permute-start(bf16[4,512,128]{2,1,0:T(8,128)(2,1)S(1)} %get-tuple-element.34), channel_id=1, source_target_pairs={{0,1},{1,0},{2,3},{3,2},{4,5},{5,4},{6,7},{7,6},{8,9},{9,8},{10,11... | collective-permute-start | bytes 1572872 | tf_op jit(solution)/shard_map/ppermute | solution.py:20
  16.2 28.9 %collective-permute-start.4 = (bf16[4,512,128]{2,1,0:T(8,128)(2,1)S(1)}, bf16[4,512,128]{2,1,0:T(8,128)(2,1)S(1)}, u32[]{:S(2)}, u32[]{:S(2)}) collective-permute-start(bf16[4,512,128]{2,1,0:T(8,128)(2,1)S(1)} %get-tuple-element.33), channel_id=1, source_target_pairs={{0,66},{1,67},{2,64},{3,65},{4,70},{5,71},{6,68},{7,69},{8,74},{9,... | collective-permute-start | bytes 1572872 | tf_op jit(solution)/shard_map/ppermute | solution.py:26
  19.0 32.4 %copy-start.8 = (f32[640,64]{1,0:T(8,128)S(1)}, f32[640,64]{1,0:T(8,128)}, u32[]{:S(2)}) copy-start(f32[640,64]{1,0:T(8,128)} %copy-done.7) | copy-start | bytes 491524
  19.0 32.4 %copy-start.10 = (f32[640,64]{1,0:T(8,128)S(1)}, f32[640,64]{1,0:T(8,128)}, u32[]{:S(2)}) copy-start(f32[640,64]{1,0:T(8,128)} %copy-done.9) | copy-start | bytes 491524
  19.0 26.1 %collective-permute-start.5 = (bf16[4,512,128]{2,1,0:T(8,128)(2,1)S(1)}, bf16[4,512,128]{2,1,0:T(8,128)(2,1)S(1)}, u32[]{:S(2)}, u32[]{:S(2)}) collective-permute-start(bf16[4,512,128]{2,1,0:T(8,128)(2,1)S(1)} %get-tuple-element.32), channel_id=1, source_target_pairs={{0,67},{1,66},{2,65},{3,64},{4,71},{5,70},{6,69},{7,68},{8,75},{9,... | collective-permute-start | bytes 1572872 | tf_op jit(solution)/shard_map/ppermute | solution.py:26
  19.2 16.9 %collective-permute-start.1 = (bf16[384,512]{1,0:T(8,128)(2,1)S(1)}, bf16[384,512]{1,0:T(8,128)(2,1)S(1)}, u32[]{:S(2)}, u32[]{:S(2)}) collective-permute-start(bf16[384,512]{1,0:T(8,128)(2,1)S(1)} %bitcast.22), channel_id=1, source_target_pairs={{0,8},{1,9},{2,10},{3,11},{4,12},{5,13},{6,14},{7,15},{8,0},{9,1},... | collective-permute-start | bytes 1179656 | tf_op jit(solution)/shard_map/ppermute | solution.py:20
  24.6 20.5 %collective-permute-start.2 = (bf16[384,512]{1,0:T(8,128)(2,1)S(1)}, bf16[384,512]{1,0:T(8,128)(2,1)S(1)}, u32[]{:S(2)}, u32[]{:S(2)}) collective-permute-start(bf16[384,512]{1,0:T(8,128)(2,1)S(1)} %bitcast.23), channel_id=1, source_target_pairs={{0,12},{1,13},{2,14},{3,15},{4,8},{5,9},{6,10},{7,11},{8,4},{9,5},... | collective-permute-start | bytes 1179656 | tf_op jit(solution)/shard_map/ppermute | solution.py:20
  47.6 4.0 %collective-permute-start.6 = (bf16[384,128]{1,0:T(8,128)(2,1)S(1)}, bf16[384,128]{1,0:T(8,128)(2,1)S(1)}, u32[]{:S(2)}, u32[]{:S(2)}) collective-permute-start(bf16[384,128]{1,0:T(8,128)(2,1)S(1)} %get-tuple-element.19), channel_id=1, source_target_pairs={{0,1},{1,0},{2,3},{3,2},{4,5},{5,4},{6,7},{7,6},{8,9},{9,8},{10,11... | collective-permute-start | bytes 294920 | tf_op jit(solution)/shard_map/ppermute | solution.py:20
  48.2 6.2 %collective-permute-start.7 = (bf16[384,128]{1,0:T(8,128)(2,1)S(1)}, bf16[384,128]{1,0:T(8,128)(2,1)S(1)}, u32[]{:S(2)}, u32[]{:S(2)}) collective-permute-start(bf16[384,128]{1,0:T(8,128)(2,1)S(1)} %get-tuple-element.20), channel_id=1, source_target_pairs={{0,2},{1,3},{2,0},{3,1},{4,6},{5,7},{6,4},{7,5},{8,10},{9,11},{10,... | collective-permute-start | bytes 294920 | tf_op jit(solution)/shard_map/ppermute | solution.py:20
  51.1 6.4 %collective-permute-start.8 = (bf16[384,128]{1,0:T(8,128)(2,1)S(1)}, bf16[384,128]{1,0:T(8,128)(2,1)S(1)}, u32[]{:S(2)}, u32[]{:S(2)}) collective-permute-start(bf16[384,128]{1,0:T(8,128)(2,1)S(1)} %get-tuple-element.21), channel_id=1, source_target_pairs={{0,3},{1,2},{2,1},{3,0},{4,7},{5,6},{6,5},{7,4},{8,11},{9,10},{10,... | collective-permute-start | bytes 294920 | tf_op jit(solution)/shard_map/ppermute | solution.py:20
  58.6 17.1 %all-to-all-start = ((bf16[8,384,128]{2,1,0:T(8,128)(2,1)}), bf16[8,384,128]{2,1,0:T(8,128)(2,1)S(1)}, u32[]{:S(2)}, u32[]{:S(2)}) async-start(bf16[8,384,128]{2,1,0:T(8,128)(2,1)} %finish.1), calls=%async_computation | async-start | bytes 1572864 | tf_op jit(solution)/shard_map/all_to_all | solution.py:305
  62.6 1.2 %copy-start.6 = (bf16[16,256,128]{2,1,0:T(8,128)(2,1)S(1)}, bf16[16,256,128]{2,1,0:T(8,128)(2,1)}, u32[]{:S(2)}) copy-start(bf16[16,256,128]{2,1,0:T(8,128)(2,1)} %all-gather.3.cloned.1.call-done) | copy-start | bytes 3145732
  63.9 14.5 %copy-start.4 = (s32[8,8]{1,0:T(8,128)S(1)}, s32[8,8]{1,0:T(8,128)}, u32[]{:S(2)}) copy-start(s32[8,8]{1,0:T(8,128)} %page_table.1) | copy-start | bytes 772
  63.9 14.5 %copy-start.5 = (s32[8,8]{1,0:T(8,128)S(1)}, s32[8,8]{1,0:T(8,128)}, u32[]{:S(2)}) copy-start(s32[8,8]{1,0:T(8,128)} %page_counts.1) | copy-start | bytes 772
  75.7 2.7 %collective-permute-start.10 = (bf16[3072,128]{1,0:T(8,128)(2,1)S(1)}, bf16[3072,128]{1,0:T(8,128)(2,1)S(1)}, u32[]{:S(2)}, u32[]{:S(2)}) collective-permute-start(bf16[3072,128]{1,0:T(8,128)(2,1)S(1)} %bitcast.19), channel_id=1, source_target_pairs={{0,1},{1,0},{2,3},{3,2},{4,5},{5,4},{6,7},{7,6},{8,9},{9,8},{10,11... | collective-permute-start | bytes 2359304 | tf_op jit(solution)/shard_map/ppermute | solution.py:20
Sparse Core Ops, SparseCore 0:
  13.7 36.2 all-gather.2

commit v4 on v3

--- a/solution.py
+++ b/solution.py
@@ -20,9 +20,9 @@
     return lax.ppermute(value, "tp", [(i, i ^ bits) for i in range(lax.axis_size("tp"))])
 
 
-def across(value, bits):
+def across(value):
     peers = lax.axis_size("ctx") * lax.axis_size("tp")
-    flip = 4 * lax.axis_size("tp") + 2 + bits
+    flip = 4 * lax.axis_size("tp") + 2
     return lax.ppermute(value, ("ctx", "tp"), [(i, i ^ flip) for i in range(peers)])
 
 
@@ -73,50 +73,59 @@
         query_out[head] = turned(block, c, s).astype(jnp.bfloat16)
     block = turn_kv[...].astype(jnp.float32)
     block = turned(block, jnp.where(is_key, c, 1.0), jnp.where(is_key, s, 0.0)).astype(jnp.bfloat16)
-    turn_out[...] = block
-
-
-def project_kernel(x0, x1, x2, x3, weight, w1, w2, w3, own_out, out1, out2, out3, x_buf, w_buf, sems):
+    for peer in range(SOURCES):
+        turn_out[peer] = block
+
+
+def project_kernel(*refs):
+    slices, (weight, far_weight, own_out, far_out, x_buf, w_buf, sems) = refs[:10], refs[10:]
     tp = lax.axis_index("tp")
     low = tp % 4
     spot = tp // 4
-    depth = x_buf.shape[2]
+    depth = slices[0].shape[1]
+    rows = x_buf.shape[1]
     copies = []
-    for r, x in enumerate((x0, x1, x2, x3)):
+    for i, r in enumerate((0, 1, 3, 2)):
         at = spot ^ r
-        row = (at * 4 + low) * depth
-        group = [pltpu.make_async_copy(x, x_buf.at[r], sems.at[r, 0])]
-        group.append(
-            pltpu.make_async_copy(
-                weight.at[pl.ds(pl.multiple_of(row, depth), depth)],
-                w_buf.at[r, :, pl.ds(0, HEAD_DIM)],
-                sems.at[r, 1],
-            )
-        )
-        for b, w in enumerate((w1, w2, w3)):
-            group.append(
+        for half in range(2):
+            part = pl.ds(half * depth, depth)
+            core = (low % 2) ^ half
+            near_row = pl.multiple_of((at * 4 + (low ^ half)) * depth, depth)
+            far_row = pl.multiple_of(core * depth, depth)
+            group = [
                 pltpu.make_async_copy(
-                    w.at[at], w_buf.at[r, :, pl.ds((b + 1) * HEAD_DIM, HEAD_DIM)], sems.at[r, b + 2]
-                )
-            )
-        for copy in group:
-            copy.start()
-        copies.append(group)
+                    weight.at[pl.ds(near_row, depth)],
+                    w_buf.at[r, part, pl.ds(0, HEAD_DIM)],
+                    sems.at[r, half, 0],
+                ),
+                pltpu.make_async_copy(
+                    far_weight.at[at, pl.ds(far_row, depth)],
+                    w_buf.at[r, part, pl.ds(HEAD_DIM, HEAD_DIM)],
+                    sems.at[r, half, 1],
+                ),
+            ]
+            sent = [(slices[2 * i + half], 0, rows)]
+            if r == 2:
+                sent = [(slices[6 + half], 0, rows // 2), (slices[8 + half], rows // 2, rows // 2)]
+            for k, (piece, first, count) in enumerate(sent):
+                place = x_buf.at[r, pl.ds(first, count), part]
+                group.append(pltpu.make_async_copy(piece, place, sems.at[r, half, 2 + k]))
+            for copy in group:
+                copy.start()
+            copies.append(group)
     total = None
-    for r in range(4):
-        for copy in copies[r]:
+    for i, r in enumerate((0, 1, 3, 2)):
+        for copy in copies[2 * i] + copies[2 * i + 1]:
             copy.wait()
         part = jnp.dot(x_buf[r], w_buf[r], preferred_element_type=jnp.float32)
         total = part if total is None else total + part
     own_out[...] = total[:, :HEAD_DIM]
-    for b, out in enumerate((out1, out2, out3)):
-        out[...] = total[:, (b + 1) * HEAD_DIM : (b + 2) * HEAD_DIM].astype(jnp.bfloat16)
-
-
-def finish_kernel(own, p1, p2, p3, cosine, sine, out):
+    far_out[...] = total[:, HEAD_DIM:].astype(jnp.bfloat16)
+
+
+def finish_kernel(own, far, cosine, sine, out):
     is_key = lax.axis_index("tp") % 2 == 0
-    value = own[...] + p1[...].astype(jnp.float32)
-    value = value + (p2[...].astype(jnp.float32) + p3[...].astype(jnp.float32))
+    value = own[...] + far[...].astype(jnp.float32)
     c = jnp.where(is_key, cosine[...], 1.0)
     s = jnp.where(is_key, sine[...], 0.0)
     block = turned(value, c, s).astype(jnp.bfloat16)
@@ -163,7 +172,7 @@
         act(pltpu.make_async_copy(own, value_buf, sems.at[1]))
 
 
-def turn_kernel(queries, pairs, top_out, total_out, acc_out):
+def turn_kernel(queries, own, other, top_out, total_out, acc_out):
     ctx = lax.axis_index("ctx")
     core = lax.axis_index("tp") % 2
     heads, rows, _ = queries.shape
@@ -176,16 +185,20 @@
         top_out[...], total_out[...], acc_out[...] = state
 
     none = jnp.zeros(top_out.shape, jnp.float32)
-    scores = jnp.where(seen, scores_of(stacked, pairs[ctx, core]), -huge_value)
-    keep(softmax_step((none - huge_value, none, none), scores, pairs[ctx, 1 - core]))
-
-    def source_step(source, carried):
-        state = (top_out[...], total_out[...], acc_out[...])
-        scores = scores_of(stacked, pairs[source, core])
-        keep(softmax_step(state, scores, pairs[source, 1 - core]))
-        return carried
-
-    lax.fori_loop(0, ctx, source_step, 0)
+
+    def attend(keys, values):
+        scores = jnp.where(seen, scores_of(stacked, keys[ctx]), -huge_value)
+        keep(softmax_step((none - huge_value, none, none), scores, values[ctx]))
+
+        def source_step(source, carried):
+            state = (top_out[...], total_out[...], acc_out[...])
+            keep(softmax_step(state, scores_of(stacked, keys[source]), values[source]))
+            return carried
+
+        lax.fori_loop(0, ctx, source_step, 0)
+
+    pl.when(core == 0)(lambda: attend(own, other))
+    pl.when(core == 1)(lambda: attend(other, own))
 
 
 def page_kernel(
@@ -245,18 +258,17 @@
     params = pltpu.CompilerParams(vmem_limit_bytes=VMEM_BYTES)
 
     own_x = stored_pages.reshape(rows, width)
-    by_group = kv_weight.reshape(4, 4, width, HEAD_DIM)
-
-    def weight_rows(bits):
-        picked = lax.dynamic_slice_in_dim(by_group, (tp_index % 4) ^ bits, 1, axis=1)
-        return picked.reshape(4, width, HEAD_DIM)
-
-    w2 = across(weight_rows(2), 0)
-    w3 = across(weight_rows(3), 1)
+    by_half = kv_weight.reshape(4, 2, 2 * width, HEAD_DIM)
+    half = (tp_index // 2) % 2
+    far_rows = lax.dynamic_slice_in_dim(by_half, 1 - half, 1, axis=1)
+    far_weight = across(far_rows.reshape(4, 2 * width, HEAD_DIM))
     x1 = swapped(own_x, 4)
-    x2 = swapped(own_x, 8)
     x3 = swapped(own_x, 12)
-    w1 = swapped(weight_rows(1), 1)
+    x2a = swapped(x1[: rows // 2], 12)
+    x2b = swapped(x3[rows // 2 :], 4)
+    pieces = []
+    for piece in (own_x, x1, x3, x2a, x2b):
+        pieces += [piece, swapped(piece, 1)]
 
     local_pos = lax.dynamic_slice_in_dim(turn_pos, ctx_index * tok_new, tok_new)
     page_pos = ctx_index * rows + jnp.arange(rows, dtype=jnp.int32)
@@ -266,48 +278,49 @@
         prepare_kernel,
         out_shape=(
             jax.ShapeDtypeStruct((heads_dev, tok_new, HEAD_DIM), bf16),
-            jax.ShapeDtypeStruct((tok_new, HEAD_DIM), bf16),
+            jax.ShapeDtypeStruct((SOURCES, tok_new, HEAD_DIM), bf16),
         ),
         in_specs=[vmem_spec()] * 4,
         out_specs=(vmem_spec(), vmem_spec()),
         compiler_params=params,
         name="prepare",
     )(queries, turn_kv, cosine[:tok_new], sine[:tok_new])
-    pair = jnp.stack([turn_block, swapped(turn_block, 1)])
-    turn_pairs = lax.all_gather(pair, "ctx", axis=0)
-
-    part_shape = jax.ShapeDtypeStruct((rows, HEAD_DIM), bf16)
-    own_part, part1, part2, part3 = pl.pallas_call(
+    turn_block, pieces[2], pieces[4] = lax.optimization_barrier((turn_block, pieces[2], pieces[4]))
+    own_turn = lax.all_to_all(turn_block, "ctx", split_axis=0, concat_axis=0)
+    other_turn = swapped(own_turn, 1)
+
+    own_part, far_part = pl.pallas_call(
         project_kernel,
-        out_shape=(jax.ShapeDtypeStruct((rows, HEAD_DIM), f32),) + (part_shape,) * 3,
-        in_specs=[any_spec()] * 8,
-        out_specs=(vmem_spec(),) * 4,
+        out_shape=(
+            jax.ShapeDtypeStruct((rows, HEAD_DIM), f32),
+            jax.ShapeDtypeStruct((rows, HEAD_DIM), bf16),
+        ),
+        in_specs=[any_spec()] * 12,
+        out_specs=(vmem_spec(),) * 2,
         scratch_shapes=[
-            pltpu.VMEM((4, rows, width), bf16),
-            pltpu.VMEM((4, width, 4 * HEAD_DIM), bf16),
-            pltpu.SemaphoreType.DMA((4, 5)),
+            pltpu.VMEM((4, rows, 2 * width), bf16),
+            pltpu.VMEM((4, 2 * width, 2 * HEAD_DIM), bf16),
+            pltpu.SemaphoreType.DMA((4, 2, 4)),
         ],
         compiler_params=params,
         name="project",
-    )(own_x, x1, x2, x3, kv_weight, w1, w2, w3)
-    got1 = swapped(part1, 1)
-    got2 = swapped(part2, 2)
-    got3 = swapped(part3, 3)
+    )(*pieces, kv_weight, far_weight)
+    arrived = swapped(far_part, 2)
     own_block = pl.pallas_call(
         finish_kernel,
         out_shape=jax.ShapeDtypeStruct((SOURCES, rows, HEAD_DIM), bf16),
-        in_specs=[vmem_spec()] * 6,
+        in_specs=[vmem_spec()] * 4,
         out_specs=vmem_spec(),
         compiler_params=params,
         name="finish",
-    )(own_part, got1, got2, got3, cosine[tok_new:], sine[tok_new:])
-    own_block, turn_pairs = lax.optimization_barrier((own_block, turn_pairs))
+    )(own_part, arrived, cosine[tok_new:], sine[tok_new:])
+    own_block, own_turn, other_turn = lax.optimization_barrier((own_block, own_turn, other_turn))
     own_pages = lax.all_to_all(own_block, "ctx", split_axis=0, concat_axis=0)
     state_shape = jax.ShapeDtypeStruct((heads_dev * tok_new, HEAD_DIM), f32)
     state = pl.pallas_call(
         turn_kernel,
         out_shape=(state_shape,) * 3,
-        in_specs=[vmem_spec()] * 2,
+        in_specs=[vmem_spec()] * 3,
         out_specs=(vmem_spec(),) * 3,
         compiler_params=params,
         cost_estimate=pl.CostEstimate(
@@ -316,7 +329,7 @@
             transcendentals=heads_dev * tok_new * tok_new * SOURCES,
         ),
         name="turn_attention",
-    )(query_heads, turn_pairs)
+    )(query_heads, own_turn, other_turn)
     own_pages, state = lax.optimization_barrier((own_pages, state))
     own_pages = own_pages.reshape(SOURCES * rows, HEAD_DIM)
     other_pages = swapped(own_pages, 1)

time: 91.7 us -> 75.7 us (0.83)
  waiting for transfers between devices: 39.3 us -> 22 us
  between operations: 14.2 us -> 0.95 us
  local copies, waits for them, and re-layouts: 2.96 us -> 12.3 us
  starting transfers between devices: 22.3 us -> 25.6 us
  Pallas kernels: 10.6 us -> 12.8 us
    ppermute x9 -> x12, waiting for transfers between devices: 28.1 us -> 7.23 us  [swapped(): lax.ppermute(value, 'tp', [(i, i ^ bits) for i in range(lax.axis_size('tp...]
    unnamed x22 -> x34, local copies, waits for them, and re-layouts: 1.93 us -> 6.97 us
    all_to_all x0 -> x1, waiting for transfers between devices: none -> 4.6 us  [local(): own_turn = lax.all_to_all(turn_block, 'ctx', split_axis=0, concat_axis=0)]
    all_to_all x0 -> x1, starting transfers between devices: none -> 4.14 us  [local(): own_turn = lax.all_to_all(turn_block, 'ctx', split_axis=0, concat_axis=0)]
    slice x0 -> x2, local copies, waits for them, and re-layouts: none -> 2.31 us  [the longest x1 1.62 us: local(): x2b = swapped(x3[rows // 2:], 4)]
    reshape x1, local copies, waits for them, and re-layouts: 0.11 us -> 2.27 us  [local(): far_weight = across(far_rows.reshape(4, 2 * width, HEAD_DIM))]
    ppermute x9 -> x12, starting transfers between devices: 15.2 us -> 13.9 us  [swapped(): lax.ppermute(value, 'tp', [(i, i ^ bits) for i in range(lax.axis_size('tp...]
    pallas_call x1, Pallas kernels: 0.66 us -> 1.8 us  [local(): pl.pallas_call(turn_kernel, out_shape=(state_shape,) * 3, in_specs=[vmem_...]
  transfers between devices with their start and end apart: 13 -> 15, of which waited for: 8 -> 6; matrix products, arithmetic and copies ran while one was open for 0% -> 9% of each run, Pallas kernels for 5% -> 9%
where the time goes in v4:
time: 75.7 us; the launch traced here: 75.1 us
  starting transfers between devices  25.6 us (34%)
  waiting for transfers between devices  22 us (29%)
  Pallas kernels  12.8 us (17%)
  local copies, waits for them, and re-layouts  12.3 us (16%)
  other arithmetic  1.56 us (2%)
  between operations  0.95 us (1%)
    ppermute x12, starting transfers between devices, swapped(): lax.ppermute(value, 'tp', [(i, i ^ bits) for i in range(lax.axis_size('tp...  13.9 us
    all_to_all x1, waiting for transfers between devices, local(): own_pages = lax.all_to_all(own_block, 'ctx', split_axis=0, concat_axis=0)  10.1 us
    ppermute x12, waiting for transfers between devices, swapped(): lax.ppermute(value, 'tp', [(i, i ^ bits) for i in range(lax.axis_size('tp...  7.23 us
    unnamed x34, local copies, waits for them, and re-layouts  6.97 us
    pallas_call x1, Pallas kernels, local(): pl.pallas_call(page_kernel, out_shape=(jax.ShapeDtypeStruct((tok_new, hea...  6.24 us
    all_to_all x1, starting transfers between devices, local(): own_pages = lax.all_to_all(own_block, 'ctx', split_axis=0, concat_axis=0)  4.86 us
    all_to_all x1, waiting for transfers between devices, local(): own_turn = lax.all_to_all(turn_block, 'ctx', split_axis=0, concat_axis=0)  4.6 us
    all_to_all x1, starting transfers between devices, local(): own_turn = lax.all_to_all(turn_block, 'ctx', split_axis=0, concat_axis=0)  4.14 us
  transfers between devices with their start and end apart: 15, of which 6 were waited for; matrix products, arithmetic and copies ran while one was open for 9% of the time, Pallas kernels for 9%

profile of v4, /device:TPU:1, one launch (start us, length us, event | category | flops | bytes accessed | tf_op | source)
XLA Modules:
  0.0 75.1 jit_solution(16650593375992583112)
XLA Ops:
  0.6 2.5 %collective-permute-start.1 = (bf16[384,512]{1,0:T(8,128)(2,1)}, bf16[384,512]{1,0:T(8,128)(2,1)S(1)}, u32[]{:S(2)}, u32[]{:S(2)}) collective-permute-start(bf16[384,512]{1,0:T(8,128)(2,1)} %bitcast.10), channel_id=1, source_target_pairs={{0,4},{1,5},{2,6},{3,7},{4,0},{5,1},{6,2},{7,3},{8,12},{9,13},{10,... | collective-permute-start | bytes 1179656 | tf_op jit(solution)/shard_map/ppermute | solution.py:20
  3.2 2.2 %collective-permute-start.2 = (bf16[384,512]{1,0:T(8,128)(2,1)}, bf16[384,512]{1,0:T(8,128)(2,1)}, u32[]{:S(2)}, u32[]{:S(2)}) collective-permute-start(bf16[384,512]{1,0:T(8,128)(2,1)} %bitcast.11), channel_id=1, source_target_pairs={{0,12},{1,13},{2,14},{3,15},{4,8},{5,9},{6,10},{7,11},{8,4},{9,5},... | collective-permute-start | bytes 1179656 | tf_op jit(solution)/shard_map/ppermute | solution.py:20
  5.4 2.3 %dynamic-slice_bitcast_fusion = bf16[4,1024,128]{2,1,0:T(8,128)(2,1)} fusion(bf16[4,2,1024,128]{3,2,1,0:T(8,128)(2,1)} %bitcast.7, s32[]{:T(128)S(6)} %select_n.37), kind=kLoop, calls=%fused_computation | loop fusion | bytes 2097156 | tf_op jit(solution)/shard_map/reshape | solution.py:264
  7.7 2.7 %collective-permute-start.9 = (bf16[4,1024,128]{2,1,0:T(8,128)(2,1)}, bf16[4,1024,128]{2,1,0:T(8,128)(2,1)S(1)}, u32[]{:S(2)}, u32[]{:S(2)}) collective-permute-start(bf16[4,1024,128]{2,1,0:T(8,128)(2,1)} %dynamic-slice_bitcast_fusion), channel_id=1, source_target_pairs={{0,66},{1,67},{2,64},{3,65},{4,70},{5,71},{6,68},{7,69},{8,74},{9,... | collective-permute-start | bytes 3145736 | tf_op jit(solution)/shard_map/ppermute | solution.py:26
  10.4 0.8 %dynamic_slice.6 = s32[256]{0:T(256)S(1)} dynamic-slice(s32[2048]{0:T(1024)} %param.13, s32[]{:T(128)S(6)} %select_n.32), dynamic_slice_sizes={256} | dynamic-slice | bytes 2052 | tf_op jit(solution)/shard_map/dynamic_slice | solution.py:273
  11.2 1.2 %fusion = (f32[640,64]{1,0:T(8,128)S(1)}, f32[640,64]{1,0:T(8,128)S(1)}, f32[640,64]{1,0:T(8,128)S(1)}) fusion(f32[64]{0:T(128)S(1)} %compare_select_fusion.1, f32[640]{0:T(1024)S(1)} %add_convert_fusion), kind=kLoop, calls=%fused_computation.7 | loop fusion | flops 81920 | bytes 494336 | tf_op jit(solution)/shard_map/neg | solution.py:47
  12.5 0.0 copy-start.11
  12.5 0.0 copy-start.13
  12.5 0.0 copy-start.15
  12.5 0.1 pad_maximum_fusion.2
  12.6 0.6 copy-done.11
  13.2 0.1 copy-done.13
  13.3 0.1 copy-done.15
  13.5 0.9 %copy-done.3 = bf16[256,512]{1,0:T(8,128)(2,1)S(1)} copy-done((bf16[256,512]{1,0:T(8,128)(2,1)S(1)}, bf16[256,512]{1,0:T(8,128)(2,1)}, u32[]{:S(2)}) %copy-start.3) | copy-done | bytes 262168
  14.4 0.8 %copy-done.6 = bf16[256,128]{1,0:T(8,128)(2,1)S(1)} copy-done((bf16[256,128]{1,0:T(8,128)(2,1)S(1)}, bf16[256,128]{1,0:T(8,128)(2,1)}, u32[]{:S(2)}) %copy-start.6) | copy-done | bytes 65560
  15.2 0.2 prepare.1
  15.5 0.0 copy-start.1
  15.5 0.8 %copy-done.1 = bf16[8,256,128]{2,1,0:T(8,128)(2,1)} copy-done((bf16[8,256,128]{2,1,0:T(8,128)(2,1)}, bf16[8,256,128]{2,1,0:T(8,128)(2,1)S(1)}, u32[]{:S(2)}) %copy-start.1) | copy-done | bytes 524312
  16.3 0.7 copy-done.4
  17.0 0.0 collective-permute-done.1.refs_2_
  17.0 0.0 collective-permute-done.2.refs_4_
  17.0 4.1 %all-to-all-start = ((bf16[8,256,128]{2,1,0:T(8,128)(2,1)}), bf16[8,256,128]{2,1,0:T(8,128)(2,1)}, u32[]{:S(2)}, u32[]{:S(2)}) async-start(bf16[8,256,128]{2,1,0:T(8,128)(2,1)} %copy-done.1), calls=%async_computation | async-start | bytes 1048576 | tf_op jit(solution)/shard_map/all_to_all | solution.py:289
  21.1 1.7 %collective-permute-start = (bf16[384,512]{1,0:T(8,128)(2,1)}, bf16[384,512]{1,0:T(8,128)(2,1)}, u32[]{:S(2)}, u32[]{:S(2)}) collective-permute-start(bf16[384,512]{1,0:T(8,128)(2,1)} %bitcast.12), channel_id=1, source_target_pairs={{0,1},{1,0},{2,3},{3,2},{4,5},{5,4},{6,7},{7,6},{8,9},{9,8},{10,11... | collective-permute-start | bytes 1179656 | tf_op jit(solution)/shard_map/ppermute | solution.py:20
  22.8 0.7 slice.24
  23.5 1.0 %collective-permute-start.5 = (bf16[192,512]{1,0:T(8,128)(2,1)}, bf16[192,512]{1,0:T(8,128)(2,1)}, u32[]{:S(2)}, u32[]{:S(2)}) collective-permute-start(bf16[192,512]{1,0:T(8,128)(2,1)} %slice.24), channel_id=1, source_target_pairs={{0,12},{1,13},{2,14},{3,15},{4,8},{5,9},{6,10},{7,11},{8,4},{9,5},... | collective-permute-start | bytes 589832 | tf_op jit(solution)/shard_map/ppermute | solution.py:20
  24.5 1.6 %slice.25 = bf16[192,512]{1,0:T(8,128)(2,1)} slice(bf16[384,512]{1,0:T(8,128)(2,1)} %collective-permute-done.2.refs_4_), slice={[192:384], [0:512]} | slice | bytes 393216 | tf_op jit(solution)/shard_map/slice | solution.py:268
  26.1 0.0 collective-permute-start.7
  26.1 4.6 %all-to-all-done.own = bf16[8,256,128]{2,1,0:T(8,128)(2,1)} async-done(((bf16[8,256,128]{2,1,0:T(8,128)(2,1)}), bf16[8,256,128]{2,1,0:T(8,128)(2,1)}, u32[]{:S(2)}, u32[]{:S(2)}) %all-to-all-start) | async-done | bytes 524320 | tf_op jit(solution)/shard_map/all_to_all | solution.py:289
  30.7 1.5 %collective-permute-start.11 = (bf16[8,256,128]{2,1,0:T(8,128)(2,1)}, bf16[8,256,128]{2,1,0:T(8,128)(2,1)S(1)}, u32[]{:S(2)}, u32[]{:S(2)}) collective-permute-start(bf16[8,256,128]{2,1,0:T(8,128)(2,1)} %all-to-all-done.own), channel_id=1, source_target_pairs={{0,1},{1,0},{2,3},{3,2},{4,5},{5,4},{6,7},{7,6},{8,9},{9,8},{10,11... | collective-permute-start | bytes 1572872 | tf_op jit(solution)/shard_map/ppermute | solution.py:20
  32.2 0.0 collective-permute-done.5.refs_6_
  32.2 0.1 collective-permute-start.6
  32.3 0.0 collective-permute-done.refs_1_
  32.3 0.4 collective-permute-start.3
  32.7 0.0 collective-permute-done.7.refs_8_
  32.7 1.0 %collective-permute-start.4 = (bf16[384,512]{1,0:T(8,128)(2,1)}, bf16[384,512]{1,0:T(8,128)(2,1)S(1)}, u32[]{:S(2)}, u32[]{:S(2)}) collective-permute-start(bf16[384,512]{1,0:T(8,128)(2,1)} %collective-permute-done.2.refs_4_), channel_id=1, source_target_pairs={{0,1},{1,0},{2,3},{3,2},{4,5},{5,4},{6,7},{7,6},{8,9},{9,8},{10,11... | collective-permute-start | bytes 1179656 | tf_op jit(solution)/shard_map/ppermute | solution.py:20
  33.7 0.7 collective-permute-done.6.refs_7_
  34.5 0.4 collective-permute-start.8
  34.9 1.3 %collective-permute-done.8.refs_9_ = bf16[192,512]{1,0:T(8,128)(2,1)S(1)} collective-permute-done((bf16[192,512]{1,0:T(8,128)(2,1)}, bf16[192,512]{1,0:T(8,128)(2,1)S(1)}, u32[]{:S(2)}, u32[]{:S(2)}) %collective-permute-start.8) | collective-permute-done | bytes 196640 | tf_op jit(solution)/shard_map/ppermute | solution.py:20
  36.1 0.0 collective-permute-done.3.refs_3_
  36.1 0.0 collective-permute-done.4.refs_5_
  36.1 0.0 collective-permute-done.9.refs_11_
  36.2 0.0 copy-done
  36.2 0.0 copy-start.2
  36.2 1.0 %copy-done.2 = bf16[3,128,512]{2,1,0:T(8,128)(2,1)S(1)} copy-done((bf16[3,128,512]{2,1,0:T(8,128)(2,1)S(1)}, bf16[3,128,512]{2,1,0:T(8,128)(2,1)}, u32[]{:S(2)}) %copy-start.2) | copy-done | bytes 393240
  37.2 3.5 %project.1 = (f32[384,128]{1,0:T(8,128)S(1)}, bf16[384,128]{1,0:T(8,128)(2,1)S(1)}) custom-call(bf16[384,512]{1,0:T(8,128)(2,1)S(1)} %bitcast.13, bf16[384,512]{1,0:T(8,128)(2,1)} %collective-permute-done.refs_1_, bf16[384,512]{1,0:T(8,128)(2,1)S(1)} %collective-permute-done.1.refs_2_, bf16[384,512]{1,0:T(8,128)(2,1)S(1)} %collective-permute-done.3.refs_3_, ...), custom_call_target="tpu_custom_call" | custom-call | tf_op jit(solution)/shard_map/project/pallas_call | solution.py:292
  40.7 0.0 copy-start.5
  40.7 2.1 %collective-permute-start.10 = (bf16[384,128]{1,0:T(8,128)(2,1)S(1)}, bf16[384,128]{1,0:T(8,128)(2,1)S(1)}, u32[]{:S(2)}, u32[]{:S(2)}) collective-permute-start(bf16[384,128]{1,0:T(8,128)(2,1)S(1)} %get-tuple-element.24), channel_id=1, source_target_pairs={{0,2},{1,3},{2,0},{3,1},{4,6},{5,7},{6,4},{7,5},{8,10},{9,11},{10,... | collective-permute-start | bytes 294920 | tf_op jit(solution)/shard_map/ppermute | solution.py:20
  42.9 0.0 copy-done.12
  42.9 0.0 copy-done.14
  42.9 0.0 copy-done.16
  42.9 0.2 pad_maximum_fusion
  43.0 3.3 %collective-permute-done.10.far = bf16[384,128]{1,0:T(8,128)(2,1)S(1)} collective-permute-done((bf16[384,128]{1,0:T(8,128)(2,1)S(1)}, bf16[384,128]{1,0:T(8,128)(2,1)S(1)}, u32[]{:S(2)}, u32[]{:S(2)}) %collective-permute-start.10) | collective-permute-done | bytes 98336 | tf_op jit(solution)/shard_map/ppermute | solution.py:20
  46.3 1.0 %finish.1 = bf16[8,384,128]{2,1,0:T(8,128)(2,1)} custom-call(f32[384,128]{1,0:T(8,128)S(1)} %get-tuple-element.23.own, bf16[384,128]{1,0:T(8,128)(2,1)S(1)} %collective-permute-done.10.far, f32[384,128]{1,0:T(8,128)S(1)} %get-tuple-element.40.cosine, f32[384,128]{1,0:T(8,128)S(1)} %get-tuple-element.39.sine), custom_call_target="tpu_custom_call" | custom-call | tf_op jit(solution)/shard_map/finish/pallas_call | solution.py:309
  47.3 0.0 collective-permute-done.11.other
  47.3 0.8 %copy-done.9 = bf16[8,256,128]{2,1,0:T(8,128)(2,1)} copy-done((bf16[8,256,128]{2,1,0:T(8,128)(2,1)}, bf16[8,256,128]{2,1,0:T(8,128)(2,1)S(1)}, u32[]{:S(2)}) %copy-start.9) | copy-done | bytes 524312
  48.1 4.9 %all-to-all-start.1 = ((bf16[8,384,128]{2,1,0:T(8,128)(2,1)}), bf16[8,384,128]{2,1,0:T(8,128)(2,1)S(1)}, u32[]{:S(2)}, u32[]{:S(2)}) async-start(bf16[8,384,128]{2,1,0:T(8,128)(2,1)} %finish.1), calls=%async_computation.1 | async-start | bytes 1572864 | tf_op jit(solution)/shard_map/all_to_all | solution.py:318
  53.0 0.0 copy-done.5
  53.0 1.0 %copy-done.10 = bf16[8,256,128]{2,1,0:T(8,128)(2,1)S(1)} copy-done((bf16[8,256,128]{2,1,0:T(8,128)(2,1)S(1)}, bf16[8,256,128]{2,1,0:T(8,128)(2,1)}, u32[]{:S(2)}) %copy-start.10) | copy-done | bytes 524312
  54.0 1.8 %turn_attention.1 = (f32[1024,128]{1,0:T(8,128)S(1)}, f32[1024,128]{1,0:T(8,128)S(1)}, f32[1024,128]{1,0:T(8,128)S(1)}) custom-call(bf16[4,256,128]{2,1,0:T(8,128)(2,1)S(1)} %copy-done.5, bf16[8,256,128]{2,1,0:T(8,128)(2,1)} %all-to-all-done.own, bf16[8,256,128]{2,1,0:T(8,128)(2,1)S(1)} %copy-done.10), custom_call_target="tpu_custom_call" | custom-call | flops 2147483648 | bytes 6291456 | tf_op jit(solution)/shard_map/turn_attention/pallas_call | solution.py:320
  55.8 10.1 %all-to-all-done.1 = bf16[8,384,128]{2,1,0:T(8,128)(2,1)S(1)} async-done(((bf16[8,384,128]{2,1,0:T(8,128)(2,1)}), bf16[8,384,128]{2,1,0:T(8,128)(2,1)S(1)}, u32[]{:S(2)}, u32[]{:S(2)}) %all-to-all-start.1) | async-done | bytes 786464 | tf_op jit(solution)/shard_map/all_to_all | solution.py:318
  66.0 0.9 %collective-permute-start.12 = (bf16[3072,128]{1,0:T(8,128)(2,1)S(1)}, bf16[3072,128]{1,0:T(8,128)(2,1)S(1)}, u32[]{:S(2)}, u32[]{:S(2)}) collective-permute-start(bf16[3072,128]{1,0:T(8,128)(2,1)S(1)} %bitcast.8), channel_id=1, source_target_pairs={{0,1},{1,0},{2,3},{3,2},{4,5},{5,4},{6,7},{7,6},{8,9},{9,8},{10,11... | collective-permute-start | bytes 2359304 | tf_op jit(solution)/shard_map/ppermute | solution.py:20
  66.8 1.9 %collective-permute-done.12.other = bf16[3072,128]{1,0:T(8,128)(2,1)S(1)} collective-permute-done((bf16[3072,128]{1,0:T(8,128)(2,1)S(1)}, bf16[3072,128]{1,0:T(8,128)(2,1)S(1)}, u32[]{:S(2)}, u32[]{:S(2)}) %collective-permute-start.12) | collective-permute-done | bytes 786464 | tf_op jit(solution)/shard_map/ppermute | solution.py:20
  68.7 0.0 copy-done.8
  68.7 6.2 %page_attention.1 = (bf16[256,512]{1,0:T(8,128)(2,1)}, bf16[1024,128]{1,0:T(8,128)(2,1)}) custom-call(s32[8,8]{1,0:T(8,128)S(1)} %copy-done.7, s32[8,8]{1,0:T(8,128)S(1)} %copy-done.8, bf16[4,256,128]{2,1,0:T(8,128)(2,1)S(1)} %copy-done.5, bf16[3072,128]{1,0:T(8,128)(2,1)S(1)} %bitcast.9, bf16[3072,128]{1,0:T(8,128)(2,1)S(1)} %collective-permute-done.12.other, ...), custom_call_target="tpu_custom_call" | custom-call | tf_op jit(solution)/shard_map/page_attention/pallas_call | solution.py:337
  (15 shorter events, 0.1 us)
Async XLA Ops:
  0.6 16.3 %collective-permute-start.1 = (bf16[384,512]{1,0:T(8,128)(2,1)}, bf16[384,512]{1,0:T(8,128)(2,1)S(1)}, u32[]{:S(2)}, u32[]{:S(2)}) collective-permute-start(bf16[384,512]{1,0:T(8,128)(2,1)} %bitcast.10), channel_id=1, source_target_pairs={{0,4},{1,5},{2,6},{3,7},{4,0},{5,1},{6,2},{7,3},{8,12},{9,13},{10,... | collective-permute-start | bytes 1179656 | tf_op jit(solution)/shard_map/ppermute | solution.py:20
  3.2 13.8 %collective-permute-start.2 = (bf16[384,512]{1,0:T(8,128)(2,1)}, bf16[384,512]{1,0:T(8,128)(2,1)}, u32[]{:S(2)}, u32[]{:S(2)}) collective-permute-start(bf16[384,512]{1,0:T(8,128)(2,1)} %bitcast.11), channel_id=1, source_target_pairs={{0,12},{1,13},{2,14},{3,15},{4,8},{5,9},{6,10},{7,11},{8,4},{9,5},... | collective-permute-start | bytes 1179656 | tf_op jit(solution)/shard_map/ppermute | solution.py:20
  7.7 28.5 %collective-permute-start.9 = (bf16[4,1024,128]{2,1,0:T(8,128)(2,1)}, bf16[4,1024,128]{2,1,0:T(8,128)(2,1)S(1)}, u32[]{:S(2)}, u32[]{:S(2)}) collective-permute-start(bf16[4,1024,128]{2,1,0:T(8,128)(2,1)} %dynamic-slice_bitcast_fusion), channel_id=1, source_target_pairs={{0,66},{1,67},{2,64},{3,65},{4,70},{5,71},{6,68},{7,69},{8,74},{9,... | collective-permute-start | bytes 3145736 | tf_op jit(solution)/shard_map/ppermute | solution.py:26
  11.2 24.9 %copy-start = (bf16[8192,128]{1,0:T(8,128)(2,1)S(1)}, bf16[8192,128]{1,0:T(8,128)(2,1)}, u32[]{:S(2)}) copy-start(bf16[8192,128]{1,0:T(8,128)(2,1)} %refs_10_.1) | copy-start | bytes 6291460
  12.5 0.7 copy-start.11
  12.5 0.9 %copy-start.13 = (f32[640,64]{1,0:T(8,128)}, f32[640,64]{1,0:T(8,128)S(1)}, u32[]{:S(2)}) copy-start(f32[640,64]{1,0:T(8,128)S(1)} %get-tuple-element.37) | copy-start | bytes 491524
  12.5 1.0 %copy-start.15 = (f32[640,64]{1,0:T(8,128)}, f32[640,64]{1,0:T(8,128)S(1)}, u32[]{:S(2)}) copy-start(f32[640,64]{1,0:T(8,128)S(1)} %get-tuple-element.38) | copy-start | bytes 491524
  13.5 0.9 %copy-start.3 = (bf16[256,512]{1,0:T(8,128)(2,1)S(1)}, bf16[256,512]{1,0:T(8,128)(2,1)}, u32[]{:S(2)}) copy-start(bf16[256,512]{1,0:T(8,128)(2,1)} %queries.1) | copy-start | bytes 786436
  14.4 0.8 %copy-start.6 = (bf16[256,128]{1,0:T(8,128)(2,1)S(1)}, bf16[256,128]{1,0:T(8,128)(2,1)}, u32[]{:S(2)}) copy-start(bf16[256,128]{1,0:T(8,128)(2,1)} %turn_kv.1) | copy-start | bytes 196612
  15.5 0.8 %copy-start.1 = (bf16[8,256,128]{2,1,0:T(8,128)(2,1)}, bf16[8,256,128]{2,1,0:T(8,128)(2,1)S(1)}, u32[]{:S(2)}) copy-start(bf16[8,256,128]{2,1,0:T(8,128)(2,1)S(1)} %get-tuple-element.25) | copy-start | bytes 1572868
  16.3 0.7 copy-start.4
  17.0 13.7 %all-to-all-start = ((bf16[8,256,128]{2,1,0:T(8,128)(2,1)}), bf16[8,256,128]{2,1,0:T(8,128)(2,1)}, u32[]{:S(2)}, u32[]{:S(2)}) async-start(bf16[8,256,128]{2,1,0:T(8,128)(2,1)} %copy-done.1), calls=%async_computation | async-start | bytes 1048576 | tf_op jit(solution)/shard_map/all_to_all | solution.py:289
  21.1 11.2 %collective-permute-start = (bf16[384,512]{1,0:T(8,128)(2,1)}, bf16[384,512]{1,0:T(8,128)(2,1)}, u32[]{:S(2)}, u32[]{:S(2)}) collective-permute-start(bf16[384,512]{1,0:T(8,128)(2,1)} %bitcast.12), channel_id=1, source_target_pairs={{0,1},{1,0},{2,3},{3,2},{4,5},{5,4},{6,7},{7,6},{8,9},{9,8},{10,11... | collective-permute-start | bytes 1179656 | tf_op jit(solution)/shard_map/ppermute | solution.py:20
  23.5 8.7 %collective-permute-start.5 = (bf16[192,512]{1,0:T(8,128)(2,1)}, bf16[192,512]{1,0:T(8,128)(2,1)}, u32[]{:S(2)}, u32[]{:S(2)}) collective-permute-start(bf16[192,512]{1,0:T(8,128)(2,1)} %slice.24), channel_id=1, source_target_pairs={{0,12},{1,13},{2,14},{3,15},{4,8},{5,9},{6,10},{7,11},{8,4},{9,5},... | collective-permute-start | bytes 589832 | tf_op jit(solution)/shard_map/ppermute | solution.py:20
  26.1 6.6 %collective-permute-start.7 = (bf16[192,512]{1,0:T(8,128)(2,1)}, bf16[192,512]{1,0:T(8,128)(2,1)}, u32[]{:S(2)}, u32[]{:S(2)}) collective-permute-start(bf16[192,512]{1,0:T(8,128)(2,1)} %slice.25), channel_id=1, source_target_pairs={{0,4},{1,5},{2,6},{3,7},{4,0},{5,1},{6,2},{7,3},{8,12},{9,13},{10,... | collective-permute-start | bytes 589832 | tf_op jit(solution)/shard_map/ppermute | solution.py:20
  30.7 16.6 %collective-permute-start.11 = (bf16[8,256,128]{2,1,0:T(8,128)(2,1)}, bf16[8,256,128]{2,1,0:T(8,128)(2,1)S(1)}, u32[]{:S(2)}, u32[]{:S(2)}) collective-permute-start(bf16[8,256,128]{2,1,0:T(8,128)(2,1)} %all-to-all-done.own), channel_id=1, source_target_pairs={{0,1},{1,0},{2,3},{3,2},{4,5},{5,4},{6,7},{7,6},{8,9},{9,8},{10,11... | collective-permute-start | bytes 1572872 | tf_op jit(solution)/shard_map/ppermute | solution.py:20
  32.2 2.3 %collective-permute-start.6 = (bf16[192,512]{1,0:T(8,128)(2,1)}, bf16[192,512]{1,0:T(8,128)(2,1)S(1)}, u32[]{:S(2)}, u32[]{:S(2)}) collective-permute-start(bf16[192,512]{1,0:T(8,128)(2,1)} %collective-permute-done.5.refs_6_), channel_id=1, source_target_pairs={{0,1},{1,0},{2,3},{3,2},{4,5},{5,4},{6,7},{7,6},{8,9},{9,8},{10,11... | collective-permute-start | bytes 589832 | tf_op jit(solution)/shard_map/ppermute | solution.py:20
  32.3 3.8 %collective-permute-start.3 = (bf16[384,512]{1,0:T(8,128)(2,1)S(1)}, bf16[384,512]{1,0:T(8,128)(2,1)S(1)}, u32[]{:S(2)}, u32[]{:S(2)}) collective-permute-start(bf16[384,512]{1,0:T(8,128)(2,1)S(1)} %collective-permute-done.1.refs_2_), channel_id=1, source_target_pairs={{0,1},{1,0},{2,3},{3,2},{4,5},{5,4},{6,7},{7,6},{8,9},{9,8},{10,11... | collective-permute-start | bytes 1179656 | tf_op jit(solution)/shard_map/ppermute | solution.py:20
  32.7 3.5 %collective-permute-start.4 = (bf16[384,512]{1,0:T(8,128)(2,1)}, bf16[384,512]{1,0:T(8,128)(2,1)S(1)}, u32[]{:S(2)}, u32[]{:S(2)}) collective-permute-start(bf16[384,512]{1,0:T(8,128)(2,1)} %collective-permute-done.2.refs_4_), channel_id=1, source_target_pairs={{0,1},{1,0},{2,3},{3,2},{4,5},{5,4},{6,7},{7,6},{8,9},{9,8},{10,11... | collective-permute-start | bytes 1179656 | tf_op jit(solution)/shard_map/ppermute | solution.py:20
  34.5 1.7 %collective-permute-start.8 = (bf16[192,512]{1,0:T(8,128)(2,1)}, bf16[192,512]{1,0:T(8,128)(2,1)S(1)}, u32[]{:S(2)}, u32[]{:S(2)}) collective-permute-start(bf16[192,512]{1,0:T(8,128)(2,1)} %collective-permute-done.7.refs_8_), channel_id=1, source_target_pairs={{0,1},{1,0},{2,3},{3,2},{4,5},{5,4},{6,7},{7,6},{8,9},{9,8},{10,11... | collective-permute-start | bytes 589832 | tf_op jit(solution)/shard_map/ppermute | solution.py:20
  36.2 1.0 %copy-start.2 = (bf16[3,128,512]{2,1,0:T(8,128)(2,1)S(1)}, bf16[3,128,512]{2,1,0:T(8,128)(2,1)}, u32[]{:S(2)}) copy-start(bf16[3,128,512]{2,1,0:T(8,128)(2,1)} %param.7) | copy-start | bytes 1179652
  37.2 5.7 %copy-start.12 = (f32[640,64]{1,0:T(8,128)S(1)}, f32[640,64]{1,0:T(8,128)}, u32[]{:S(2)}) copy-start(f32[640,64]{1,0:T(8,128)} %copy-done.11) | copy-start | bytes 491524
  37.2 5.7 %copy-start.14 = (f32[640,64]{1,0:T(8,128)S(1)}, f32[640,64]{1,0:T(8,128)}, u32[]{:S(2)}) copy-start(f32[640,64]{1,0:T(8,128)} %copy-done.13) | copy-start | bytes 491524
  37.2 5.7 %copy-start.16 = (f32[640,64]{1,0:T(8,128)S(1)}, f32[640,64]{1,0:T(8,128)}, u32[]{:S(2)}) copy-start(f32[640,64]{1,0:T(8,128)} %copy-done.15) | copy-start | bytes 491524
  40.7 12.3 %copy-start.5 = (bf16[4,256,128]{2,1,0:T(8,128)(2,1)S(1)}, bf16[4,256,128]{2,1,0:T(8,128)(2,1)}, u32[]{:S(2)}) copy-start(bf16[4,256,128]{2,1,0:T(8,128)(2,1)} %copy-done.4) | copy-start | bytes 786436
  40.7 5.6 %collective-permute-start.10 = (bf16[384,128]{1,0:T(8,128)(2,1)S(1)}, bf16[384,128]{1,0:T(8,128)(2,1)S(1)}, u32[]{:S(2)}, u32[]{:S(2)}) collective-permute-start(bf16[384,128]{1,0:T(8,128)(2,1)S(1)} %get-tuple-element.24), channel_id=1, source_target_pairs={{0,2},{1,3},{2,0},{3,1},{4,6},{5,7},{6,4},{7,5},{8,10},{9,11},{10,... | collective-permute-start | bytes 294920 | tf_op jit(solution)/shard_map/ppermute | solution.py:20
  47.3 0.8 %copy-start.9 = (bf16[8,256,128]{2,1,0:T(8,128)(2,1)}, bf16[8,256,128]{2,1,0:T(8,128)(2,1)S(1)}, u32[]{:S(2)}) copy-start(bf16[8,256,128]{2,1,0:T(8,128)(2,1)S(1)} %collective-permute-done.11.other) | copy-start | bytes 1572868
  48.1 17.9 %all-to-all-start.1 = ((bf16[8,384,128]{2,1,0:T(8,128)(2,1)}), bf16[8,384,128]{2,1,0:T(8,128)(2,1)S(1)}, u32[]{:S(2)}, u32[]{:S(2)}) async-start(bf16[8,384,128]{2,1,0:T(8,128)(2,1)} %finish.1), calls=%async_computation.1 | async-start | bytes 1572864 | tf_op jit(solution)/shard_map/all_to_all | solution.py:318
  53.0 1.0 %copy-start.10 = (bf16[8,256,128]{2,1,0:T(8,128)(2,1)S(1)}, bf16[8,256,128]{2,1,0:T(8,128)(2,1)}, u32[]{:S(2)}) copy-start(bf16[8,256,128]{2,1,0:T(8,128)(2,1)} %copy-done.9) | copy-start | bytes 1572868
  54.0 14.7 %copy-start.7 = (s32[8,8]{1,0:T(8,128)S(1)}, s32[8,8]{1,0:T(8,128)}, u32[]{:S(2)}) copy-start(s32[8,8]{1,0:T(8,128)} %page_table.1) | copy-start | bytes 772
  54.0 14.7 %copy-start.8 = (s32[8,8]{1,0:T(8,128)S(1)}, s32[8,8]{1,0:T(8,128)}, u32[]{:S(2)}) copy-start(s32[8,8]{1,0:T(8,128)} %page_counts.1) | copy-start | bytes 772
  66.0 2.8 %collective-permute-start.12 = (bf16[3072,128]{1,0:T(8,128)(2,1)S(1)}, bf16[3072,128]{1,0:T(8,128)(2,1)S(1)}, u32[]{:S(2)}, u32[]{:S(2)}) collective-permute-start(bf16[3072,128]{1,0:T(8,128)(2,1)S(1)} %bitcast.8), channel_id=1, source_target_pairs={{0,1},{1,0},{2,3},{3,2},{4,5},{5,4},{6,7},{7,6},{8,9},{9,8},{10,11... | collective-permute-start | bytes 2359304 | tf_op jit(solution)/shard_map/ppermute | solution.py:20

commit v5 on v4

v5 whole, which is shorter than its diff:
```python
import functools
import math

import jax
import jax.numpy as jnp
from jax import lax
from jax.experimental import pallas as pl
from jax.experimental.pallas import tpu as pltpu
from jax.sharding import PartitionSpec as P

HEAD_DIM = 128
PAGE = 128
SOURCES = 8
huge_value = 1e30
SCORE_SCALE = math.log2(math.e) / math.sqrt(HEAD_DIM)
VMEM_BYTES = 32 * 1024 * 1024


def swapped(value, bits):
    return lax.ppermute(value, "tp", [(i, i ^ bits) for i in range(lax.axis_size("tp"))])


def shifted(value, bits):
    return lax.ppermute(value, "ctx", [(i, i ^ bits) for i in range(lax.axis_size("ctx"))])


def across(value):
    peers = lax.axis_size("ctx") * lax.axis_size("tp")
    flip = 4 * lax.axis_size("tp") + 2
    return lax.ppermute(value, ("ctx", "tp"), [(i, i ^ flip) for i in range(peers)])


def inverse_freq(head_width):
    half_width = head_width // 2
    exponent = jnp.arange(half_width, dtype=jnp.float32) * 2.0 / head_width
    base_freq = jnp.exp(-exponent * math.log(500000.0))
    wavelength = 2.0 * math.pi / base_freq
    smooth = (8192.0 / wavelength - 1.0) / 3.0
    blended = (1.0 - smooth) * base_freq / 8.0 + smooth * base_freq
    return jnp.where(
        wavelength < 2048.0, base_freq, jnp.where(wavelength > 8192.0, base_freq / 8.0, blended)
    )


def rope_tables(positions):
    angle = positions.astype(jnp.float32)[:, None] * inverse_freq(HEAD_DIM)[None, :]
    cosine = jnp.cos(angle)
    sine = jnp.sin(angle)
    return (
        jnp.concatenate([cosine, cosine], axis=1),
        jnp.concatenate([-sine, sine], axis=1),
    )


def turned(value, cosine, sine):
    return value * cosine + pltpu.roll(value, HEAD_DIM // 2, 1) * sine


def any_spec():
    return pl.BlockSpec(memory_space=pl.ANY)


def hbm_spec():
    return pl.BlockSpec(memory_space=pltpu.HBM)


def vmem_spec():
    return pl.BlockSpec(memory_space=pltpu.VMEM)


def smem_spec():
    return pl.BlockSpec(memory_space=pltpu.SMEM)


def prepare_kernel(queries, turn_kv, cosine, sine, query_out, turn_out):
    is_key = lax.axis_index("tp") % 2 == 0
    c = cosine[...]
    s = sine[...]
    for head in range(query_out.shape[0]):
        block = queries[:, head * HEAD_DIM : (head + 1) * HEAD_DIM].astype(jnp.float32)
        query_out[head] = turned(block, c, s).astype(jnp.bfloat16)
    block = turn_kv[...].astype(jnp.float32)
    block = turned(block, jnp.where(is_key, c, 1.0), jnp.where(is_key, s, 0.0)).astype(jnp.bfloat16)
    turn_out[...] = block


def pick_kernel(weight, first_out, rest_out, sems):
    odd = lax.axis_index("ctx") % 2
    far = 1 - (lax.axis_index("tp") // 2) % 2
    depth = first_out.shape[0]
    copies = []
    for i, (group, out) in enumerate(((3 * odd, first_out), (1, rest_out.at[0]), (2, rest_out.at[1]))):
        row = pl.multiple_of((group * 2 + far) * depth, depth)
        copies.append(pltpu.make_async_copy(weight.at[pl.ds(row, depth)], out, sems.at[i]))
    for copy in copies:
        copy.start()
    for copy in copies:
        copy.wait()


def project_kernel(*refs):
    slices = refs[:10]
    weight, first, rest, relayed, own_out, near_out, far_out, x_buf, w_buf, sems = refs[10:]
    odd = lax.axis_index("ctx") % 2
    tp = lax.axis_index("tp")
    low = tp % 4
    spot = tp // 4
    rows = x_buf.shape[1]
    depth = slices[0].shape[1]

    def far_copy(at, r, half, act):
        part = pl.ds(half * depth, depth)
        source = pl.ds(pl.multiple_of(((low % 2) ^ half) * depth, depth), depth)

        def go(ref):
            place = w_buf.at[r, part, pl.ds(HEAD_DIM, HEAD_DIM)]
            act(pltpu.make_async_copy(ref.at[source], place, sems.at[r, half, 1]))

        pl.when(at == 3 * odd)(lambda: go(first))
        pl.when(at == 1)(lambda: go(rest.at[0]))
        pl.when(at == 2)(lambda: go(rest.at[1]))
        pl.when(at == 3 - 3 * odd)(lambda: go(relayed))

    copies = []
    for i, r in enumerate((0, 1, 3, 2)):
        at = spot ^ r
        for half in range(2):
            part = pl.ds(half * depth, depth)
            near_row = pl.multiple_of((at * 4 + (low ^ half)) * depth, depth)
            group = [
                pltpu.make_async_copy(
                    weight.at[pl.ds(near_row, depth)],
                    w_buf.at[r, part, pl.ds(0, HEAD_DIM)],
                    sems.at[r, half, 0],
                ),
            ]
            sent = [(slices[2 * i + half], 0, rows)]
            if r == 2:
                sent = [(slices[6 + half], 0, rows // 2), (slices[8 + half], rows // 2, rows // 2)]
            for k, (piece, start, count) in enumerate(sent):
                place = x_buf.at[r, pl.ds(start, count), part]
                group.append(pltpu.make_async_copy(piece, place, sems.at[r, half, 2 + k]))
            for copy in group:
                copy.start()
            far_copy(at, r, half, lambda copy: copy.start())
            copies.append(group)
    total = None
    for i, r in enumerate((0, 1, 3, 2)):
        for half in range(2):
            for copy in copies[2 * i + half]:
                copy.wait()
            far_copy(spot ^ r, r, half, lambda copy: copy.wait())
        part = jnp.dot(x_buf[r], w_buf[r], preferred_element_type=jnp.float32)
        total = part if total is None else total + part
    own_out[...] = total[:, :HEAD_DIM]
    near_out[...] = total[:, :HEAD_DIM].astype(jnp.bfloat16)
    far_out[...] = total[:, HEAD_DIM:].astype(jnp.bfloat16)


def finish_kernel(own, p1, p2, p3, cosine, sine, out):
    is_key = lax.axis_index("tp") % 2 == 0
    rows = own.shape[0]
    mine = own[...] + p1[...].astype(jnp.float32)
    other = p2[...].astype(jnp.float32) + p3[...].astype(jnp.float32)
    for i, value in enumerate((mine, other)):
        c = jnp.where(is_key, cosine[i * rows : (i + 1) * rows], 1.0)
        s = jnp.where(is_key, sine[i * rows : (i + 1) * rows], 0.0)
        out[i * rows : (i + 1) * rows] = turned(value, c, s).astype(jnp.bfloat16)


def scores_of(query, keys):
    return lax.dot_general(
        query, keys, (((1,), (1,)), ((), ())), preferred_element_type=jnp.float32
    )


def widened(value, width):
    return value if width == HEAD_DIM else jnp.concatenate([value] * (width // HEAD_DIM), axis=1)


def softmax_step(state, scores, values):
    top, total, acc = state
    width = scores.shape[1]
    new_top = jnp.maximum(top, jnp.max(scores, axis=1, keepdims=True))
    decay = jnp.exp2((top - new_top) * SCORE_SCALE)
    weights = jnp.exp2((scores - widened(new_top, width)) * SCORE_SCALE)
    total = total * decay
    for at in range(0, width, HEAD_DIM):
        total = total + weights[:, at : at + HEAD_DIM]
    acc = acc * decay + jnp.dot(
        weights.astype(jnp.bfloat16), values, preferred_element_type=jnp.float32
    )
    return new_top, total, acc


def turn_kernel(queries, near, far, other_near, other_far, top_out, total_out, acc_out):
    ctx = lax.axis_index("ctx")
    core = lax.axis_index("tp") % 2
    heads, rows, _ = queries.shape
    stacked = queries[...].reshape(heads * rows, HEAD_DIM)
    shape = (heads * rows, rows)
    token = lax.broadcasted_iota(jnp.int32, shape, 0) % rows
    seen = lax.broadcasted_iota(jnp.int32, shape, 1) <= token

    def keep(state):
        top_out[...], total_out[...], acc_out[...] = state

    none = jnp.zeros(top_out.shape, jnp.float32)

    def attend(keys, values):
        for i in range(SOURCES):
            source = ctx ^ ((0, 4, 1, 5, 3, 7, 2, 6)[i])
            part = slice(i % 4 * rows, (i % 4 + 1) * rows)

            def step():
                state = (top_out[...], total_out[...], acc_out[...])
                key, value = keys[i // 4][part], values[i // 4][part]
                keep(softmax_step(state, scores_of(stacked, key), value))

            if i:
                pl.when(source < ctx)(step)
            else:
                scores = jnp.where(seen, scores_of(stacked, keys[0][part]), -huge_value)
                keep(softmax_step((none - huge_value, none, none), scores, values[0][part]))

    pl.when(core == 0)(lambda: attend((near, far), (other_near, other_far)))
    pl.when(core == 1)(lambda: attend((other_near, other_far), (near, far)))


def attend_pages(queries, pairs, state_in, done):
    core = lax.axis_index("tp") % 2
    heads, rows, _ = queries.shape
    none = jnp.zeros((heads * rows, HEAD_DIM), jnp.float32)

    def attend(which):
        stacked = queries[...].reshape(heads * rows, HEAD_DIM)
        state = tuple(ref[...] for ref in state_in) or (none - huge_value, none, none)
        for pair in pairs:
            keys, values = pair[which], pair[1 - which]
            state = softmax_step(state, scores_of(stacked, keys[...]), values[...])
        done(state)

    pl.when(core == 0)(lambda: attend(0))
    pl.when(core == 1)(lambda: attend(1))


def pages_kernel(count, queries, *refs):
    pairs = [refs[2 * i : 2 * i + 2] for i in range(count)]
    state_in, state_out = refs[2 * count : -3], refs[-3:]

    def done(state):
        for ref, value in zip(state_out, state):
            ref[...] = value

    attend_pages(queries, pairs, state_in, done)


def last_kernel(
    page_table, page_counts, queries, own, other, top_in, total_in, acc_in,
    turn_top, turn_total, turn_acc, b0, b1, b3, b2, out, cache_out, zero_buf, sems,
):
    ctx = lax.axis_index("ctx")
    heads, rows, _ = queries.shape
    zero_buf[...] = jnp.zeros_like(zero_buf)
    held = b0.shape[0] // (2 * PAGE)
    waits = []
    for r, block in ((0, b0), (1, b1), (3, b3), (2, b2)):
        for half in range(2):
            slot = ctx ^ (r + 4 * half)
            page = page_table[ctx, slot] - slot * held + half * held
            live = page_counts[ctx, slot] > 0
            start = pl.multiple_of(page * PAGE, PAGE)
            place = cache_out.at[pl.ds(pl.multiple_of(slot * PAGE, PAGE), PAGE)]
            sem = sems.at[r, half]

            @pl.when(live)
            def _():
                pltpu.make_async_copy(block.at[pl.ds(start, PAGE)], place, sem).start()

            @pl.when(jnp.logical_not(live))
            def _():
                pltpu.make_async_copy(zero_buf, place, sem).start()

            waits.append(pltpu.make_async_copy(zero_buf, place, sem))

    def done(state):
        top, total, acc = state
        most = jnp.maximum(top, turn_top[...])
        scale = jnp.exp2((top - most) * SCORE_SCALE)
        turn_scale = jnp.exp2((turn_top[...] - most) * SCORE_SCALE)
        total = total * scale + turn_total[...] * turn_scale
        acc = acc * scale + turn_acc[...] * turn_scale
        result = acc / jnp.sum(total, axis=1, keepdims=True)
        result = result.astype(jnp.bfloat16)
        for head in range(heads):
            out[:, head * HEAD_DIM : (head + 1) * HEAD_DIM] = result[head * rows : (head + 1) * rows]

    attend_pages(queries, [(own, other)], (top_in, total_in, acc_in), done)
    for wait in waits:
        wait.wait()


def local(stored_pages, kv_weight, page_table, page_counts, queries, turn_kv, turn_pos):
    ctx_index = lax.axis_index("ctx")
    tp_index = lax.axis_index("tp")
    held, page_rows, width = stored_pages.shape
    rows = held * page_rows
    tok_new = queries.shape[0]
    heads_dev = queries.shape[1] // HEAD_DIM
    bf16 = jnp.bfloat16
    f32 = jnp.float32
    params = pltpu.CompilerParams(vmem_limit_bytes=VMEM_BYTES)

    own_x = stored_pages.reshape(rows, width)
    first, rest = pl.pallas_call(
        pick_kernel,
        out_shape=(
            jax.ShapeDtypeStruct((2 * width, HEAD_DIM), bf16),
            jax.ShapeDtypeStruct((2, 2 * width, HEAD_DIM), bf16),
        ),
        in_specs=[hbm_spec()],
        out_specs=(hbm_spec(),) * 2,
        scratch_shapes=[pltpu.SemaphoreType.DMA((3,))],
        compiler_params=params,
        name="pick",
    )(kv_weight)
    first, rest, turn_kv = lax.optimization_barrier((first, rest, turn_kv))
    first = across(first)
    rest = across(rest)
    local_pos = lax.dynamic_slice_in_dim(turn_pos, ctx_index * tok_new, tok_new)
    within = jnp.arange(rows, dtype=jnp.int32)
    page_pos = [ctx_index * rows + within, (ctx_index ^ 4) * rows + within]
    cosine, sine = rope_tables(jnp.concatenate([local_pos] + page_pos))

    query_heads, turn_block = pl.pallas_call(
        prepare_kernel,
        out_shape=(
            jax.ShapeDtypeStruct((heads_dev, tok_new, HEAD_DIM), bf16),
            jax.ShapeDtypeStruct((tok_new, HEAD_DIM), bf16),
        ),
        in_specs=[vmem_spec()] * 4,
        out_specs=(vmem_spec(), vmem_spec()),
        compiler_params=params,
        name="prepare",
    )(queries, turn_kv, cosine[:tok_new], sine[:tok_new])
    turn_pair = jnp.concatenate([turn_block, shifted(turn_block, 4)])
    carried = shifted(jnp.concatenate([first, turn_pair]), 1)
    relayed = carried[: 2 * width]
    turn_near = jnp.concatenate([turn_pair, carried[2 * width :]])

    x1 = swapped(own_x, 4)
    x3 = swapped(own_x, 12)
    x2a = swapped(x1[: rows // 2], 12)
    x2b = swapped(x3[rows // 2 :], 4)
    late_x, x1 = lax.optimization_barrier((own_x, x1))
    own_pair = swapped(late_x, 1)

    pieces = [own_x, own_pair]
    for piece in (x1, x3, x2a, x2b):
        pieces += [piece, swapped(piece, 1)]

    part_shape = jax.ShapeDtypeStruct((rows, HEAD_DIM), bf16)
    own_part, near_part, far_part = pl.pallas_call(
        project_kernel,
        out_shape=(jax.ShapeDtypeStruct((rows, HEAD_DIM), f32), part_shape, part_shape),
        in_specs=[any_spec()] * 14,
        out_specs=(vmem_spec(),) * 3,
        scratch_shapes=[
            pltpu.VMEM((4, rows, 2 * width), bf16),
            pltpu.VMEM((4, 2 * width, 2 * HEAD_DIM), bf16),
            pltpu.SemaphoreType.DMA((4, 2, 4)),
        ],
        compiler_params=params,
        name="project",
    )(*pieces, kv_weight, first, rest, relayed)
    turn_far = shifted(turn_near, 3)
    got1 = swapped(far_part, 2)
    got2 = shifted(near_part, 4)
    got3 = across(far_part)
    own_block = pl.pallas_call(
        finish_kernel,
        out_shape=jax.ShapeDtypeStruct((2 * rows, HEAD_DIM), bf16),
        in_specs=[vmem_spec()] * 6,
        out_specs=vmem_spec(),
        compiler_params=params,
        name="finish",
    )(own_part, got1, got2, got3, cosine[tok_new:], sine[tok_new:])
    blocks = [own_block] + [shifted(own_block, bits) for bits in (1, 3, 2)]
    own_pair = swapped(own_block, 1)

    def cost(keys):
        work = heads_dev * tok_new * keys
        return pl.CostEstimate(
            flops=4 * work * HEAD_DIM, bytes_accessed=4 * 1024 * 1024, transcendentals=work
        )

    state_shape = (jax.ShapeDtypeStruct((heads_dev * tok_new, HEAD_DIM), f32),) * 3
    turn_state = pl.pallas_call(
        turn_kernel,
        out_shape=state_shape,
        in_specs=[vmem_spec()] * 5,
        out_specs=(vmem_spec(),) * 3,
        compiler_params=params,
        cost_estimate=cost(SOURCES * tok_new),
        name="turn_attention",
    )(query_heads, turn_near, turn_far, swapped(turn_near, 1), swapped(turn_far, 1))

    def attend_more(name, group, state):
        flat = [part for pair in group for part in pair]
        return pl.pallas_call(
            functools.partial(pages_kernel, len(group)),
            out_shape=state_shape,
            in_specs=[vmem_spec()] * (1 + len(flat) + len(state)),
            out_specs=(vmem_spec(),) * 3,
            compiler_params=params,
            cost_estimate=cost(2 * rows * len(group)),
            name=name,
        )(query_heads, *flat, *state)

    state = attend_more("pages_near", [(own_block, own_pair)], ())
    blocks[1], blocks[2], state, turn_state = lax.optimization_barrier(
        (blocks[1], blocks[2], state, turn_state)
    )
    pairs = [(block, swapped(block, 1)) for block in blocks[1:]]
    state = attend_more("pages_side", pairs[:2], state)
    attended, cache = pl.pallas_call(
        last_kernel,
        out_shape=(
            jax.ShapeDtypeStruct((tok_new, heads_dev * HEAD_DIM), bf16),
            jax.ShapeDtypeStruct((SOURCES * PAGE, HEAD_DIM), bf16),
        ),
        in_specs=[smem_spec(), smem_spec()] + [vmem_spec()] * 9 + [any_spec()] * 4,
        out_specs=(vmem_spec(), any_spec()),
        scratch_shapes=[
            pltpu.VMEM((PAGE, HEAD_DIM), bf16),
            pltpu.SemaphoreType.DMA((4, 2)),
        ],
        compiler_params=params,
        cost_estimate=cost(2 * rows),
        name="pages_last",
    )(page_table, page_counts, query_heads, *pairs[2], *state, *turn_state, *blocks)
    return (attended, cache)


def solution(mesh):
    placed = (P("ctx", None, "tp"), P(None, "tp"), P(), P(), P("ctx", "tp"), P("ctx", "tp"), P())
    return jax.shard_map(
        local,
        mesh=mesh,
        in_specs=placed,
        out_specs=(P("ctx", "tp"), P("ctx", "tp")),
        check_vma=False,
    )
```

time: 75.7 us -> 68.3 us (0.902)
  local copies, waits for them, and re-layouts: 12.3 us -> 2.44 us
  starting transfers between devices: 25.6 us -> 32.1 us
  waiting for transfers between devices: 22 us -> 18.2 us
  Pallas kernels: 12.8 us -> 11.7 us
  other arithmetic: 1.56 us -> 2.52 us
    all_to_all x2 -> x0, waiting for transfers between devices: 14.7 us -> none  [the longest x1 10.1 us: local(): own_pages = lax.all_to_all(own_block, 'ctx', split_axis=0, concat_axis=0)]
    ppermute x0 -> x7, waiting for transfers between devices: none -> 9.09 us  [shifted(): lax.ppermute(value, 'ctx', [(i, i ^ bits) for i in range(lax.axis_size('c...]
    all_to_all x2 -> x0, starting transfers between devices: 9 us -> none  [the longest x1 4.86 us: local(): own_pages = lax.all_to_all(own_block, 'ctx', split_axis=0, concat_axis=0)]
    ppermute x0 -> x7, starting transfers between devices: none -> 7 us  [shifted(): lax.ppermute(value, 'ctx', [(i, i ^ bits) for i in range(lax.axis_size('c...]
    ppermute x12 -> x16, starting transfers between devices: 13.9 us -> 20.3 us  [swapped(): lax.ppermute(value, 'tp', [(i, i ^ bits) for i in range(lax.axis_size('tp...]
    unnamed x34 -> x14, local copies, waits for them, and re-layouts: 6.97 us -> 1.62 us
    reshape x1 -> x0, local copies, waits for them, and re-layouts: 2.27 us -> none  [local(): far_weight = across(far_rows.reshape(4, 2 * width, HEAD_DIM))]
    ppermute x1 -> x3, starting transfers between devices: 2.73 us -> 4.83 us  [across(): lax.ppermute(value, ('ctx', 'tp'), [(i, i ^ flip) for i in range(peers)])]
  transfers between devices with their start and end apart: 15 -> 26, of which waited for: 6 -> 8; matrix products, arithmetic and copies ran while one was open for 9% -> 5% of each run, Pallas kernels for 9% -> 12%
where the time goes in v5:
time: 68.3 us; the launch traced here: 68.1 us
  starting transfers between devices  32.1 us (47%)
  waiting for transfers between devices  18.2 us (27%)
  Pallas kernels  11.7 us (17%)
  other arithmetic  2.52 us (4%)
  local copies, waits for them, and re-layouts  2.44 us (4%)
  between operations  1.11 us (2%)
    ppermute x16, starting transfers between devices, swapped(): lax.ppermute(value, 'tp', [(i, i ^ bits) for i in range(lax.axis_size('tp...  20.3 us
    ppermute x7, waiting for transfers between devices, shifted(): lax.ppermute(value, 'ctx', [(i, i ^ bits) for i in range(lax.axis_size('c...  9.09 us
    ppermute x16, waiting for transfers between devices, swapped(): lax.ppermute(value, 'tp', [(i, i ^ bits) for i in range(lax.axis_size('tp...  9.03 us
    ppermute x7, starting transfers between devices, shifted(): lax.ppermute(value, 'ctx', [(i, i ^ bits) for i in range(lax.axis_size('c...  7 us
    ppermute x3, starting transfers between devices, across(): lax.ppermute(value, ('ctx', 'tp'), [(i, i ^ flip) for i in range(peers)])  4.83 us
    pallas_call x2, Pallas kernels, attend_more(): pl.pallas_call(functools.partial(pages_kernel, len(group)), out_shape=sta...  4.02 us
    pallas_call x1, Pallas kernels, local(): pl.pallas_call(last_kernel, out_shape=(jax.ShapeDtypeStruct((tok_new, hea...  3.29 us
    pallas_call x1, Pallas kernels, local(): pl.pallas_call(project_kernel, out_shape=(jax.ShapeDtypeStruct((rows, HEA...  3.15 us
  transfers between devices with their start and end apart: 26, of which 8 were waited for; matrix products, arithmetic and copies ran while one was open for 5% of the time, Pallas kernels for 12%

profile of v5, /device:TPU:1, one launch (start us, length us, event | category | flops | bytes accessed | tf_op | source)
XLA Modules:
  0.0 68.1 jit_solution(16580430282926202588)
XLA Ops:
  0.6 0.0 copy-start
  0.6 1.6 %copy-done = bf16[8192,128]{1,0:T(8,128)(2,1)S(1)} copy-done((bf16[8192,128]{1,0:T(8,128)(2,1)S(1)}, bf16[8192,128]{1,0:T(8,128)(2,1)}, u32[]{:S(2)}) %copy-start) | copy-done | bytes 2097176
  2.2 0.1 pick.1
  2.3 0.0 copy-start.3
  2.3 0.0 copy-start.4
  2.3 0.0 copy-start.2
  2.4 3.6 %collective-permute-start.9 = (bf16[1024,128]{1,0:T(8,128)(2,1)S(1)}, bf16[1024,128]{1,0:T(8,128)(2,1)S(1)}, u32[]{:S(2)}, u32[]{:S(2)}) collective-permute-start(bf16[1024,128]{1,0:T(8,128)(2,1)S(1)} %get-tuple-element.37), channel_id=1, source_target_pairs={{0,66},{1,67},{2,64},{3,65},{4,70},{5,71},{6,68},{7,69},{8,74},{9,... | collective-permute-start | bytes 786440 | tf_op jit(solution)/shard_map/ppermute | solution.py:30
  6.0 0.8 %dynamic_slice.3 = s32[256]{0:T(256)S(1)} dynamic-slice(s32[2048]{0:T(1024)} %param.13, s32[]{:T(128)S(6)} %select_n.18), dynamic_slice_sizes={256} | dynamic-slice | bytes 2052 | tf_op jit(solution)/shard_map/dynamic_slice | solution.py:330
  6.8 1.9 %fusion = (f32[1024,64]{1,0:T(8,128)S(1)}, f32[1024,64]{1,0:T(8,128)S(1)}, f32[1024,64]{1,0:T(8,128)S(1)}) fusion(f32[64]{0:T(128)S(1)} %compare_select_fusion.1, f32[1024]{0:T(1024)S(1)} %add_convert_fusion), kind=kLoop, calls=%fused_computation.6 | loop fusion | flops 131072 | bytes 790784 | tf_op jit(solution)/shard_map/neg | solution.py:51
  8.7 0.1 pad_maximum_fusion.5.cosine
  8.8 0.1 pad_maximum_fusion.4.sine
  8.9 0.2 prepare.1
  9.2 0.1 collective-permute-start.11
  9.3 0.0 copy-start.1
  9.3 3.8 %collective-permute-start.3 = (bf16[384,512]{1,0:T(8,128)(2,1)S(1)}, bf16[384,512]{1,0:T(8,128)(2,1)S(1)}, u32[]{:S(2)}, u32[]{:S(2)}) collective-permute-start(bf16[384,512]{1,0:T(8,128)(2,1)S(1)} %bitcast.1), channel_id=1, source_target_pairs={{0,12},{1,13},{2,14},{3,15},{4,8},{5,9},{6,10},{7,11},{8,4},{9,5},... | collective-permute-start | bytes 1179656 | tf_op jit(solution)/shard_map/ppermute | solution.py:20
  13.1 0.5 collective-permute-start.10
  13.6 0.0 collective-permute-done.9.refs_11_
  13.7 1.3 %collective-permute-start.12 = (bf16[1536,128]{1,0:T(8,128)(2,1)S(1)}, bf16[1536,128]{1,0:T(8,128)(2,1)S(1)}, u32[]{:S(2)}, u32[]{:S(2)}) collective-permute-start(bf16[1536,128]{1,0:T(8,128)(2,1)S(1)} %pad_maximum_fusion.2), channel_id=1, source_target_pairs={{0,16},{16,0},{32,48},{48,32},{64,80},{80,64},{96,112},{112,96},{1... | collective-permute-start | bytes 1179656 | tf_op jit(solution)/shard_map/ppermute | solution.py:24
  15.0 6.6 %collective-permute-done.3.refs_4_ = bf16[384,512]{1,0:T(8,128)(2,1)S(1)} collective-permute-done((bf16[384,512]{1,0:T(8,128)(2,1)S(1)}, bf16[384,512]{1,0:T(8,128)(2,1)S(1)}, u32[]{:S(2)}, u32[]{:S(2)}) %collective-permute-start.3) | collective-permute-done | bytes 393248 | tf_op jit(solution)/shard_map/ppermute | solution.py:20
  21.6 0.1 collective-permute-start.7
  21.7 0.7 %collective-permute-done.refs_2_ = bf16[384,512]{1,0:T(8,128)(2,1)S(1)} collective-permute-done((bf16[384,512]{1,0:T(8,128)(2,1)S(1)}, bf16[384,512]{1,0:T(8,128)(2,1)S(1)}, u32[]{:S(2)}, u32[]{:S(2)}) %collective-permute-start) | collective-permute-done | bytes 393248 | tf_op jit(solution)/shard_map/ppermute | solution.py:20
  22.5 1.7 %collective-permute-start.5 = (bf16[192,512]{1,0:T(8,128)(2,1)S(1)}, bf16[192,512]{1,0:T(8,128)(2,1)S(1)}, u32[]{:S(2)}, u32[]{:S(2)}) collective-permute-start(bf16[192,512]{1,0:T(8,128)(2,1)S(1)} %slice.32), channel_id=1, source_target_pairs={{0,12},{1,13},{2,14},{3,15},{4,8},{5,9},{6,10},{7,11},{8,4},{9,5},... | collective-permute-start | bytes 589832 | tf_op jit(solution)/shard_map/ppermute | solution.py:20
  24.2 2.2 %collective-permute-start.1 = (bf16[384,512]{1,0:T(8,128)(2,1)S(1)}, bf16[384,512]{1,0:T(8,128)(2,1)S(1)}, u32[]{:S(2)}, u32[]{:S(2)}) collective-permute-start(bf16[384,512]{1,0:T(8,128)(2,1)S(1)} %bitcast.3), channel_id=1, source_target_pairs={{0,1},{1,0},{2,3},{3,2},{4,5},{5,4},{6,7},{7,6},{8,9},{9,8},{10,11... | collective-permute-start | bytes 1179656 | tf_op jit(solution)/shard_map/ppermute | solution.py:20
  26.3 0.1 collective-permute-done.10.refs_12_
  26.5 2.2 %collective-permute-start.4 = (bf16[384,512]{1,0:T(8,128)(2,1)S(1)}, bf16[384,512]{1,0:T(8,128)(2,1)S(1)}, u32[]{:S(2)}, u32[]{:S(2)}) collective-permute-start(bf16[384,512]{1,0:T(8,128)(2,1)S(1)} %collective-permute-done.3.refs_4_), channel_id=1, source_target_pairs={{0,1},{1,0},{2,3},{3,2},{4,5},{5,4},{6,7},{7,6},{8,9},{9,8},{10,11... | collective-permute-start | bytes 1179656 | tf_op jit(solution)/shard_map/ppermute | solution.py:20
  28.7 0.0 collective-permute-done.7.refs_8_
  28.7 0.3 collective-permute-start.8
  29.0 0.0 collective-permute-done.12
  29.0 0.2 collective-permute-start.2
  29.2 0.0 collective-permute-done.5.refs_6_
  29.2 2.6 %collective-permute-start.21 = (bf16[1024,128]{1,0:T(8,128)(2,1)S(1)}, bf16[1024,128]{1,0:T(8,128)(2,1)S(1)}, u32[]{:S(2)}, u32[]{:S(2)}) collective-permute-start(bf16[1024,128]{1,0:T(8,128)(2,1)S(1)} %pad_maximum_fusion.3.near), channel_id=1, source_target_pairs={{0,48},{16,32},{32,16},{48,0},{64,112},{80,96},{96,80},{112,64},{1... | collective-permute-start | bytes 786440 | tf_op jit(solution)/shard_map/ppermute | solution.py:24
  31.8 0.0 collective-permute-done.8.refs_9_
  31.8 2.6 %collective-permute-start.6 = (bf16[192,512]{1,0:T(8,128)(2,1)S(1)}, bf16[192,512]{1,0:T(8,128)(2,1)S(1)}, u32[]{:S(2)}, u32[]{:S(2)}) collective-permute-start(bf16[192,512]{1,0:T(8,128)(2,1)S(1)} %collective-permute-done.5.refs_6_), channel_id=1, source_target_pairs={{0,1},{1,0},{2,3},{3,2},{4,5},{5,4},{6,7},{7,6},{8,9},{9,8},{10,11... | collective-permute-start | bytes 589832 | tf_op jit(solution)/shard_map/ppermute | solution.py:20
  34.4 0.2 pad_maximum_fusion.sine
  34.6 0.0 collective-permute-done.4.refs_5_
  34.6 0.1 collective-permute-start.22
  34.7 0.8 %collective-permute-done.6.refs_7_ = bf16[192,512]{1,0:T(8,128)(2,1)S(1)} collective-permute-done((bf16[192,512]{1,0:T(8,128)(2,1)S(1)}, bf16[192,512]{1,0:T(8,128)(2,1)S(1)}, u32[]{:S(2)}, u32[]{:S(2)}) %collective-permute-start.6) | collective-permute-done | bytes 196640 | tf_op jit(solution)/shard_map/ppermute | solution.py:20
  35.5 3.1 %project.1 = (f32[384,128]{1,0:T(8,128)S(1)}, bf16[384,128]{1,0:T(8,128)(2,1)S(1)}, bf16[384,128]{1,0:T(8,128)(2,1)S(1)}) custom-call(bf16[384,512]{1,0:T(8,128)(2,1)S(1)} %bitcast.4, bf16[384,512]{1,0:T(8,128)(2,1)S(1)} %collective-permute-done.1.refs_1_, bf16[384,512]{1,0:T(8,128)(2,1)S(1)} %collective-permute-done.refs_2_, ...), custom_call_target="tpu_custom_call" | custom-call | tf_op jit(solution)/shard_map/project/pallas_call | solution.py:363
  38.6 0.7 collective-permute-start.15
  39.3 2.6 %collective-permute-start.13 = (bf16[384,128]{1,0:T(8,128)(2,1)S(1)}, bf16[384,128]{1,0:T(8,128)(2,1)S(1)}, u32[]{:S(2)}, u32[]{:S(2)}) collective-permute-start(bf16[384,128]{1,0:T(8,128)(2,1)S(1)} %get-tuple-element.41), channel_id=1, source_target_pairs={{0,2},{1,3},{2,0},{3,1},{4,6},{5,7},{6,4},{7,5},{8,10},{9,11},{10,... | collective-permute-start | bytes 294920 | tf_op jit(solution)/shard_map/ppermute | solution.py:20
  41.9 0.0 collective-permute-start.14
  42.0 1.2 %collective-permute-start.23 = (bf16[1024,128]{1,0:T(8,128)(2,1)S(1)}, bf16[1024,128]{1,0:T(8,128)(2,1)S(1)}, u32[]{:S(2)}, u32[]{:S(2)}) collective-permute-start(bf16[1024,128]{1,0:T(8,128)(2,1)S(1)} %collective-permute-done.21.far), channel_id=1, source_target_pairs={{0,1},{1,0},{2,3},{3,2},{4,5},{5,4},{6,7},{7,6},{8,9},{9,8},{10,11... | collective-permute-start | bytes 786440 | tf_op jit(solution)/shard_map/ppermute | solution.py:20
  43.2 0.2 pad_maximum_fusion.1.cosine
  43.3 3.4 %collective-permute-done.14.p2 = bf16[384,128]{1,0:T(8,128)(2,1)S(1)} collective-permute-done((bf16[384,128]{1,0:T(8,128)(2,1)S(1)}, bf16[384,128]{1,0:T(8,128)(2,1)S(1)}, u32[]{:S(2)}, u32[]{:S(2)}) %collective-permute-start.14) | collective-permute-done | bytes 98336 | tf_op jit(solution)/shard_map/ppermute | solution.py:24
  46.7 0.0 collective-permute-done.15.p3
  46.7 0.0 collective-permute-done.13.p1
  46.7 0.2 finish.1.refs_0_.b0
  46.9 1.2 %collective-permute-start.20 = (bf16[768,128]{1,0:T(8,128)(2,1)S(1)}, bf16[768,128]{1,0:T(8,128)(2,1)S(1)}, u32[]{:S(2)}, u32[]{:S(2)}) collective-permute-start(bf16[768,128]{1,0:T(8,128)(2,1)S(1)} %finish.1.refs_0_.b0), channel_id=1, source_target_pairs={{0,1},{1,0},{2,3},{3,2},{4,5},{5,4},{6,7},{7,6},{8,9},{9,8},{10,11... | collective-permute-start | bytes 589832 | tf_op jit(solution)/shard_map/ppermute | solution.py:20
  48.1 0.2 collective-permute-start.19
  48.3 0.0 collective-permute-start.18
  48.3 0.9 %collective-permute-done.20.refs_1_ = bf16[768,128]{1,0:T(8,128)(2,1)S(1)} collective-permute-done((bf16[768,128]{1,0:T(8,128)(2,1)S(1)}, bf16[768,128]{1,0:T(8,128)(2,1)S(1)}, u32[]{:S(2)}, u32[]{:S(2)}) %collective-permute-start.20) | collective-permute-done | bytes 196640 | tf_op jit(solution)/shard_map/ppermute | solution.py:20
  49.2 2.8 %collective-permute-start.16 = (bf16[768,128]{1,0:T(8,128)(2,1)S(1)}, bf16[768,128]{1,0:T(8,128)(2,1)S(1)}, u32[]{:S(2)}, u32[]{:S(2)}) collective-permute-start(bf16[768,128]{1,0:T(8,128)(2,1)S(1)} %finish.1.refs_0_.b0), channel_id=1, source_target_pairs={{0,32},{16,48},{32,0},{48,16},{64,96},{80,112},{96,64},{112,80},{1... | collective-permute-start | bytes 589832 | tf_op jit(solution)/shard_map/ppermute | solution.py:24
  52.0 1.4 %pages_near.1 = (f32[1024,128]{1,0:T(8,128)S(1)}, f32[1024,128]{1,0:T(8,128)S(1)}, f32[1024,128]{1,0:T(8,128)S(1)}) custom-call(bf16[4,256,128]{2,1,0:T(8,128)(2,1)S(1)} %get-tuple-element.34.queries, bf16[768,128]{1,0:T(8,128)(2,1)S(1)} %finish.1.refs_0_.b0, bf16[768,128]{1,0:T(8,128)(2,1)S(1)} %collective-permute-done.20.refs_1_), custom_call_target="tpu_custom_call" | custom-call | flops 402653184 | bytes 4194304 | tf_op jit(solution)/shard_map/pages_near/pallas_call | solution.py:410
  53.5 0.0 collective-permute-done.22.other_near
  53.5 0.8 %turn_attention.1 = (f32[1024,128]{1,0:T(8,128)S(1)}, f32[1024,128]{1,0:T(8,128)S(1)}, f32[1024,128]{1,0:T(8,128)S(1)}) custom-call(bf16[4,256,128]{2,1,0:T(8,128)(2,1)S(1)} %get-tuple-element.34.queries, bf16[1024,128]{1,0:T(8,128)(2,1)S(1)} %pad_maximum_fusion.3.near, bf16[1024,128]{1,0:T(8,128)(2,1)S(1)} %collective-permute-done.21.far, ...), custom_call_target="tpu_custom_call" | custom-call | flops 1073741824 | bytes 4194304 | tf_op jit(solution)/shard_map/turn_attention/pallas_call | solution.py:398
  54.3 0.0 copy-start.5
  54.3 0.0 copy-start.6
  54.3 1.5 %collective-permute-done.19.refs_2_.b3 = bf16[768,128]{1,0:T(8,128)(2,1)S(1)} collective-permute-done((bf16[768,128]{1,0:T(8,128)(2,1)S(1)}, bf16[768,128]{1,0:T(8,128)(2,1)S(1)}, u32[]{:S(2)}, u32[]{:S(2)}) %collective-permute-start.19) | collective-permute-done | bytes 196640 | tf_op jit(solution)/shard_map/ppermute | solution.py:24
  55.8 0.9 %collective-permute-start.24 = (bf16[768,128]{1,0:T(8,128)(2,1)S(1)}, bf16[768,128]{1,0:T(8,128)(2,1)S(1)}, u32[]{:S(2)}, u32[]{:S(2)}) collective-permute-start(bf16[768,128]{1,0:T(8,128)(2,1)S(1)} %collective-permute-done.18.refs_0_.b1), channel_id=1, source_target_pairs={{0,1},{1,0},{2,3},{3,2},{4,5},{5,4},{6,7},{7,6},{8,9},{9,8},{10,11... | collective-permute-start | bytes 589832 | tf_op jit(solution)/shard_map/ppermute | solution.py:20
  56.7 0.0 collective-permute-start.25
  56.7 4.2 %collective-permute-done.16.own.b2 = bf16[768,128]{1,0:T(8,128)(2,1)S(1)} collective-permute-done((bf16[768,128]{1,0:T(8,128)(2,1)S(1)}, bf16[768,128]{1,0:T(8,128)(2,1)S(1)}, u32[]{:S(2)}, u32[]{:S(2)}) %collective-permute-start.16) | collective-permute-done | bytes 196640 | tf_op jit(solution)/shard_map/ppermute | solution.py:24
  60.9 1.2 %collective-permute-start.17 = (bf16[768,128]{1,0:T(8,128)(2,1)S(1)}, bf16[768,128]{1,0:T(8,128)(2,1)S(1)}, u32[]{:S(2)}, u32[]{:S(2)}) collective-permute-start(bf16[768,128]{1,0:T(8,128)(2,1)S(1)} %collective-permute-done.16.own.b2), channel_id=1, source_target_pairs={{0,1},{1,0},{2,3},{3,2},{4,5},{5,4},{6,7},{7,6},{8,9},{9,8},{10,11... | collective-permute-start | bytes 589832 | tf_op jit(solution)/shard_map/ppermute | solution.py:20
  62.1 2.6 %pages_side.1 = (f32[1024,128]{1,0:T(8,128)S(1)}, f32[1024,128]{1,0:T(8,128)S(1)}, f32[1024,128]{1,0:T(8,128)S(1)}) custom-call(bf16[4,256,128]{2,1,0:T(8,128)(2,1)S(1)} %get-tuple-element.34.queries, bf16[768,128]{1,0:T(8,128)(2,1)S(1)} %collective-permute-done.18.refs_0_.b1, bf16[768,128]{1,0:T(8,128)(2,1)S(1)} %collective-permute-done.24.refs_1_, ...), custom_call_target="tpu_custom_call" | custom-call | flops 805306368 | bytes 4194304 | tf_op jit(solution)/shard_map/pages_side/pallas_call | solution.py:410
  64.7 3.3 %pages_last.1 = (bf16[256,512]{1,0:T(8,128)(2,1)}, bf16[1024,128]{1,0:T(8,128)(2,1)}) custom-call(s32[8,8]{1,0:T(8,128)S(1)} %copy-done.5, s32[8,8]{1,0:T(8,128)S(1)} %copy-done.6, bf16[4,256,128]{2,1,0:T(8,128)(2,1)S(1)} %get-tuple-element.34.queries, bf16[768,128]{1,0:T(8,128)(2,1)S(1)} %collective-permute-done.16.own.b2, ...), custom_call_target="tpu_custom_call" | custom-call | flops 402653184 | bytes 4194304 | tf_op jit(solution)/shard_map/pages_last/pallas_call | solution.py:426
  (25 shorter events, 0.2 us)
Async XLA Ops:
  0.6 1.6 %copy-start = (bf16[8192,128]{1,0:T(8,128)(2,1)S(1)}, bf16[8192,128]{1,0:T(8,128)(2,1)}, u32[]{:S(2)}) copy-start(bf16[8192,128]{1,0:T(8,128)(2,1)} %refs_10_.1) | copy-start | bytes 6291460
  2.3 6.6 %copy-start.3 = (bf16[256,512]{1,0:T(8,128)(2,1)S(1)}, bf16[256,512]{1,0:T(8,128)(2,1)}, u32[]{:S(2)}) copy-start(bf16[256,512]{1,0:T(8,128)(2,1)} %queries.1) | copy-start | bytes 786436
  2.3 6.6 %copy-start.4 = (bf16[256,128]{1,0:T(8,128)(2,1)S(1)}, bf16[256,128]{1,0:T(8,128)(2,1)}, u32[]{:S(2)}) copy-start(bf16[256,128]{1,0:T(8,128)(2,1)} %turn_kv) | copy-start | bytes 196612
  2.3 6.9 %copy-start.2 = (bf16[3,128,512]{2,1,0:T(8,128)(2,1)S(1)}, bf16[3,128,512]{2,1,0:T(8,128)(2,1)}, u32[]{:S(2)}) copy-start(bf16[3,128,512]{2,1,0:T(8,128)(2,1)} %param.7) | copy-start | bytes 1179652
  2.4 11.3 %collective-permute-start.9 = (bf16[1024,128]{1,0:T(8,128)(2,1)S(1)}, bf16[1024,128]{1,0:T(8,128)(2,1)S(1)}, u32[]{:S(2)}, u32[]{:S(2)}) collective-permute-start(bf16[1024,128]{1,0:T(8,128)(2,1)S(1)} %get-tuple-element.37), channel_id=1, source_target_pairs={{0,66},{1,67},{2,64},{3,65},{4,70},{5,71},{6,68},{7,69},{8,74},{9,... | collective-permute-start | bytes 786440 | tf_op jit(solution)/shard_map/ppermute | solution.py:30
  9.2 4.5 %collective-permute-start.11 = (bf16[256,128]{1,0:T(8,128)(2,1)S(1)}, bf16[256,128]{1,0:T(8,128)(2,1)S(1)}, u32[]{:S(2)}, u32[]{:S(2)}) collective-permute-start(bf16[256,128]{1,0:T(8,128)(2,1)S(1)} %get-tuple-element.39), channel_id=1, source_target_pairs={{0,64},{16,80},{32,96},{48,112},{64,0},{80,16},{96,32},{112,48},{1... | collective-permute-start | bytes 196616 | tf_op jit(solution)/shard_map/ppermute | solution.py:24
  9.3 26.2 %copy-start.1 = (bf16[8192,128]{1,0:T(8,128)(2,1)S(1)}, bf16[8192,128]{1,0:T(8,128)(2,1)}, u32[]{:S(2)}) copy-start(bf16[8192,128]{1,0:T(8,128)(2,1)} %refs_10_.1) | copy-start | bytes 6291460
  9.3 12.3 %collective-permute-start.3 = (bf16[384,512]{1,0:T(8,128)(2,1)S(1)}, bf16[384,512]{1,0:T(8,128)(2,1)S(1)}, u32[]{:S(2)}, u32[]{:S(2)}) collective-permute-start(bf16[384,512]{1,0:T(8,128)(2,1)S(1)} %bitcast.1), channel_id=1, source_target_pairs={{0,12},{1,13},{2,14},{3,15},{4,8},{5,9},{6,10},{7,11},{8,4},{9,5},... | collective-permute-start | bytes 1179656 | tf_op jit(solution)/shard_map/ppermute | solution.py:20
  13.1 9.3 %collective-permute-start = (bf16[384,512]{1,0:T(8,128)(2,1)S(1)}, bf16[384,512]{1,0:T(8,128)(2,1)S(1)}, u32[]{:S(2)}, u32[]{:S(2)}) collective-permute-start(bf16[384,512]{1,0:T(8,128)(2,1)S(1)} %bitcast.2), channel_id=1, source_target_pairs={{0,4},{1,5},{2,6},{3,7},{4,0},{5,1},{6,2},{7,3},{8,12},{9,13},{10,... | collective-permute-start | bytes 1179656 | tf_op jit(solution)/shard_map/ppermute | solution.py:20
  13.1 13.4 %collective-permute-start.10 = (bf16[2,1024,128]{2,1,0:T(8,128)(2,1)S(1)}, bf16[2,1024,128]{2,1,0:T(8,128)(2,1)S(1)}, u32[]{:S(2)}, u32[]{:S(2)}) collective-permute-start(bf16[2,1024,128]{2,1,0:T(8,128)(2,1)S(1)} %get-tuple-element.38), channel_id=1, source_target_pairs={{0,66},{1,67},{2,64},{3,65},{4,70},{5,71},{6,68},{7,69},{8,74},{9,... | collective-permute-start | bytes 1572872 | tf_op jit(solution)/shard_map/ppermute | solution.py:30
  13.7 15.3 %collective-permute-start.12 = (bf16[1536,128]{1,0:T(8,128)(2,1)S(1)}, bf16[1536,128]{1,0:T(8,128)(2,1)S(1)}, u32[]{:S(2)}, u32[]{:S(2)}) collective-permute-start(bf16[1536,128]{1,0:T(8,128)(2,1)S(1)} %pad_maximum_fusion.2), channel_id=1, source_target_pairs={{0,16},{16,0},{32,48},{48,32},{64,80},{80,64},{96,112},{112,96},{1... | collective-permute-start | bytes 1179656 | tf_op jit(solution)/shard_map/ppermute | solution.py:24
  21.6 7.0 %collective-permute-start.7 = (bf16[192,512]{1,0:T(8,128)(2,1)S(1)}, bf16[192,512]{1,0:T(8,128)(2,1)S(1)}, u32[]{:S(2)}, u32[]{:S(2)}) collective-permute-start(bf16[192,512]{1,0:T(8,128)(2,1)S(1)} %slice.33), channel_id=1, source_target_pairs={{0,4},{1,5},{2,6},{3,7},{4,0},{5,1},{6,2},{7,3},{8,12},{9,13},{10,... | collective-permute-start | bytes 589832 | tf_op jit(solution)/shard_map/ppermute | solution.py:20
  22.5 6.8 %collective-permute-start.5 = (bf16[192,512]{1,0:T(8,128)(2,1)S(1)}, bf16[192,512]{1,0:T(8,128)(2,1)S(1)}, u32[]{:S(2)}, u32[]{:S(2)}) collective-permute-start(bf16[192,512]{1,0:T(8,128)(2,1)S(1)} %slice.32), channel_id=1, source_target_pairs={{0,12},{1,13},{2,14},{3,15},{4,8},{5,9},{6,10},{7,11},{8,4},{9,5},... | collective-permute-start | bytes 589832 | tf_op jit(solution)/shard_map/ppermute | solution.py:20
  24.2 11.3 %collective-permute-start.1 = (bf16[384,512]{1,0:T(8,128)(2,1)S(1)}, bf16[384,512]{1,0:T(8,128)(2,1)S(1)}, u32[]{:S(2)}, u32[]{:S(2)}) collective-permute-start(bf16[384,512]{1,0:T(8,128)(2,1)S(1)} %bitcast.3), channel_id=1, source_target_pairs={{0,1},{1,0},{2,3},{3,2},{4,5},{5,4},{6,7},{7,6},{8,9},{9,8},{10,11... | collective-permute-start | bytes 1179656 | tf_op jit(solution)/shard_map/ppermute | solution.py:20
  26.5 8.1 %collective-permute-start.4 = (bf16[384,512]{1,0:T(8,128)(2,1)S(1)}, bf16[384,512]{1,0:T(8,128)(2,1)S(1)}, u32[]{:S(2)}, u32[]{:S(2)}) collective-permute-start(bf16[384,512]{1,0:T(8,128)(2,1)S(1)} %collective-permute-done.3.refs_4_), channel_id=1, source_target_pairs={{0,1},{1,0},{2,3},{3,2},{4,5},{5,4},{6,7},{7,6},{8,9},{9,8},{10,11... | collective-permute-start | bytes 1179656 | tf_op jit(solution)/shard_map/ppermute | solution.py:20
  28.7 3.1 %collective-permute-start.8 = (bf16[192,512]{1,0:T(8,128)(2,1)S(1)}, bf16[192,512]{1,0:T(8,128)(2,1)S(1)}, u32[]{:S(2)}, u32[]{:S(2)}) collective-permute-start(bf16[192,512]{1,0:T(8,128)(2,1)S(1)} %collective-permute-done.7.refs_8_), channel_id=1, source_target_pairs={{0,1},{1,0},{2,3},{3,2},{4,5},{5,4},{6,7},{7,6},{8,9},{9,8},{10,11... | collective-permute-start | bytes 589832 | tf_op jit(solution)/shard_map/ppermute | solution.py:20
  29.0 6.4 %collective-permute-start.2 = (bf16[384,512]{1,0:T(8,128)(2,1)S(1)}, bf16[384,512]{1,0:T(8,128)(2,1)S(1)}, u32[]{:S(2)}, u32[]{:S(2)}) collective-permute-start(bf16[384,512]{1,0:T(8,128)(2,1)S(1)} %collective-permute-done.refs_2_), channel_id=1, source_target_pairs={{0,1},{1,0},{2,3},{3,2},{4,5},{5,4},{6,7},{7,6},{8,9},{9,8},{10,11... | collective-permute-start | bytes 1179656 | tf_op jit(solution)/shard_map/ppermute | solution.py:20
  29.2 12.7 %collective-permute-start.21 = (bf16[1024,128]{1,0:T(8,128)(2,1)S(1)}, bf16[1024,128]{1,0:T(8,128)(2,1)S(1)}, u32[]{:S(2)}, u32[]{:S(2)}) collective-permute-start(bf16[1024,128]{1,0:T(8,128)(2,1)S(1)} %pad_maximum_fusion.3.near), channel_id=1, source_target_pairs={{0,48},{16,32},{32,16},{48,0},{64,112},{80,96},{96,80},{112,64},{1... | collective-permute-start | bytes 786440 | tf_op jit(solution)/shard_map/ppermute | solution.py:24
  31.8 3.7 %collective-permute-start.6 = (bf16[192,512]{1,0:T(8,128)(2,1)S(1)}, bf16[192,512]{1,0:T(8,128)(2,1)S(1)}, u32[]{:S(2)}, u32[]{:S(2)}) collective-permute-start(bf16[192,512]{1,0:T(8,128)(2,1)S(1)} %collective-permute-done.5.refs_6_), channel_id=1, source_target_pairs={{0,1},{1,0},{2,3},{3,2},{4,5},{5,4},{6,7},{7,6},{8,9},{9,8},{10,11... | collective-permute-start | bytes 589832 | tf_op jit(solution)/shard_map/ppermute | solution.py:20
  34.6 18.9 %collective-permute-start.22 = (bf16[1024,128]{1,0:T(8,128)(2,1)S(1)}, bf16[1024,128]{1,0:T(8,128)(2,1)S(1)}, u32[]{:S(2)}, u32[]{:S(2)}) collective-permute-start(bf16[1024,128]{1,0:T(8,128)(2,1)S(1)} %pad_maximum_fusion.3.near), channel_id=1, source_target_pairs={{0,1},{1,0},{2,3},{3,2},{4,5},{5,4},{6,7},{7,6},{8,9},{9,8},{10,11... | collective-permute-start | bytes 786440 | tf_op jit(solution)/shard_map/ppermute | solution.py:20
  38.6 8.1 %collective-permute-start.15 = (bf16[384,128]{1,0:T(8,128)(2,1)S(1)}, bf16[384,128]{1,0:T(8,128)(2,1)S(1)}, u32[]{:S(2)}, u32[]{:S(2)}) collective-permute-start(bf16[384,128]{1,0:T(8,128)(2,1)S(1)} %get-tuple-element.41), channel_id=1, source_target_pairs={{0,66},{1,67},{2,64},{3,65},{4,70},{5,71},{6,68},{7,69},{8,74},{9,... | collective-permute-start | bytes 294920 | tf_op jit(solution)/shard_map/ppermute | solution.py:30
  39.3 7.4 %collective-permute-start.13 = (bf16[384,128]{1,0:T(8,128)(2,1)S(1)}, bf16[384,128]{1,0:T(8,128)(2,1)S(1)}, u32[]{:S(2)}, u32[]{:S(2)}) collective-permute-start(bf16[384,128]{1,0:T(8,128)(2,1)S(1)} %get-tuple-element.41), channel_id=1, source_target_pairs={{0,2},{1,3},{2,0},{3,1},{4,6},{5,7},{6,4},{7,5},{8,10},{9,11},{10,... | collective-permute-start | bytes 294920 | tf_op jit(solution)/shard_map/ppermute | solution.py:20
  41.9 4.8 %collective-permute-start.14 = (bf16[384,128]{1,0:T(8,128)(2,1)S(1)}, bf16[384,128]{1,0:T(8,128)(2,1)S(1)}, u32[]{:S(2)}, u32[]{:S(2)}) collective-permute-start(bf16[384,128]{1,0:T(8,128)(2,1)S(1)} %get-tuple-element.42), channel_id=1, source_target_pairs={{0,64},{16,80},{32,96},{48,112},{64,0},{80,16},{96,32},{112,48},{1... | collective-permute-start | bytes 294920 | tf_op jit(solution)/shard_map/ppermute | solution.py:24
  42.0 11.5 %collective-permute-start.23 = (bf16[1024,128]{1,0:T(8,128)(2,1)S(1)}, bf16[1024,128]{1,0:T(8,128)(2,1)S(1)}, u32[]{:S(2)}, u32[]{:S(2)}) collective-permute-start(bf16[1024,128]{1,0:T(8,128)(2,1)S(1)} %collective-permute-done.21.far), channel_id=1, source_target_pairs={{0,1},{1,0},{2,3},{3,2},{4,5},{5,4},{6,7},{7,6},{8,9},{9,8},{10,11... | collective-permute-start | bytes 786440 | tf_op jit(solution)/shard_map/ppermute | solution.py:20
  46.9 2.3 %collective-permute-start.20 = (bf16[768,128]{1,0:T(8,128)(2,1)S(1)}, bf16[768,128]{1,0:T(8,128)(2,1)S(1)}, u32[]{:S(2)}, u32[]{:S(2)}) collective-permute-start(bf16[768,128]{1,0:T(8,128)(2,1)S(1)} %finish.1.refs_0_.b0), channel_id=1, source_target_pairs={{0,1},{1,0},{2,3},{3,2},{4,5},{5,4},{6,7},{7,6},{8,9},{9,8},{10,11... | collective-permute-start | bytes 589832 | tf_op jit(solution)/shard_map/ppermute | solution.py:20
  48.1 7.7 %collective-permute-start.19 = (bf16[768,128]{1,0:T(8,128)(2,1)S(1)}, bf16[768,128]{1,0:T(8,128)(2,1)S(1)}, u32[]{:S(2)}, u32[]{:S(2)}) collective-permute-start(bf16[768,128]{1,0:T(8,128)(2,1)S(1)} %finish.1.refs_0_.b0), channel_id=1, source_target_pairs={{0,48},{16,32},{32,16},{48,0},{64,112},{80,96},{96,80},{112,64},{1... | collective-permute-start | bytes 589832 | tf_op jit(solution)/shard_map/ppermute | solution.py:24
  48.3 7.5 %collective-permute-start.18 = (bf16[768,128]{1,0:T(8,128)(2,1)S(1)}, bf16[768,128]{1,0:T(8,128)(2,1)S(1)}, u32[]{:S(2)}, u32[]{:S(2)}) collective-permute-start(bf16[768,128]{1,0:T(8,128)(2,1)S(1)} %finish.1.refs_0_.b0), channel_id=1, source_target_pairs={{0,16},{16,0},{32,48},{48,32},{64,80},{80,64},{96,112},{112,96},{1... | collective-permute-start | bytes 589832 | tf_op jit(solution)/shard_map/ppermute | solution.py:24
  49.2 11.7 %collective-permute-start.16 = (bf16[768,128]{1,0:T(8,128)(2,1)S(1)}, bf16[768,128]{1,0:T(8,128)(2,1)S(1)}, u32[]{:S(2)}, u32[]{:S(2)}) collective-permute-start(bf16[768,128]{1,0:T(8,128)(2,1)S(1)} %finish.1.refs_0_.b0), channel_id=1, source_target_pairs={{0,32},{16,48},{32,0},{48,16},{64,96},{80,112},{96,64},{112,80},{1... | collective-permute-start | bytes 589832 | tf_op jit(solution)/shard_map/ppermute | solution.py:24
  54.3 10.4 %copy-start.5 = (s32[8,8]{1,0:T(8,128)S(1)}, s32[8,8]{1,0:T(8,128)}, u32[]{:S(2)}) copy-start(s32[8,8]{1,0:T(8,128)} %page_table.1) | copy-start | bytes 772
  54.3 10.4 %copy-start.6 = (s32[8,8]{1,0:T(8,128)S(1)}, s32[8,8]{1,0:T(8,128)}, u32[]{:S(2)}) copy-start(s32[8,8]{1,0:T(8,128)} %page_counts.1) | copy-start | bytes 772
  55.8 6.3 %collective-permute-start.24 = (bf16[768,128]{1,0:T(8,128)(2,1)S(1)}, bf16[768,128]{1,0:T(8,128)(2,1)S(1)}, u32[]{:S(2)}, u32[]{:S(2)}) collective-permute-start(bf16[768,128]{1,0:T(8,128)(2,1)S(1)} %collective-permute-done.18.refs_0_.b1), channel_id=1, source_target_pairs={{0,1},{1,0},{2,3},{3,2},{4,5},{5,4},{6,7},{7,6},{8,9},{9,8},{10,11... | collective-permute-start | bytes 589832 | tf_op jit(solution)/shard_map/ppermute | solution.py:20
  56.7 5.4 %collective-permute-start.25 = (bf16[768,128]{1,0:T(8,128)(2,1)S(1)}, bf16[768,128]{1,0:T(8,128)(2,1)S(1)}, u32[]{:S(2)}, u32[]{:S(2)}) collective-permute-start(bf16[768,128]{1,0:T(8,128)(2,1)S(1)} %collective-permute-done.19.refs_2_.b3), channel_id=1, source_target_pairs={{0,1},{1,0},{2,3},{3,2},{4,5},{5,4},{6,7},{7,6},{8,9},{9,8},{10,11... | collective-permute-start | bytes 589832 | tf_op jit(solution)/shard_map/ppermute | solution.py:20
  60.9 3.8 %collective-permute-start.17 = (bf16[768,128]{1,0:T(8,128)(2,1)S(1)}, bf16[768,128]{1,0:T(8,128)(2,1)S(1)}, u32[]{:S(2)}, u32[]{:S(2)}) collective-permute-start(bf16[768,128]{1,0:T(8,128)(2,1)S(1)} %collective-permute-done.16.own.b2), channel_id=1, source_target_pairs={{0,1},{1,0},{2,3},{3,2},{4,5},{5,4},{6,7},{7,6},{8,9},{9,8},{10,11... | collective-permute-start | bytes 589832 | tf_op jit(solution)/shard_map/ppermute | solution.py:20

commit v6 on v5

--- a/solution.py
+++ b/solution.py
@@ -244,11 +244,22 @@
     pl.when(core == 1)(lambda: attend(1))
 
 
+def merged(state, others):
+    top, total, acc = state
+    most = jnp.maximum(top, others[0][...])
+    scale = jnp.exp2((top - most) * SCORE_SCALE)
+    other_scale = jnp.exp2((others[0][...] - most) * SCORE_SCALE)
+    total = total * scale + others[1][...] * other_scale
+    return most, total, acc * scale + others[2][...] * other_scale
+
+
 def pages_kernel(count, queries, *refs):
     pairs = [refs[2 * i : 2 * i + 2] for i in range(count)]
-    state_in, state_out = refs[2 * count : -3], refs[-3:]
+    state_in, others, state_out = refs[2 * count : -3][:3], refs[2 * count : -3][3:], refs[-3:]
 
     def done(state):
+        if others:
+            state = merged(state, others)
         for ref, value in zip(state_out, state):
             ref[...] = value
 
@@ -256,8 +267,8 @@
 
 
 def last_kernel(
-    page_table, page_counts, queries, own, other, top_in, total_in, acc_in,
-    turn_top, turn_total, turn_acc, b0, b1, b3, b2, out, cache_out, zero_buf, sems,
+    page_table, page_counts, queries, own, other, top_in, total_in, acc_in, b0, b1, b3, b2,
+    out, cache_out, zero_buf, sems,
 ):
     ctx = lax.axis_index("ctx")
     heads, rows, _ = queries.shape
@@ -284,13 +295,7 @@
             waits.append(pltpu.make_async_copy(zero_buf, place, sem))
 
     def done(state):
-        top, total, acc = state
-        most = jnp.maximum(top, turn_top[...])
-        scale = jnp.exp2((top - most) * SCORE_SCALE)
-        turn_scale = jnp.exp2((turn_top[...] - most) * SCORE_SCALE)
-        total = total * scale + turn_total[...] * turn_scale
-        acc = acc * scale + turn_acc[...] * turn_scale
-        result = acc / jnp.sum(total, axis=1, keepdims=True)
+        result = state[2] * (1.0 / jnp.sum(state[1], axis=1, keepdims=True))
         result = result.astype(jnp.bfloat16)
         for head in range(heads):
             out[:, head * HEAD_DIM : (head + 1) * HEAD_DIM] = result[head * rows : (head + 1) * rows]
@@ -344,9 +349,8 @@
         name="prepare",
     )(queries, turn_kv, cosine[:tok_new], sine[:tok_new])
     turn_pair = jnp.concatenate([turn_block, shifted(turn_block, 4)])
-    carried = shifted(jnp.concatenate([first, turn_pair]), 1)
-    relayed = carried[: 2 * width]
-    turn_near = jnp.concatenate([turn_pair, carried[2 * width :]])
+    relayed = shifted(first, 1)
+    turn_near = jnp.concatenate([turn_pair, shifted(turn_pair, 1)])
 
     x1 = swapped(own_x, 4)
     x3 = swapped(own_x, 12)
@@ -373,6 +377,7 @@
         compiler_params=params,
         name="project",
     )(*pieces, kv_weight, first, rest, relayed)
+    turn_near, far_part = lax.optimization_barrier((turn_near, far_part))
     turn_far = shifted(turn_near, 3)
     got1 = swapped(far_part, 2)
     got2 = shifted(near_part, 4)
@@ -421,15 +426,15 @@
     blocks[1], blocks[2], state, turn_state = lax.optimization_barrier(
         (blocks[1], blocks[2], state, turn_state)
     )
-    pairs = [(block, swapped(block, 1)) for block in blocks[1:]]
-    state = attend_more("pages_side", pairs[:2], state)
+    pairs = [(block, swapped(block, 1)) for block in blocks[1:3]]
+    state = attend_more("pages_side", pairs, (*state, *turn_state))
     attended, cache = pl.pallas_call(
         last_kernel,
         out_shape=(
             jax.ShapeDtypeStruct((tok_new, heads_dev * HEAD_DIM), bf16),
             jax.ShapeDtypeStruct((SOURCES * PAGE, HEAD_DIM), bf16),
         ),
-        in_specs=[smem_spec(), smem_spec()] + [vmem_spec()] * 9 + [any_spec()] * 4,
+        in_specs=[smem_spec(), smem_spec()] + [vmem_spec()] * 6 + [any_spec()] * 4,
         out_specs=(vmem_spec(), any_spec()),
         scratch_shapes=[
             pltpu.VMEM((PAGE, HEAD_DIM), bf16),
@@ -438,7 +443,7 @@
         compiler_params=params,
         cost_estimate=cost(2 * rows),
         name="pages_last",
-    )(page_table, page_counts, query_heads, *pairs[2], *state, *turn_state, *blocks)
+    )(page_table, page_counts, query_heads, blocks[3], swapped(blocks[3], 1), *state, *blocks)
     return (attended, cache)
 
 

time: 68.3 us -> 67.6 us (0.990)
  waiting for transfers between devices: 18.2 us -> 15.4 us
  starting transfers between devices: 32.1 us -> 34.8 us
    ppermute x16, waiting for transfers between devices: 9.03 us -> 1.93 us  [swapped(): lax.ppermute(value, 'tp', [(i, i ^ bits) for i in range(lax.axis_size('tp...]
    ppermute x7 -> x8, waiting for transfers between devices: 9.09 us -> 11.3 us  [shifted(): lax.ppermute(value, 'ctx', [(i, i ^ bits) for i in range(lax.axis_size('c...]
    ppermute x3, waiting for transfers between devices: 0.12 us -> 2.1 us  [across(): lax.ppermute(value, ('ctx', 'tp'), [(i, i ^ flip) for i in range(peers)])]
    ppermute x7 -> x8, starting transfers between devices: 7 us -> 8.96 us  [shifted(): lax.ppermute(value, 'ctx', [(i, i ^ bits) for i in range(lax.axis_size('c...]
    ppermute x3, starting transfers between devices: 4.83 us -> 5.72 us  [across(): lax.ppermute(value, ('ctx', 'tp'), [(i, i ^ flip) for i in range(peers)])]
  transfers between devices with their start and end apart: 26 -> 27, of which waited for: 8 -> 10; matrix products, arithmetic and copies ran while one was open for 5% -> 5% of each run, Pallas kernels for 12% -> 8%
where the time goes in v6:
time: 67.6 us; the launch traced here: 67.4 us
  starting transfers between devices  34.8 us (51%)
  waiting for transfers between devices  15.4 us (23%)
  Pallas kernels  11.3 us (17%)
  other arithmetic  2.5 us (4%)
  local copies, waits for them, and re-layouts  2.41 us (4%)
  between operations  1.04 us (2%)
    ppermute x16, starting transfers between devices, swapped(): lax.ppermute(value, 'tp', [(i, i ^ bits) for i in range(lax.axis_size('tp...  20.1 us
    ppermute x8, waiting for transfers between devices, shifted(): lax.ppermute(value, 'ctx', [(i, i ^ bits) for i in range(lax.axis_size('c...  11.3 us
    ppermute x8, starting transfers between devices, shifted(): lax.ppermute(value, 'ctx', [(i, i ^ bits) for i in range(lax.axis_size('c...  8.96 us
    ppermute x3, starting transfers between devices, across(): lax.ppermute(value, ('ctx', 'tp'), [(i, i ^ flip) for i in range(peers)])  5.72 us
    pallas_call x2, Pallas kernels, attend_more(): pl.pallas_call(functools.partial(pages_kernel, len(group)), out_shape=sta...  3.91 us
    pallas_call x1, Pallas kernels, local(): pl.pallas_call(project_kernel, out_shape=(jax.ShapeDtypeStruct((rows, HEA...  3.15 us
    pallas_call x1, Pallas kernels, local(): pl.pallas_call(last_kernel, out_shape=(jax.ShapeDtypeStruct((tok_new, hea...  3.04 us
    ppermute x3, waiting for transfers between devices, across(): lax.ppermute(value, ('ctx', 'tp'), [(i, i ^ flip) for i in range(peers)])  2.1 us
  transfers between devices with their start and end apart: 27, of which 10 were waited for; matrix products, arithmetic and copies ran while one was open for 5% of the time, Pallas kernels for 8%

profile of v6, /device:TPU:1, one launch (start us, length us, event | category | flops | bytes accessed | tf_op | source)
XLA Modules:
  0.0 67.4 jit_solution(5534755927351698932)
XLA Ops:
  0.6 4.7 %collective-permute-start.3 = (bf16[384,512]{1,0:T(8,128)(2,1)}, bf16[384,512]{1,0:T(8,128)(2,1)S(1)}, u32[]{:S(2)}, u32[]{:S(2)}) collective-permute-start(bf16[384,512]{1,0:T(8,128)(2,1)} %bitcast.1), channel_id=1, source_target_pairs={{0,12},{1,13},{2,14},{3,15},{4,8},{5,9},{6,10},{7,11},{8,4},{9,5},... | collective-permute-start | bytes 1179656 | tf_op jit(solution)/shard_map/ppermute | solution.py:20
  5.3 0.0 collective-permute-start
  5.3 1.6 %copy-done = bf16[8192,128]{1,0:T(8,128)(2,1)S(1)} copy-done((bf16[8192,128]{1,0:T(8,128)(2,1)S(1)}, bf16[8192,128]{1,0:T(8,128)(2,1)}, u32[]{:S(2)}) %copy-start) | copy-done | bytes 2097176
  6.9 0.1 pick.1
  7.0 0.0 copy-start.3
  7.0 0.0 copy-start.4
  7.0 2.8 %collective-permute-start.9 = (bf16[1024,128]{1,0:T(8,128)(2,1)S(1)}, bf16[1024,128]{1,0:T(8,128)(2,1)S(1)}, u32[]{:S(2)}, u32[]{:S(2)}) collective-permute-start(bf16[1024,128]{1,0:T(8,128)(2,1)S(1)} %get-tuple-element.39), channel_id=1, source_target_pairs={{0,66},{1,67},{2,64},{3,65},{4,70},{5,71},{6,68},{7,69},{8,74},{9,... | collective-permute-start | bytes 786440 | tf_op jit(solution)/shard_map/ppermute | solution.py:30
  9.8 0.1 collective-permute-start.10
  9.9 0.8 %dynamic_slice.3 = s32[256]{0:T(256)S(1)} dynamic-slice(s32[2048]{0:T(1024)} %param.13, s32[]{:T(128)S(6)} %select_n.18), dynamic_slice_sizes={256} | dynamic-slice | bytes 2052 | tf_op jit(solution)/shard_map/dynamic_slice | solution.py:335
  10.7 1.9 %fusion = (f32[1024,64]{1,0:T(8,128)S(1)}, f32[1024,64]{1,0:T(8,128)S(1)}, f32[1024,64]{1,0:T(8,128)S(1)}) fusion(f32[64]{0:T(128)S(1)} %compare_select_fusion.1, f32[1024]{0:T(1024)S(1)} %add_convert_fusion), kind=kLoop, calls=%fused_computation.5 | loop fusion | flops 131072 | bytes 790784 | tf_op jit(solution)/shard_map/neg | solution.py:51
  12.6 0.0 copy-start.2
  12.6 0.0 copy-start.1
  12.7 0.1 pad_maximum_fusion.4.cosine
  12.8 0.1 pad_maximum_fusion.3.sine
  12.9 0.2 prepare.1
  13.1 0.1 collective-permute-start.12
  13.2 2.1 %collective-permute-done.9.refs_11_ = bf16[1024,128]{1,0:T(8,128)(2,1)S(1)} collective-permute-done((bf16[1024,128]{1,0:T(8,128)(2,1)S(1)}, bf16[1024,128]{1,0:T(8,128)(2,1)S(1)}, u32[]{:S(2)}, u32[]{:S(2)}) %collective-permute-start.9) | collective-permute-done | bytes 262176 | tf_op jit(solution)/shard_map/ppermute | solution.py:30
  15.3 1.2 %collective-permute-start.11 = (bf16[1024,128]{1,0:T(8,128)(2,1)S(1)}, bf16[1024,128]{1,0:T(8,128)(2,1)S(1)}, u32[]{:S(2)}, u32[]{:S(2)}) collective-permute-start(bf16[1024,128]{1,0:T(8,128)(2,1)S(1)} %collective-permute-done.9.refs_11_), channel_id=1, source_target_pairs={{0,16},{16,0},{32,48},{48,32},{64,80},{80,64},{96,112},{112,96},{1... | collective-permute-start | bytes 786440 | tf_op jit(solution)/shard_map/ppermute | solution.py:24
  16.5 0.1 collective-permute-done.12
  16.6 1.3 %collective-permute-start.13 = (bf16[512,128]{1,0:T(8,128)(2,1)S(1)}, bf16[512,128]{1,0:T(8,128)(2,1)S(1)}, u32[]{:S(2)}, u32[]{:S(2)}) collective-permute-start(bf16[512,128]{1,0:T(8,128)(2,1)S(1)} %pad_maximum_fusion.5), channel_id=1, source_target_pairs={{0,16},{16,0},{32,48},{48,32},{64,80},{80,64},{96,112},{112,96},{1... | collective-permute-start | bytes 393224 | tf_op jit(solution)/shard_map/ppermute | solution.py:24
  17.9 0.0 collective-permute-done.3.refs_4_
  17.9 1.5 %collective-permute-start.7 = (bf16[192,512]{1,0:T(8,128)(2,1)S(1)}, bf16[192,512]{1,0:T(8,128)(2,1)S(1)}, u32[]{:S(2)}, u32[]{:S(2)}) collective-permute-start(bf16[192,512]{1,0:T(8,128)(2,1)S(1)} %slice.25), channel_id=1, source_target_pairs={{0,4},{1,5},{2,6},{3,7},{4,0},{5,1},{6,2},{7,3},{8,12},{9,13},{10,... | collective-permute-start | bytes 589832 | tf_op jit(solution)/shard_map/ppermute | solution.py:20
  19.5 0.0 collective-permute-done.refs_2_
  19.5 0.2 collective-permute-start.5
  19.6 3.0 %collective-permute-done.13 = bf16[512,128]{1,0:T(8,128)(2,1)S(1)} collective-permute-done((bf16[512,128]{1,0:T(8,128)(2,1)S(1)}, bf16[512,128]{1,0:T(8,128)(2,1)S(1)}, u32[]{:S(2)}, u32[]{:S(2)}) %collective-permute-start.13) | collective-permute-done | bytes 131104 | tf_op jit(solution)/shard_map/ppermute | solution.py:24
  22.7 4.1 %collective-permute-start.1 = (bf16[384,512]{1,0:T(8,128)(2,1)S(1)}, bf16[384,512]{1,0:T(8,128)(2,1)S(1)}, u32[]{:S(2)}, u32[]{:S(2)}) collective-permute-start(bf16[384,512]{1,0:T(8,128)(2,1)S(1)} %bitcast.3), channel_id=1, source_target_pairs={{0,1},{1,0},{2,3},{3,2},{4,5},{5,4},{6,7},{7,6},{8,9},{9,8},{10,11... | collective-permute-start | bytes 1179656 | tf_op jit(solution)/shard_map/ppermute | solution.py:20
  26.8 0.0 collective-permute-done.11.refs_13_
  26.8 0.1 collective-permute-start.4
  26.9 0.0 collective-permute-done.10.refs_12_
  26.9 1.4 %collective-permute-start.2 = (bf16[384,512]{1,0:T(8,128)(2,1)S(1)}, bf16[384,512]{1,0:T(8,128)(2,1)S(1)}, u32[]{:S(2)}, u32[]{:S(2)}) collective-permute-start(bf16[384,512]{1,0:T(8,128)(2,1)S(1)} %collective-permute-done.refs_2_), channel_id=1, source_target_pairs={{0,1},{1,0},{2,3},{3,2},{4,5},{5,4},{6,7},{7,6},{8,9},{9,8},{10,11... | collective-permute-start | bytes 1179656 | tf_op jit(solution)/shard_map/ppermute | solution.py:20
  28.3 0.0 collective-permute-done.7.refs_8_
  28.3 0.0 collective-permute-start.8
  28.3 0.0 collective-permute-done.5.refs_6_
  28.3 1.4 %collective-permute-start.6 = (bf16[192,512]{1,0:T(8,128)(2,1)S(1)}, bf16[192,512]{1,0:T(8,128)(2,1)S(1)}, u32[]{:S(2)}, u32[]{:S(2)}) collective-permute-start(bf16[192,512]{1,0:T(8,128)(2,1)S(1)} %collective-permute-done.5.refs_6_), channel_id=1, source_target_pairs={{0,1},{1,0},{2,3},{3,2},{4,5},{5,4},{6,7},{7,6},{8,9},{9,8},{10,11... | collective-permute-start | bytes 589832 | tf_op jit(solution)/shard_map/ppermute | solution.py:20
  29.7 0.2 collective-permute-done.8.refs_9_
  29.9 0.0 collective-permute-done.4.refs_5_
  30.0 0.8 %collective-permute-done.6.refs_7_ = bf16[192,512]{1,0:T(8,128)(2,1)S(1)} collective-permute-done((bf16[192,512]{1,0:T(8,128)(2,1)S(1)}, bf16[192,512]{1,0:T(8,128)(2,1)S(1)}, u32[]{:S(2)}, u32[]{:S(2)}) %collective-permute-start.6) | collective-permute-done | bytes 196640 | tf_op jit(solution)/shard_map/ppermute | solution.py:20
  30.8 0.0 collective-permute-done.1.refs_1_
  30.8 0.0 collective-permute-done.2.refs_3_
  30.8 3.1 %project.1 = (f32[384,128]{1,0:T(8,128)S(1)}, bf16[384,128]{1,0:T(8,128)(2,1)S(1)}, bf16[384,128]{1,0:T(8,128)(2,1)S(1)}) custom-call(bf16[384,512]{1,0:T(8,128)(2,1)S(1)} %bitcast.4, bf16[384,512]{1,0:T(8,128)(2,1)S(1)} %collective-permute-done.1.refs_1_, bf16[384,512]{1,0:T(8,128)(2,1)S(1)} %collective-permute-done.refs_2_, ...), custom_call_target="tpu_custom_call" | custom-call | tf_op jit(solution)/shard_map/project/pallas_call | solution.py:367
  34.0 2.6 %collective-permute-start.22 = (bf16[1024,128]{1,0:T(8,128)(2,1)S(1)}, bf16[1024,128]{1,0:T(8,128)(2,1)S(1)}, u32[]{:S(2)}, u32[]{:S(2)}) collective-permute-start(bf16[1024,128]{1,0:T(8,128)(2,1)S(1)} %pad_maximum_fusion.2.near), channel_id=1, source_target_pairs={{0,48},{16,32},{32,16},{48,0},{64,112},{80,96},{96,80},{112,64},{1... | collective-permute-start | bytes 786440 | tf_op jit(solution)/shard_map/ppermute | solution.py:24
  36.5 0.2 pad_maximum_fusion.sine
  36.7 2.8 %collective-permute-start.16 = (bf16[384,128]{1,0:T(8,128)(2,1)S(1)}, bf16[384,128]{1,0:T(8,128)(2,1)S(1)}, u32[]{:S(2)}, u32[]{:S(2)}) collective-permute-start(bf16[384,128]{1,0:T(8,128)(2,1)S(1)} %get-tuple-element.44), channel_id=1, source_target_pairs={{0,66},{1,67},{2,64},{3,65},{4,70},{5,71},{6,68},{7,69},{8,74},{9,... | collective-permute-start | bytes 294920 | tf_op jit(solution)/shard_map/ppermute | solution.py:30
  39.5 0.0 collective-permute-start.14
  39.5 0.9 %collective-permute-start.23 = (bf16[1024,128]{1,0:T(8,128)(2,1)S(1)}, bf16[1024,128]{1,0:T(8,128)(2,1)S(1)}, u32[]{:S(2)}, u32[]{:S(2)}) collective-permute-start(bf16[1024,128]{1,0:T(8,128)(2,1)S(1)} %pad_maximum_fusion.2.near), channel_id=1, source_target_pairs={{0,1},{1,0},{2,3},{3,2},{4,5},{5,4},{6,7},{7,6},{8,9},{9,8},{10,11... | collective-permute-start | bytes 786440 | tf_op jit(solution)/shard_map/ppermute | solution.py:20
  40.4 0.8 %collective-permute-start.15 = (bf16[384,128]{1,0:T(8,128)(2,1)S(1)}, bf16[384,128]{1,0:T(8,128)(2,1)S(1)}, u32[]{:S(2)}, u32[]{:S(2)}) collective-permute-start(bf16[384,128]{1,0:T(8,128)(2,1)S(1)} %get-tuple-element.45), channel_id=1, source_target_pairs={{0,64},{16,80},{32,96},{48,112},{64,0},{80,16},{96,32},{112,48},{1... | collective-permute-start | bytes 294920 | tf_op jit(solution)/shard_map/ppermute | solution.py:24
  41.2 1.5 %collective-permute-done.22.far = bf16[1024,128]{1,0:T(8,128)(2,1)S(1)} collective-permute-done((bf16[1024,128]{1,0:T(8,128)(2,1)S(1)}, bf16[1024,128]{1,0:T(8,128)(2,1)S(1)}, u32[]{:S(2)}, u32[]{:S(2)}) %collective-permute-start.22) | collective-permute-done | bytes 262176 | tf_op jit(solution)/shard_map/ppermute | solution.py:24
  42.8 1.2 %collective-permute-start.24 = (bf16[1024,128]{1,0:T(8,128)(2,1)S(1)}, bf16[1024,128]{1,0:T(8,128)(2,1)S(1)}, u32[]{:S(2)}, u32[]{:S(2)}) collective-permute-start(bf16[1024,128]{1,0:T(8,128)(2,1)S(1)} %collective-permute-done.22.far), channel_id=1, source_target_pairs={{0,1},{1,0},{2,3},{3,2},{4,5},{5,4},{6,7},{7,6},{8,9},{9,8},{10,11... | collective-permute-start | bytes 786440 | tf_op jit(solution)/shard_map/ppermute | solution.py:20
  44.0 0.2 pad_maximum_fusion.1.cosine
  44.2 1.0 %collective-permute-done.15.p2 = bf16[384,128]{1,0:T(8,128)(2,1)S(1)} collective-permute-done((bf16[384,128]{1,0:T(8,128)(2,1)S(1)}, bf16[384,128]{1,0:T(8,128)(2,1)S(1)}, u32[]{:S(2)}, u32[]{:S(2)}) %collective-permute-start.15) | collective-permute-done | bytes 98336 | tf_op jit(solution)/shard_map/ppermute | solution.py:24
  45.2 0.2 finish.1.refs_0_.b0
  45.4 2.3 %collective-permute-start.21 = (bf16[768,128]{1,0:T(8,128)(2,1)S(1)}, bf16[768,128]{1,0:T(8,128)(2,1)S(1)}, u32[]{:S(2)}, u32[]{:S(2)}) collective-permute-start(bf16[768,128]{1,0:T(8,128)(2,1)S(1)} %finish.1.refs_0_.b0), channel_id=1, source_target_pairs={{0,1},{1,0},{2,3},{3,2},{4,5},{5,4},{6,7},{7,6},{8,9},{9,8},{10,11... | collective-permute-start | bytes 589832 | tf_op jit(solution)/shard_map/ppermute | solution.py:20
  47.7 0.2 collective-permute-start.20
  47.9 0.9 %collective-permute-done.21.refs_1_ = bf16[768,128]{1,0:T(8,128)(2,1)S(1)} collective-permute-done((bf16[768,128]{1,0:T(8,128)(2,1)S(1)}, bf16[768,128]{1,0:T(8,128)(2,1)S(1)}, u32[]{:S(2)}, u32[]{:S(2)}) %collective-permute-start.21) | collective-permute-done | bytes 196640 | tf_op jit(solution)/shard_map/ppermute | solution.py:20
  48.8 2.8 %collective-permute-start.17 = (bf16[768,128]{1,0:T(8,128)(2,1)S(1)}, bf16[768,128]{1,0:T(8,128)(2,1)S(1)}, u32[]{:S(2)}, u32[]{:S(2)}) collective-permute-start(bf16[768,128]{1,0:T(8,128)(2,1)S(1)} %finish.1.refs_0_.b0), channel_id=1, source_target_pairs={{0,32},{16,48},{32,0},{48,16},{64,96},{80,112},{96,64},{112,80},{1... | collective-permute-start | bytes 589832 | tf_op jit(solution)/shard_map/ppermute | solution.py:24
  51.6 1.4 %pages_near.1 = (f32[1024,128]{1,0:T(8,128)S(1)}, f32[1024,128]{1,0:T(8,128)S(1)}, f32[1024,128]{1,0:T(8,128)S(1)}) custom-call(bf16[4,256,128]{2,1,0:T(8,128)(2,1)S(1)} %get-tuple-element.36.queries, bf16[768,128]{1,0:T(8,128)(2,1)S(1)} %finish.1.refs_0_.b0, bf16[768,128]{1,0:T(8,128)(2,1)S(1)} %collective-permute-done.21.refs_1_), custom_call_target="tpu_custom_call" | custom-call | flops 402653184 | bytes 4194304 | tf_op jit(solution)/shard_map/pages_near/pallas_call | solution.py:415
  53.0 0.8 %turn_attention.1 = (f32[1024,128]{1,0:T(8,128)S(1)}, f32[1024,128]{1,0:T(8,128)S(1)}, f32[1024,128]{1,0:T(8,128)S(1)}) custom-call(bf16[4,256,128]{2,1,0:T(8,128)(2,1)S(1)} %get-tuple-element.36.queries, bf16[1024,128]{1,0:T(8,128)(2,1)S(1)} %pad_maximum_fusion.2.near, bf16[1024,128]{1,0:T(8,128)(2,1)S(1)} %collective-permute-done.22.far, ...), custom_call_target="tpu_custom_call" | custom-call | flops 1073741824 | bytes 4194304 | tf_op jit(solution)/shard_map/turn_attention/pallas_call | solution.py:403
  53.8 1.6 %collective-permute-done.20.refs_2_.b3 = bf16[768,128]{1,0:T(8,128)(2,1)S(1)} collective-permute-done((bf16[768,128]{1,0:T(8,128)(2,1)S(1)}, bf16[768,128]{1,0:T(8,128)(2,1)S(1)}, u32[]{:S(2)}, u32[]{:S(2)}) %collective-permute-start.20) | collective-permute-done | bytes 196640 | tf_op jit(solution)/shard_map/ppermute | solution.py:24
  55.4 0.9 %collective-permute-start.25 = (bf16[768,128]{1,0:T(8,128)(2,1)S(1)}, bf16[768,128]{1,0:T(8,128)(2,1)S(1)}, u32[]{:S(2)}, u32[]{:S(2)}) collective-permute-start(bf16[768,128]{1,0:T(8,128)(2,1)S(1)} %collective-permute-done.19.refs_0_.b1), channel_id=1, source_target_pairs={{0,1},{1,0},{2,3},{3,2},{4,5},{5,4},{6,7},{7,6},{8,9},{9,8},{10,11... | collective-permute-start | bytes 589832 | tf_op jit(solution)/shard_map/ppermute | solution.py:20
  56.3 0.1 collective-permute-start.26
  56.4 4.0 %collective-permute-done.17.own.b2 = bf16[768,128]{1,0:T(8,128)(2,1)S(1)} collective-permute-done((bf16[768,128]{1,0:T(8,128)(2,1)S(1)}, bf16[768,128]{1,0:T(8,128)(2,1)S(1)}, u32[]{:S(2)}, u32[]{:S(2)}) %collective-permute-start.17) | collective-permute-done | bytes 196640 | tf_op jit(solution)/shard_map/ppermute | solution.py:24
  60.4 1.2 %collective-permute-start.18 = (bf16[768,128]{1,0:T(8,128)(2,1)S(1)}, bf16[768,128]{1,0:T(8,128)(2,1)S(1)}, u32[]{:S(2)}, u32[]{:S(2)}) collective-permute-start(bf16[768,128]{1,0:T(8,128)(2,1)S(1)} %collective-permute-done.17.own.b2), channel_id=1, source_target_pairs={{0,1},{1,0},{2,3},{3,2},{4,5},{5,4},{6,7},{7,6},{8,9},{9,8},{10,11... | collective-permute-start | bytes 589832 | tf_op jit(solution)/shard_map/ppermute | solution.py:20
  61.6 2.5 %pages_side.1 = (f32[1024,128]{1,0:T(8,128)S(1)}, f32[1024,128]{1,0:T(8,128)S(1)}, f32[1024,128]{1,0:T(8,128)S(1)}) custom-call(bf16[4,256,128]{2,1,0:T(8,128)(2,1)S(1)} %get-tuple-element.36.queries, bf16[768,128]{1,0:T(8,128)(2,1)S(1)} %collective-permute-done.19.refs_0_.b1, bf16[768,128]{1,0:T(8,128)(2,1)S(1)} %collective-permute-done.25.refs_1_, ...), custom_call_target="tpu_custom_call" | custom-call | flops 805306368 | bytes 4194304 | tf_op jit(solution)/shard_map/pages_side/pallas_call | solution.py:415
  64.2 3.0 %pages_last.1 = (bf16[256,512]{1,0:T(8,128)(2,1)}, bf16[1024,128]{1,0:T(8,128)(2,1)}) custom-call(s32[8,8]{1,0:T(8,128)S(1)} %copy-done.5, s32[8,8]{1,0:T(8,128)S(1)} %copy-done.6, bf16[4,256,128]{2,1,0:T(8,128)(2,1)S(1)} %get-tuple-element.36.queries, bf16[768,128]{1,0:T(8,128)(2,1)S(1)} %collective-permute-done.17.own.b2, ...), custom_call_target="tpu_custom_call" | custom-call | flops 402653184 | bytes 4194304 | tf_op jit(solution)/shard_map/pages_last/pallas_call | solution.py:431
  (25 shorter events, 0.1 us)
Async XLA Ops:
  0.6 17.3 %collective-permute-start.3 = (bf16[384,512]{1,0:T(8,128)(2,1)}, bf16[384,512]{1,0:T(8,128)(2,1)S(1)}, u32[]{:S(2)}, u32[]{:S(2)}) collective-permute-start(bf16[384,512]{1,0:T(8,128)(2,1)} %bitcast.1), channel_id=1, source_target_pairs={{0,12},{1,13},{2,14},{3,15},{4,8},{5,9},{6,10},{7,11},{8,4},{9,5},... | collective-permute-start | bytes 1179656 | tf_op jit(solution)/shard_map/ppermute | solution.py:20
  5.3 14.2 %collective-permute-start = (bf16[384,512]{1,0:T(8,128)(2,1)}, bf16[384,512]{1,0:T(8,128)(2,1)S(1)}, u32[]{:S(2)}, u32[]{:S(2)}) collective-permute-start(bf16[384,512]{1,0:T(8,128)(2,1)} %bitcast.2), channel_id=1, source_target_pairs={{0,4},{1,5},{2,6},{3,7},{4,0},{5,1},{6,2},{7,3},{8,12},{9,13},{10,... | collective-permute-start | bytes 1179656 | tf_op jit(solution)/shard_map/ppermute | solution.py:20
  5.3 1.6 %copy-start = (bf16[8192,128]{1,0:T(8,128)(2,1)S(1)}, bf16[8192,128]{1,0:T(8,128)(2,1)}, u32[]{:S(2)}) copy-start(bf16[8192,128]{1,0:T(8,128)(2,1)} %refs_10_.1) | copy-start | bytes 6291460
  7.0 5.9 %copy-start.3 = (bf16[256,512]{1,0:T(8,128)(2,1)S(1)}, bf16[256,512]{1,0:T(8,128)(2,1)}, u32[]{:S(2)}) copy-start(bf16[256,512]{1,0:T(8,128)(2,1)} %queries.1) | copy-start | bytes 786436
  7.0 5.9 %copy-start.4 = (bf16[256,128]{1,0:T(8,128)(2,1)S(1)}, bf16[256,128]{1,0:T(8,128)(2,1)}, u32[]{:S(2)}) copy-start(bf16[256,128]{1,0:T(8,128)(2,1)} %turn_kv) | copy-start | bytes 196612
  7.0 8.3 %collective-permute-start.9 = (bf16[1024,128]{1,0:T(8,128)(2,1)S(1)}, bf16[1024,128]{1,0:T(8,128)(2,1)S(1)}, u32[]{:S(2)}, u32[]{:S(2)}) collective-permute-start(bf16[1024,128]{1,0:T(8,128)(2,1)S(1)} %get-tuple-element.39), channel_id=1, source_target_pairs={{0,66},{1,67},{2,64},{3,65},{4,70},{5,71},{6,68},{7,69},{8,74},{9,... | collective-permute-start | bytes 786440 | tf_op jit(solution)/shard_map/ppermute | solution.py:30
  9.8 17.1 %collective-permute-start.10 = (bf16[2,1024,128]{2,1,0:T(8,128)(2,1)S(1)}, bf16[2,1024,128]{2,1,0:T(8,128)(2,1)S(1)}, u32[]{:S(2)}, u32[]{:S(2)}) collective-permute-start(bf16[2,1024,128]{2,1,0:T(8,128)(2,1)S(1)} %get-tuple-element.40), channel_id=1, source_target_pairs={{0,66},{1,67},{2,64},{3,65},{4,70},{5,71},{6,68},{7,69},{8,74},{9,... | collective-permute-start | bytes 1572872 | tf_op jit(solution)/shard_map/ppermute | solution.py:30
  12.6 10.1 %copy-start.2 = (bf16[3,128,512]{2,1,0:T(8,128)(2,1)S(1)}, bf16[3,128,512]{2,1,0:T(8,128)(2,1)}, u32[]{:S(2)}) copy-start(bf16[3,128,512]{2,1,0:T(8,128)(2,1)} %param.7) | copy-start | bytes 1179652
  12.6 18.2 %copy-start.1 = (bf16[8192,128]{1,0:T(8,128)(2,1)S(1)}, bf16[8192,128]{1,0:T(8,128)(2,1)}, u32[]{:S(2)}) copy-start(bf16[8192,128]{1,0:T(8,128)(2,1)} %refs_10_.1) | copy-start | bytes 6291460
  13.1 3.5 %collective-permute-start.12 = (bf16[256,128]{1,0:T(8,128)(2,1)S(1)}, bf16[256,128]{1,0:T(8,128)(2,1)S(1)}, u32[]{:S(2)}, u32[]{:S(2)}) collective-permute-start(bf16[256,128]{1,0:T(8,128)(2,1)S(1)} %get-tuple-element.42), channel_id=1, source_target_pairs={{0,64},{16,80},{32,96},{48,112},{64,0},{80,16},{96,32},{112,48},{1... | collective-permute-start | bytes 196616 | tf_op jit(solution)/shard_map/ppermute | solution.py:24
  15.3 11.5 %collective-permute-start.11 = (bf16[1024,128]{1,0:T(8,128)(2,1)S(1)}, bf16[1024,128]{1,0:T(8,128)(2,1)S(1)}, u32[]{:S(2)}, u32[]{:S(2)}) collective-permute-start(bf16[1024,128]{1,0:T(8,128)(2,1)S(1)} %collective-permute-done.9.refs_11_), channel_id=1, source_target_pairs={{0,16},{16,0},{32,48},{48,32},{64,80},{80,64},{96,112},{112,96},{1... | collective-permute-start | bytes 786440 | tf_op jit(solution)/shard_map/ppermute | solution.py:24
  16.6 6.1 %collective-permute-start.13 = (bf16[512,128]{1,0:T(8,128)(2,1)S(1)}, bf16[512,128]{1,0:T(8,128)(2,1)S(1)}, u32[]{:S(2)}, u32[]{:S(2)}) collective-permute-start(bf16[512,128]{1,0:T(8,128)(2,1)S(1)} %pad_maximum_fusion.5), channel_id=1, source_target_pairs={{0,16},{16,0},{32,48},{48,32},{64,80},{80,64},{96,112},{112,96},{1... | collective-permute-start | bytes 393224 | tf_op jit(solution)/shard_map/ppermute | solution.py:24
  17.9 10.4 %collective-permute-start.7 = (bf16[192,512]{1,0:T(8,128)(2,1)S(1)}, bf16[192,512]{1,0:T(8,128)(2,1)S(1)}, u32[]{:S(2)}, u32[]{:S(2)}) collective-permute-start(bf16[192,512]{1,0:T(8,128)(2,1)S(1)} %slice.25), channel_id=1, source_target_pairs={{0,4},{1,5},{2,6},{3,7},{4,0},{5,1},{6,2},{7,3},{8,12},{9,13},{10,... | collective-permute-start | bytes 589832 | tf_op jit(solution)/shard_map/ppermute | solution.py:20
  19.5 8.9 %collective-permute-start.5 = (bf16[192,512]{1,0:T(8,128)(2,1)S(1)}, bf16[192,512]{1,0:T(8,128)(2,1)S(1)}, u32[]{:S(2)}, u32[]{:S(2)}) collective-permute-start(bf16[192,512]{1,0:T(8,128)(2,1)S(1)} %slice.24), channel_id=1, source_target_pairs={{0,12},{1,13},{2,14},{3,15},{4,8},{5,9},{6,10},{7,11},{8,4},{9,5},... | collective-permute-start | bytes 589832 | tf_op jit(solution)/shard_map/ppermute | solution.py:20
  22.7 8.1 %collective-permute-start.1 = (bf16[384,512]{1,0:T(8,128)(2,1)S(1)}, bf16[384,512]{1,0:T(8,128)(2,1)S(1)}, u32[]{:S(2)}, u32[]{:S(2)}) collective-permute-start(bf16[384,512]{1,0:T(8,128)(2,1)S(1)} %bitcast.3), channel_id=1, source_target_pairs={{0,1},{1,0},{2,3},{3,2},{4,5},{5,4},{6,7},{7,6},{8,9},{9,8},{10,11... | collective-permute-start | bytes 1179656 | tf_op jit(solution)/shard_map/ppermute | solution.py:20
  26.8 3.1 %collective-permute-start.4 = (bf16[384,512]{1,0:T(8,128)(2,1)S(1)}, bf16[384,512]{1,0:T(8,128)(2,1)S(1)}, u32[]{:S(2)}, u32[]{:S(2)}) collective-permute-start(bf16[384,512]{1,0:T(8,128)(2,1)S(1)} %collective-permute-done.3.refs_4_), channel_id=1, source_target_pairs={{0,1},{1,0},{2,3},{3,2},{4,5},{5,4},{6,7},{7,6},{8,9},{9,8},{10,11... | collective-permute-start | bytes 1179656 | tf_op jit(solution)/shard_map/ppermute | solution.py:20
  26.9 3.9 %collective-permute-start.2 = (bf16[384,512]{1,0:T(8,128)(2,1)S(1)}, bf16[384,512]{1,0:T(8,128)(2,1)S(1)}, u32[]{:S(2)}, u32[]{:S(2)}) collective-permute-start(bf16[384,512]{1,0:T(8,128)(2,1)S(1)} %collective-permute-done.refs_2_), channel_id=1, source_target_pairs={{0,1},{1,0},{2,3},{3,2},{4,5},{5,4},{6,7},{7,6},{8,9},{9,8},{10,11... | collective-permute-start | bytes 1179656 | tf_op jit(solution)/shard_map/ppermute | solution.py:20
  28.3 1.6 %collective-permute-start.8 = (bf16[192,512]{1,0:T(8,128)(2,1)S(1)}, bf16[192,512]{1,0:T(8,128)(2,1)S(1)}, u32[]{:S(2)}, u32[]{:S(2)}) collective-permute-start(bf16[192,512]{1,0:T(8,128)(2,1)S(1)} %collective-permute-done.7.refs_8_), channel_id=1, source_target_pairs={{0,1},{1,0},{2,3},{3,2},{4,5},{5,4},{6,7},{7,6},{8,9},{9,8},{10,11... | collective-permute-start | bytes 589832 | tf_op jit(solution)/shard_map/ppermute | solution.py:20
  28.3 2.5 %collective-permute-start.6 = (bf16[192,512]{1,0:T(8,128)(2,1)S(1)}, bf16[192,512]{1,0:T(8,128)(2,1)S(1)}, u32[]{:S(2)}, u32[]{:S(2)}) collective-permute-start(bf16[192,512]{1,0:T(8,128)(2,1)S(1)} %collective-permute-done.5.refs_6_), channel_id=1, source_target_pairs={{0,1},{1,0},{2,3},{3,2},{4,5},{5,4},{6,7},{7,6},{8,9},{9,8},{10,11... | collective-permute-start | bytes 589832 | tf_op jit(solution)/shard_map/ppermute | solution.py:20
  34.0 8.8 %collective-permute-start.22 = (bf16[1024,128]{1,0:T(8,128)(2,1)S(1)}, bf16[1024,128]{1,0:T(8,128)(2,1)S(1)}, u32[]{:S(2)}, u32[]{:S(2)}) collective-permute-start(bf16[1024,128]{1,0:T(8,128)(2,1)S(1)} %pad_maximum_fusion.2.near), channel_id=1, source_target_pairs={{0,48},{16,32},{32,16},{48,0},{64,112},{80,96},{96,80},{112,64},{1... | collective-permute-start | bytes 786440 | tf_op jit(solution)/shard_map/ppermute | solution.py:24
  36.7 8.5 %collective-permute-start.16 = (bf16[384,128]{1,0:T(8,128)(2,1)S(1)}, bf16[384,128]{1,0:T(8,128)(2,1)S(1)}, u32[]{:S(2)}, u32[]{:S(2)}) collective-permute-start(bf16[384,128]{1,0:T(8,128)(2,1)S(1)} %get-tuple-element.44), channel_id=1, source_target_pairs={{0,66},{1,67},{2,64},{3,65},{4,70},{5,71},{6,68},{7,69},{8,74},{9,... | collective-permute-start | bytes 294920 | tf_op jit(solution)/shard_map/ppermute | solution.py:30
  39.5 5.7 %collective-permute-start.14 = (bf16[384,128]{1,0:T(8,128)(2,1)S(1)}, bf16[384,128]{1,0:T(8,128)(2,1)S(1)}, u32[]{:S(2)}, u32[]{:S(2)}) collective-permute-start(bf16[384,128]{1,0:T(8,128)(2,1)S(1)} %get-tuple-element.44), channel_id=1, source_target_pairs={{0,2},{1,3},{2,0},{3,1},{4,6},{5,7},{6,4},{7,5},{8,10},{9,11},{10,... | collective-permute-start | bytes 294920 | tf_op jit(solution)/shard_map/ppermute | solution.py:20
  39.5 13.5 %collective-permute-start.23 = (bf16[1024,128]{1,0:T(8,128)(2,1)S(1)}, bf16[1024,128]{1,0:T(8,128)(2,1)S(1)}, u32[]{:S(2)}, u32[]{:S(2)}) collective-permute-start(bf16[1024,128]{1,0:T(8,128)(2,1)S(1)} %pad_maximum_fusion.2.near), channel_id=1, source_target_pairs={{0,1},{1,0},{2,3},{3,2},{4,5},{5,4},{6,7},{7,6},{8,9},{9,8},{10,11... | collective-permute-start | bytes 786440 | tf_op jit(solution)/shard_map/ppermute | solution.py:20
  40.4 4.7 %collective-permute-start.15 = (bf16[384,128]{1,0:T(8,128)(2,1)S(1)}, bf16[384,128]{1,0:T(8,128)(2,1)S(1)}, u32[]{:S(2)}, u32[]{:S(2)}) collective-permute-start(bf16[384,128]{1,0:T(8,128)(2,1)S(1)} %get-tuple-element.45), channel_id=1, source_target_pairs={{0,64},{16,80},{32,96},{48,112},{64,0},{80,16},{96,32},{112,48},{1... | collective-permute-start | bytes 294920 | tf_op jit(solution)/shard_map/ppermute | solution.py:24
  42.8 10.2 %collective-permute-start.24 = (bf16[1024,128]{1,0:T(8,128)(2,1)S(1)}, bf16[1024,128]{1,0:T(8,128)(2,1)S(1)}, u32[]{:S(2)}, u32[]{:S(2)}) collective-permute-start(bf16[1024,128]{1,0:T(8,128)(2,1)S(1)} %collective-permute-done.22.far), channel_id=1, source_target_pairs={{0,1},{1,0},{2,3},{3,2},{4,5},{5,4},{6,7},{7,6},{8,9},{9,8},{10,11... | collective-permute-start | bytes 786440 | tf_op jit(solution)/shard_map/ppermute | solution.py:20
  45.4 3.4 %collective-permute-start.21 = (bf16[768,128]{1,0:T(8,128)(2,1)S(1)}, bf16[768,128]{1,0:T(8,128)(2,1)S(1)}, u32[]{:S(2)}, u32[]{:S(2)}) collective-permute-start(bf16[768,128]{1,0:T(8,128)(2,1)S(1)} %finish.1.refs_0_.b0), channel_id=1, source_target_pairs={{0,1},{1,0},{2,3},{3,2},{4,5},{5,4},{6,7},{7,6},{8,9},{9,8},{10,11... | collective-permute-start | bytes 589832 | tf_op jit(solution)/shard_map/ppermute | solution.py:20
  47.7 7.7 %collective-permute-start.20 = (bf16[768,128]{1,0:T(8,128)(2,1)S(1)}, bf16[768,128]{1,0:T(8,128)(2,1)S(1)}, u32[]{:S(2)}, u32[]{:S(2)}) collective-permute-start(bf16[768,128]{1,0:T(8,128)(2,1)S(1)} %finish.1.refs_0_.b0), channel_id=1, source_target_pairs={{0,48},{16,32},{32,16},{48,0},{64,112},{80,96},{96,80},{112,64},{1... | collective-permute-start | bytes 589832 | tf_op jit(solution)/shard_map/ppermute | solution.py:24
  47.9 7.5 %collective-permute-start.19 = (bf16[768,128]{1,0:T(8,128)(2,1)S(1)}, bf16[768,128]{1,0:T(8,128)(2,1)S(1)}, u32[]{:S(2)}, u32[]{:S(2)}) collective-permute-start(bf16[768,128]{1,0:T(8,128)(2,1)S(1)} %finish.1.refs_0_.b0), channel_id=1, source_target_pairs={{0,16},{16,0},{32,48},{48,32},{64,80},{80,64},{96,112},{112,96},{1... | collective-permute-start | bytes 589832 | tf_op jit(solution)/shard_map/ppermute | solution.py:24
  48.8 11.7 %collective-permute-start.17 = (bf16[768,128]{1,0:T(8,128)(2,1)S(1)}, bf16[768,128]{1,0:T(8,128)(2,1)S(1)}, u32[]{:S(2)}, u32[]{:S(2)}) collective-permute-start(bf16[768,128]{1,0:T(8,128)(2,1)S(1)} %finish.1.refs_0_.b0), channel_id=1, source_target_pairs={{0,32},{16,48},{32,0},{48,16},{64,96},{80,112},{96,64},{112,80},{1... | collective-permute-start | bytes 589832 | tf_op jit(solution)/shard_map/ppermute | solution.py:24
  55.4 8.8 %copy-start.5 = (s32[8,8]{1,0:T(8,128)S(1)}, s32[8,8]{1,0:T(8,128)}, u32[]{:S(2)}) copy-start(s32[8,8]{1,0:T(8,128)} %page_table.1) | copy-start | bytes 772
  55.4 8.8 %copy-start.6 = (s32[8,8]{1,0:T(8,128)S(1)}, s32[8,8]{1,0:T(8,128)}, u32[]{:S(2)}) copy-start(s32[8,8]{1,0:T(8,128)} %page_counts.1) | copy-start | bytes 772
  55.4 6.3 %collective-permute-start.25 = (bf16[768,128]{1,0:T(8,128)(2,1)S(1)}, bf16[768,128]{1,0:T(8,128)(2,1)S(1)}, u32[]{:S(2)}, u32[]{:S(2)}) collective-permute-start(bf16[768,128]{1,0:T(8,128)(2,1)S(1)} %collective-permute-done.19.refs_0_.b1), channel_id=1, source_target_pairs={{0,1},{1,0},{2,3},{3,2},{4,5},{5,4},{6,7},{7,6},{8,9},{9,8},{10,11... | collective-permute-start | bytes 589832 | tf_op jit(solution)/shard_map/ppermute | solution.py:20
  56.3 5.3 %collective-permute-start.26 = (bf16[768,128]{1,0:T(8,128)(2,1)S(1)}, bf16[768,128]{1,0:T(8,128)(2,1)S(1)}, u32[]{:S(2)}, u32[]{:S(2)}) collective-permute-start(bf16[768,128]{1,0:T(8,128)(2,1)S(1)} %collective-permute-done.20.refs_2_.b3), channel_id=1, source_target_pairs={{0,1},{1,0},{2,3},{3,2},{4,5},{5,4},{6,7},{7,6},{8,9},{9,8},{10,11... | collective-permute-start | bytes 589832 | tf_op jit(solution)/shard_map/ppermute | solution.py:20
  60.4 3.7 %collective-permute-start.18 = (bf16[768,128]{1,0:T(8,128)(2,1)S(1)}, bf16[768,128]{1,0:T(8,128)(2,1)S(1)}, u32[]{:S(2)}, u32[]{:S(2)}) collective-permute-start(bf16[768,128]{1,0:T(8,128)(2,1)S(1)} %collective-permute-done.17.own.b2), channel_id=1, source_target_pairs={{0,1},{1,0},{2,3},{3,2},{4,5},{5,4},{6,7},{7,6},{8,9},{9,8},{10,11... | collective-permute-start | bytes 589832 | tf_op jit(solution)/shard_map/ppermute | solution.py:20
